TPU v7x, 32 devices: a whole 2x2x4 slice. The times are simulated.
32 devices in a mesh: col: 8 (over z, y), sec: 4 (over x, core).
Axes of the slice: x: 2, y: 2, z: 4, core: 2. Of those that a mesh axis runs over, the one named last changes fastest.
Arguments:
- transfer: float32 [16, 4, 256, 256], P('col', 'sec'), as said below
- hamiltonian: float32 [16, 3, 4, 256, 256], P('col', None, 'sec'), may hold values from -0.375 to 0.375
- kept: int32 [16, 4], P('col', 'sec'), may hold values from 128 to 256, as said below
Outputs:
- left_env: float32 [16, 4, 256, 256], P('col', 'sec')
- energy: float32 [16, 3], P('col')
Inputs may be any that keep to these rules, and one draw needn't show every extreme that they name: Every kept dimension lies between half a sector and a whole sector, and some sector keeps all 256 states. `transfer`: each block is the identity plus an independent normal matrix of entries with deviation 0.2 / sqrt(256).
All inputs are finite; a program needn't handle non-finite values.
Results may differ from a plain program's by a relative error of at most 0.0003.
Values sent between devices are 32-bit elements; how exact they have to be, the bound alone decides.
No kernel may reach another device: no remote copies, remote signals or barrier semaphores. Data moves between devices by JAX's collectives and lax.ppermute only.
A program may use at most 64 MiB of HBM per device.

v0:
```python
import jax
import jax.numpy as jnp
from jax import lax
from jax.sharding import PartitionSpec as P


def matmul(first, second):
    return jnp.einsum("sij,sjk->sik", first, second, precision=lax.Precision.HIGHEST)


def per_device(transfer, hamiltonian, kept):
    col_count = transfer.shape[0]
    sectors = transfer.shape[1]
    width = transfer.shape[2]
    eye = jnp.broadcast_to(jnp.eye(width, dtype=jnp.float32), (sectors, width, width))
    group = transfer[0]
    column = 1
    group = matmul(group, transfer[column])
    groups = lax.all_gather(group[None], "col", axis=0, tiled=True)
    place = lax.axis_index("col")
    total = lax.axis_size("col")

    def select_left_side(step, acc):
        return matmul(acc, groups[step])

    prior_environment = lax.fori_loop(0, place, select_left_side, eye)

    def take_high(step, acc):
        return matmul(groups[total - 1 - step], acc)

    after = lax.fori_loop(0, total - 1 - place, take_high, eye)
    whole = matmul(matmul(prior_environment, group), after)
    lefts = [prior_environment]
    column = 1
    lefts.append(matmul(lefts[-1], transfer[column - 1]))
    right_environments = [after]
    column = 1
    right_environments.insert(0, matmul(transfer[column], right_environments[0]))
    column_positions = jnp.arange(width, dtype=jnp.int32)
    masked_list = []
    partial_results = []
    for column in range(col_count):
        mask = (column_positions[None, :] < kept[column][:, None]).astype(jnp.float32)
        masked = lefts[column] * mask[:, None, :]
        masked_list.append(masked)
        inner_contraction = jnp.einsum(
            "sji,sjk->sik", masked, whole, precision=lax.Precision.HIGHEST
        )
        inner_contraction = jnp.einsum(
            "sik,slk->sil",
            inner_contraction,
            right_environments[column],
            precision=lax.Precision.HIGHEST,
        )
        partial_results.append(
            jnp.einsum(
                "sil,tsil->t",
                inner_contraction,
                hamiltonian[column],
                precision=lax.Precision.HIGHEST,
            )
        )
    partial_value = jnp.stack(partial_results, axis=0)
    norm = jnp.sum(whole * whole)
    partial_value, norm = lax.psum((partial_value, norm), "sec")
    scale = float(width * sectors * lax.axis_size("sec"))
    energy = scale * partial_value / norm
    left_env = jnp.stack(masked_list, axis=0)
    return (left_env, energy)


def solution(mesh):
    in_specs = (P("col", "sec", None, None), P("col", None, "sec", None, None), P("col", "sec"))
    out_specs = (P("col", "sec", None, None), P("col", None))
    return jax.shard_map(
        per_device, mesh=mesh, in_specs=in_specs, out_specs=out_specs, check_vma=False
    )
```

profile of v0, /device:TPU:0, one launch (start us, length us, event | category | flops | bytes accessed | tf_op | source)
XLA Modules:
  0.0 103.6 jit_solution(16220908053536458304)
XLA Ops:
  7.2 0.0 copy-start.2
  7.2 0.0 all-gather.3.cloned.1.call-start
  7.2 2.2 %fusion.21 = f32[256,256]{1,0:T(8,128)} fusion(f32[2,1,256,256]{3,2,1,0:T(8,128)} %param.7), kind=kOutput, calls=%fused_computation.31 | convolution fusion | flops 201326592 | bytes 786432 | tf_op jit(solution)/shard_map/sij,sjk->sik/dot_general | solution.py:8
  9.4 0.0 all-gather.3.cloned.1.call-update
  9.5 0.1 copy.5
  9.6 1.4 %fusion.34 = (s32[1,1]{0,1:T(1,128)}, s32[1,1]{0,1:T(1,128)}) fusion(s32[2,1]{0,1:T(1,128)} %param.9), kind=kLoop, calls=%fused_computation.51 | loop fusion | bytes 16 | tf_op jit(solution)/shard_map/slice | solution.py:43
  11.0 0.7 compare_convert_fusion.1
  11.7 0.6 compare_convert_fusion
  12.4 0.0 copy-done.2
  12.4 1.0 slice_bitcast_fusion.1
  13.4 49.3 %all-gather.3.cloned.1.call-done = f32[2048,256]{1,0:T(8,128)} async-done(((f32[256,256]{1,0:T(8,128)}), f32[2048,256]{1,0:T(8,128)}) %all-gather.3.cloned.1.call-update) | async-done | bytes 2097168 | tf_op jit(solution)/shard_map/all_gather | solution.py:19
  62.7 0.0 copy-start
  62.7 0.9 copy-done
  63.7 0.6 fusion.17
  64.3 0.1 copy.7
  64.4 0.0 copy-start.1
  64.4 10.0 %while.23 = (s32[]{:T(128)}, f32[1,256,256]{2,1,0:T(8,128)S(1)}, s32[]{:T(128)}, f32[8,1,256,256]{3,2,1,0:T(8,128)}, s32[]{:T(128)}, /*index=5*/s32[]{:T(128)}, s32[]{:T(128)}, s32[]{:T(128)}) while((s32[]{:T(128)}, f32[1,256,256]{2,1,0:T(8,128)S(1)}, s32[]{:T(128)}, f32[8,1,256,256]{3,2,1,0:T(8,128)}, s32[]{:T(128)}, /*index=5*/s32[]{:T(128)}, ...), condition=%wide.region_3.0_spmd, body=%wide.region_2.0_spmd.sunk | while | flops 201326592 | bytes 1310855 | solution.py:31
  64.5 1.4 %convolution_bitcast_fusion.9 = f32[1,256,256]{2,1,0:T(8,128)S(1)} fusion(f32[1,256,256]{2,1,0:T(8,128)S(1)} %copy.36, f32[8,1,256,256]{3,2,1,0:T(8,128)} %get-tuple-element.207, s32[]{:T(128)S(6)} %select_n.12), kind=kOutput, calls=%fused_computation.5.clone.1 | convolution fusion | flops 201326592 | bytes 786436 | tf_op jit(solution)/shard_map/while/body/sij,sjk->sik/dot_general | solution.py:8
  65.9 1.3 %convolution_bitcast_fusion.9 = f32[1,256,256]{2,1,0:T(8,128)S(1)} fusion(f32[1,256,256]{2,1,0:T(8,128)S(1)} %copy.36, f32[8,1,256,256]{3,2,1,0:T(8,128)} %get-tuple-element.207, s32[]{:T(128)S(6)} %select_n.12), kind=kOutput, calls=%fused_computation.5.clone.1 | convolution fusion | flops 201326592 | bytes 786436 | tf_op jit(solution)/shard_map/while/body/sij,sjk->sik/dot_general | solution.py:8
  67.3 1.3 %convolution_bitcast_fusion.9 = f32[1,256,256]{2,1,0:T(8,128)S(1)} fusion(f32[1,256,256]{2,1,0:T(8,128)S(1)} %copy.36, f32[8,1,256,256]{3,2,1,0:T(8,128)} %get-tuple-element.207, s32[]{:T(128)S(6)} %select_n.12), kind=kOutput, calls=%fused_computation.5.clone.1 | convolution fusion | flops 201326592 | bytes 786436 | tf_op jit(solution)/shard_map/while/body/sij,sjk->sik/dot_general | solution.py:8
  68.7 1.3 %convolution_bitcast_fusion.9 = f32[1,256,256]{2,1,0:T(8,128)S(1)} fusion(f32[1,256,256]{2,1,0:T(8,128)S(1)} %copy.36, f32[8,1,256,256]{3,2,1,0:T(8,128)} %get-tuple-element.207, s32[]{:T(128)S(6)} %select_n.12), kind=kOutput, calls=%fused_computation.5.clone.1 | convolution fusion | flops 201326592 | bytes 786436 | tf_op jit(solution)/shard_map/while/body/sij,sjk->sik/dot_general | solution.py:8
  70.1 1.3 %convolution_bitcast_fusion.9 = f32[1,256,256]{2,1,0:T(8,128)S(1)} fusion(f32[1,256,256]{2,1,0:T(8,128)S(1)} %copy.36, f32[8,1,256,256]{3,2,1,0:T(8,128)} %get-tuple-element.207, s32[]{:T(128)S(6)} %select_n.12), kind=kOutput, calls=%fused_computation.5.clone.1 | convolution fusion | flops 201326592 | bytes 786436 | tf_op jit(solution)/shard_map/while/body/sij,sjk->sik/dot_general | solution.py:8
  71.5 1.3 %convolution_bitcast_fusion.9 = f32[1,256,256]{2,1,0:T(8,128)S(1)} fusion(f32[1,256,256]{2,1,0:T(8,128)S(1)} %copy.36, f32[8,1,256,256]{3,2,1,0:T(8,128)} %get-tuple-element.207, s32[]{:T(128)S(6)} %select_n.12), kind=kOutput, calls=%fused_computation.5.clone.1 | convolution fusion | flops 201326592 | bytes 786436 | tf_op jit(solution)/shard_map/while/body/sij,sjk->sik/dot_general | solution.py:8
  72.9 1.3 %convolution_bitcast_fusion.9 = f32[1,256,256]{2,1,0:T(8,128)S(1)} fusion(f32[1,256,256]{2,1,0:T(8,128)S(1)} %copy.36, f32[8,1,256,256]{3,2,1,0:T(8,128)} %get-tuple-element.207, s32[]{:T(128)S(6)} %select_n.12), kind=kOutput, calls=%fused_computation.5.clone.1 | convolution fusion | flops 201326592 | bytes 786436 | tf_op jit(solution)/shard_map/while/body/sij,sjk->sik/dot_general | solution.py:8
  74.4 0.0 copy-done.1
  74.4 0.6 fusion.11
  75.0 1.0 multiply_reduce_fusion
  76.0 0.0 copy-start.3
  76.0 0.6 fusion.15
  76.7 0.6 convolution_multiply_fusion
  77.3 0.6 fusion.35
  77.9 0.4 convolution_bitcast_fusion.2
  78.3 0.4 convolution_bitcast_fusion.3
  78.7 0.0 copy-done.3
  78.7 4.8 %convolution_bitcast_fusion.5 = f32[1,3]{1,0:T(1,128)S(1)} fusion(f32[3,256,256]{2,1,0:T(8,128)S(1)} %copy-done.3, f32[256,256,1]{1,0,2:T(8,128)S(1)} %convolution_bitcast_fusion.3), kind=kOutput, calls=%fused_computation.14 | convolution fusion | flops 2359296 | bytes 1048588 | tf_op jit(solution)/shard_map/sil,tsil->t/dot_general | solution.py:56
  83.5 4.9 %convolution_bitcast_fusion.4 = f32[1,3]{1,0:T(1,128)S(1)} fusion(f32[3,256,256]{2,1,0:T(8,128)S(1)} %get-tuple-element.110, f32[256,256,1]{1,0,2:T(8,128)S(1)} %convolution_bitcast_fusion.2), kind=kOutput, calls=%fused_computation.13 | convolution fusion | flops 2359296 | bytes 1048588 | tf_op jit(solution)/shard_map/sil,tsil->t/dot_general | solution.py:56
  88.4 6.3 %all-reduce = (f32[2,3]{1,0:T(2,128)S(1)}, f32[]{:T(128)}) all-reduce(f32[2,3]{1,0:T(2,128)S(1)} %pad_maximum_fusion.1, f32[]{:T(128)} %get-tuple-element.113), channel_id=1, replica_groups=mesh['col'=8,'sec'=4] {'sec'}, use_global_device_ids=true, to_apply=%region_4.0 | all-reduce | flops 7 | bytes 56 | tf_op jit(solution)/shard_map/psum | solution.py:65
  94.7 1.2 %multiply_divide_fusion = f32[2,3]{1,0:T(2,128)} fusion(f32[2,3]{1,0:T(2,128)S(1)} %get-tuple-element.107, f32[]{:T(128)} %get-tuple-element.108), kind=kLoop, calls=%fused_computation.50 | loop fusion | flops 12 | bytes 52 | tf_op jit(solution)/shard_map/div | solution.py:67
  95.9 0.8 pad_maximum_fusion
  (11 shorter events, 0.2 us)
Async XLA Ops:
  7.2 5.2 %copy-start.2 = (f32[2,3,1,256,256]{4,3,2,1,0:T(8,128)S(1)}, f32[2,3,1,256,256]{4,3,2,1,0:T(8,128)}, u32[]{:S(2)}) copy-start(f32[2,3,1,256,256]{4,3,2,1,0:T(8,128)} %param.8) | copy-start | bytes 4718596
  7.2 55.6 %all-gather.3.cloned.1.call-start = ((), (), s32[]{:S(2)}) async-start(), calls=%async_computation | async-start | bytes 2359296 | tf_op jit(solution)/shard_map/all_gather | solution.py:19
  62.7 0.9 copy-start
  64.4 10.0 %copy-start.1 = (f32[2,1,256,256]{3,2,1,0:T(8,128)S(1)}, f32[2,1,256,256]{3,2,1,0:T(8,128)}, u32[]{:S(2)}) copy-start(f32[2,1,256,256]{3,2,1,0:T(8,128)} %param.7) | copy-start | bytes 1572868
  76.0 2.6 %copy-start.3 = (f32[3,256,256]{2,1,0:T(8,128)S(1)}, f32[3,256,256]{2,1,0:T(8,128)}, u32[]{:S(2)}) copy-start(f32[3,256,256]{2,1,0:T(8,128)} %get-tuple-element.109) | copy-start | bytes 2359300
Sparse Core Ops, SparseCore 0:
  10.7 51.9 all-gather.2
where the time goes:
time: 104 us
  waiting for transfers between devices  49.4 us (48%)
  matrix products  26.1 us (25%)
  between operations  14.2 us (14%)
  blocking collectives  6.3 us (6%)
  local copies, waits for them, and re-layouts  3.77 us (4%)
  other arithmetic  3.41 us (3%)
    all_gather x1, waiting for transfers between devices, per_device(): groups = lax.all_gather(group[None], 'col', axis=0, tiled=True)  49.3 us
    dot_general x12, matrix products, matmul(): jnp.einsum('sij,sjk->sik', first, second, precision=lax.Precision.HIGHEST)  14.4 us
    dot_general x2, matrix products, per_device(): jnp.einsum('sil,tsil->t', inner_contraction, hamiltonian[column], precisi...  9.71 us
    psum x1, blocking collectives, per_device(): partial_value, norm = lax.psum((partial_value, norm), 'sec')  6.3 us
  transfers between devices with their start and end apart: 1, of which 1 were waited for; matrix products, arithmetic and copies ran while one was open for 4% of the time, Pallas kernels for 0%

commit v1 on v0

v1 whole, which is shorter than its diff:
```python
import jax
import jax.numpy as jnp
from jax import lax
from jax.experimental import pallas as pl
from jax.experimental.pallas import tpu as pltpu
from jax.sharding import PartitionSpec as P

F32 = jnp.float32
BF16 = jnp.bfloat16
VMEM = pl.BlockSpec(memory_space=pltpu.VMEM)
SMEM = pl.BlockSpec(memory_space=pltpu.SMEM)
LIMIT = 40 * 1024 * 1024


def split(a):
    high = a.astype(BF16)
    return high, (a - high.astype(F32)).astype(BF16)


def dot(a, b, over):
    return lax.dot_general(a, b, ((over[0], over[1]), ((), ())), preferred_element_type=F32)


def multiply(a, b, over=((1,), (0,))):
    return dot(a[0], b[0], over) + (dot(a[0], b[1], over) + dot(a[1], b[0], over))


TN = ((0,), (0,))
NT = ((1,), (1,))


def group_kernel(transfer, out):
    out[...] = multiply(split(transfer[0, 0]), split(transfer[1, 0]))


def call(kernel, outs, in_specs, flops, *args):
    return pl.pallas_call(
        kernel,
        out_shape=outs,
        in_specs=in_specs,
        out_specs=jax.tree.map(lambda _: VMEM, outs),
        compiler_params=pltpu.CompilerParams(vmem_limit_bytes=LIMIT),
        cost_estimate=pl.CostEstimate(flops=flops, bytes_accessed=1 << 20, transcendentals=0),
    )(*args)


def eye(width):
    rows = lax.broadcasted_iota(jnp.int32, (width, width), 0)
    cols = lax.broadcasted_iota(jnp.int32, (width, width), 1)
    return jnp.where(rows == cols, 1.0, 0.0).astype(F32)


def quad_kernel(place, own, near, far, cross, sent, other_out):
    odd, high, upper = place[0] == 1, place[1] == 1, place[2] == 1
    own, near, far, cross = own[...], near[...], far[...], cross[...]
    mine = multiply(split(jnp.where(odd, near, own)), split(jnp.where(odd, own, near)))
    other = multiply(split(jnp.where(odd, cross, far)), split(jnp.where(odd, far, cross)))
    other_out[...] = other
    first = split(jnp.where(high, other, mine))
    second = split(jnp.where(high, mine, other))
    total = multiply(first, second)
    sent[...] = jnp.where(upper, total.T, total)


def shadow_kernel(place, kept, transfer, near, other, sent, hamiltonian, lefts_out, terms_out, norm_out):
    odd, high, upper = place[0] == 1, place[1] == 1, place[2] == 1
    width = near.shape[0]
    one = eye(width)
    near, other = near[...], other[...]
    left = multiply(split(jnp.where(high, other, one)), split(jnp.where(odd, near, one)))
    right = multiply(split(jnp.where(odd, one, near)), split(jnp.where(high, one, other)))
    lefts = [left, multiply(split(left), split(transfer[0, 0]))]
    rights = [multiply(split(transfer[1, 0]), split(right)), right]
    y = split(sent[...])
    norm_out[...] = multiply(y, y, TN)
    column = lax.broadcasted_iota(jnp.int32, (width, width), 1)
    for c in range(2):
        masked = jnp.where(column < kept[c, 0], lefts[c], 0.0)
        lefts_out[c] = masked
        a = jnp.where(upper, masked, multiply(y, split(masked), TN))
        b = jnp.where(upper, multiply(split(rights[c]), y), rights[c])
        a, b = split(a), split(b)
        for k in range(hamiltonian.shape[1]):
            inner = multiply(a, split(hamiltonian[c, k, 0]))
            terms_out[c, k] = multiply(split(inner), b)


def finish_kernel(x, terms, norm, out):
    x = split(x[...])
    z = multiply(x, x, TN)
    width = z.shape[0]
    rows = []
    for c in range(2):
        for k in range(terms.shape[1]):
            rows.append(jnp.sum(z * terms[c, k], axis=0, keepdims=True))
    rows.append(jnp.sum(z * norm[...], axis=0, keepdims=True))
    rows.append(jnp.zeros_like(rows[0]))
    table = jnp.concatenate(rows, axis=0)
    out[...] = table


def left_kernel(place, x, lefts, out):
    upper = place[2] == 1

    @pl.when(upper)
    def _():
        xs = split(x[...])
        for c in range(2):
            out[c, 0] = multiply(xs, split(lefts[c]))

    @pl.when(jnp.logical_not(upper))
    def _():
        for c in range(2):
            out[c, 0] = lefts[c]


def per_device(transfer, hamiltonian, kept):
    columns, width, terms = transfer.shape[0], transfer.shape[2], hamiltonian.shape[1]
    total = lax.axis_size("col")
    sectors = lax.axis_size("sec")
    place = lax.axis_index("col")
    bits = jnp.stack([place & 1, (place >> 1) & 1, place // (total // 2)]).astype(jnp.int32)
    matrix = jax.ShapeDtypeStruct((width, width), F32)
    one_product = 6 * width**3

    def swap(a, k):
        return lax.ppermute(a, "col", [(i, i ^ k) for i in range(total)])

    group = call(group_kernel, matrix, [VMEM], one_product, transfer)
    near, far, cross = swap(group, 1), swap(group, 2), swap(group, 3)
    sent, other = call(
        quad_kernel, (matrix, matrix), [SMEM] + [VMEM] * 4, 3 * one_product, bits, group, near, far, cross
    )
    x = swap(sent, total // 2)
    lefts, products, norm = call(
        shadow_kernel,
        (
            jax.ShapeDtypeStruct((columns, width, width), F32),
            jax.ShapeDtypeStruct((columns, terms, width, width), F32),
            matrix,
        ),
        [SMEM, SMEM] + [VMEM] * 5,
        24 * one_product,
        bits, kept, transfer, near, other, sent, hamiltonian,
    )
    table = call(
        finish_kernel, jax.ShapeDtypeStruct((8, width), F32), [VMEM] * 3, 2 * one_product, x, products, norm
    )
    parts = [table] + [lax.ppermute(table, "sec", [(i, i ^ k) for i in range(sectors)]) for k in range(1, sectors)]
    left_env = call(
        left_kernel, jax.ShapeDtypeStruct((columns, 1, width, width), F32), [SMEM, VMEM, VMEM], 2 * one_product,
        bits, x, lefts,
    )
    while len(parts) > 1:
        parts = [a + b for a, b in zip(parts[::2], parts[1::2])]
    sums = jnp.sum(parts[0], axis=1)
    scale = float(width * sectors)
    energy = scale * sums[:6].reshape(columns, terms) / sums[6]
    return left_env, energy


def solution(mesh):
    in_specs = (P("col", "sec", None, None), P("col", None, "sec", None, None), P("col", "sec"))
    out_specs = (P("col", "sec", None, None), P("col", None))
    return jax.shard_map(
        per_device, mesh=mesh, in_specs=in_specs, out_specs=out_specs, check_vma=False
    )
```

time: 104 us -> 40.5 us (0.39)
  waiting for transfers between devices: 49.4 us -> 18.7 us
  matrix products: 26.1 us -> 0 us
  between operations: 14.2 us -> 0.7 us
  starting transfers between devices: 0.04 us -> 9.34 us
  Pallas kernels: 0 us -> 7.01 us
  blocking collectives: 6.3 us -> 0 us
  other arithmetic: 3.41 us -> 0.84 us
    all_gather x1 -> x0, waiting for transfers between devices: 49.3 us -> none  [per_device(): groups = lax.all_gather(group[None], 'col', axis=0, tiled=True)]
    dot_general x18 -> x0, matrix products: 26.1 us -> none  [the longest x12 14.4 us: matmul(): jnp.einsum('sij,sjk->sik', first, second, precision=lax.Precision.HIGHEST)]
    ppermute x0 -> x7, waiting for transfers between devices: none -> 18.7 us  [the longest x4 17.5 us: swap(): return lax.ppermute(a, 'col', [(i, i ^ k) for i in range(total)])]
    ppermute x0 -> x7, starting transfers between devices: none -> 9.34 us  [the longest x4 7.41 us: swap(): return lax.ppermute(a, 'col', [(i, i ^ k) for i in range(total)])]
    pallas_call x0 -> x5, Pallas kernels: none -> 7.01 us  [call(): pl.pallas_call(kernel, out_shape=outs, in_specs=in_specs, out_specs=jax.t...]
    psum x1 -> x0, blocking collectives: 6.3 us -> none  [per_device(): partial_value, norm = lax.psum((partial_value, norm), 'sec')]
    unnamed x8 -> x9, local copies, waits for them, and re-layouts: 0.96 us -> 2.54 us
    convert_element_type x3 -> x0, other arithmetic: 1.33 us -> none  [the longest x2 1.32 us: per_device(): (column_positions[None, :] < kept[column][:, None]).astype(jnp.float32)]
  transfers between devices with their start and end apart: 1 -> 7, of which waited for: 1 -> 6; matrix products, arithmetic and copies ran while one was open for 4% -> 0% of each run, Pallas kernels for 0% -> 12%
where the time goes in v1:
time: 40.5 us; the launch traced here: 40.3 us
  waiting for transfers between devices  18.7 us (46%)
  starting transfers between devices  9.34 us (23%)
  Pallas kernels  7.01 us (17%)
  local copies, waits for them, and re-layouts  3.77 us (9%)
  other arithmetic  0.84 us (2%)
  between operations  0.7 us (2%)
    ppermute x4, waiting for transfers between devices, swap(): return lax.ppermute(a, 'col', [(i, i ^ k) for i in range(total)])  17.5 us
    ppermute x4, starting transfers between devices, swap(): return lax.ppermute(a, 'col', [(i, i ^ k) for i in range(total)])  7.41 us
    pallas_call x5, Pallas kernels, call(): pl.pallas_call(kernel, out_shape=outs, in_specs=in_specs, out_specs=jax.t...  7.01 us
    unnamed x9, local copies, waits for them, and re-layouts  2.54 us
    ppermute x3, starting transfers between devices, per_device(): lax.ppermute(table, 'sec', [(i, i ^ k) for i in range(sectors)])  1.93 us
    ppermute x3, waiting for transfers between devices, per_device(): lax.ppermute(table, 'sec', [(i, i ^ k) for i in range(sectors)])  1.22 us
  transfers between devices with their start and end apart: 7, of which 6 were waited for; matrix products, arithmetic and copies ran while one was open for 0% of the time, Pallas kernels for 12%

profile of v1, /device:TPU:0, one launch (start us, length us, event | category | flops | bytes accessed | tf_op | source)
XLA Modules:
  0.0 40.3 jit_solution(13311659610524550470)
XLA Ops:
  0.6 0.0 copy-start
  0.6 1.0 %copy-done = f32[2,1,256,256]{3,2,1,0:T(8,128)S(1)} copy-done((f32[2,1,256,256]{3,2,1,0:T(8,128)S(1)}, f32[2,1,256,256]{3,2,1,0:T(8,128)}, u32[]{:S(2)}) %copy-start) | copy-done | bytes 524312
  1.7 0.0 copy-start.3
  1.7 0.0 copy-start.1
  1.7 0.3 shard_map.50.own
  2.0 3.0 %collective-permute-start = (f32[256,256]{1,0:T(8,128)S(1)}, f32[256,256]{1,0:T(8,128)S(1)}, u32[]{:S(2)}, u32[]{:S(2)}) collective-permute-start(f32[256,256]{1,0:T(8,128)S(1)} %shard_map.50.own), channel_id=1, source_target_pairs={{0,4},{4,0},{8,12},{12,8},{16,20},{20,16},{24,28},{28,24},{1,5},{5... | collective-permute-start | bytes 786440 | tf_op jit(solution)/shard_map/ppermute | solution.py:127
  5.0 1.6 %collective-permute-start.1 = (f32[256,256]{1,0:T(8,128)S(1)}, f32[256,256]{1,0:T(8,128)S(1)}, u32[]{:S(2)}, u32[]{:S(2)}) collective-permute-start(f32[256,256]{1,0:T(8,128)S(1)} %shard_map.50.own), channel_id=1, source_target_pairs={{0,8},{4,12},{8,0},{12,4},{16,24},{20,28},{24,16},{28,20},{1,9},{5... | collective-permute-start | bytes 786440 | tf_op jit(solution)/shard_map/ppermute | solution.py:127
  6.6 0.0 collective-permute-start.2
  6.6 0.1 pad_add_fusion.place
  6.6 4.7 %collective-permute-done.near = f32[256,256]{1,0:T(8,128)S(1)} collective-permute-done((f32[256,256]{1,0:T(8,128)S(1)}, f32[256,256]{1,0:T(8,128)S(1)}, u32[]{:S(2)}, u32[]{:S(2)}) %collective-permute-start) | collective-permute-done | bytes 262176 | tf_op jit(solution)/shard_map/ppermute | solution.py:127
  11.3 2.9 %collective-permute-done.1.far = f32[256,256]{1,0:T(8,128)S(1)} collective-permute-done((f32[256,256]{1,0:T(8,128)S(1)}, f32[256,256]{1,0:T(8,128)S(1)}, u32[]{:S(2)}, u32[]{:S(2)}) %collective-permute-start.1) | collective-permute-done | bytes 262176 | tf_op jit(solution)/shard_map/ppermute | solution.py:127
  14.2 3.9 %collective-permute-done.2.cross = f32[256,256]{1,0:T(8,128)S(1)} collective-permute-done((f32[256,256]{1,0:T(8,128)S(1)}, f32[256,256]{1,0:T(8,128)S(1)}, u32[]{:S(2)}, u32[]{:S(2)}) %collective-permute-start.2) | collective-permute-done | bytes 262176 | tf_op jit(solution)/shard_map/ppermute | solution.py:127
  18.2 1.4 %shard_map.51 = (f32[256,256]{1,0:T(8,128)S(1)}, f32[256,256]{1,0:T(8,128)S(1)}) custom-call(s32[3]{0:T(128)S(1)} %pad_add_fusion.place, f32[256,256]{1,0:T(8,128)S(1)} %shard_map.50.own, f32[256,256]{1,0:T(8,128)S(1)} %collective-permute-done.near, f32[256,256]{1,0:T(8,128)S(1)} %collective-permute-done.1.far, f32[256,256]{1,0:T(8,128)S(1)} %collective-permute-done.2.cross), custom_call_target="tpu_custom_call" | custom-call | flops 301989888 | bytes 1048576 | tf_op jit(solution)/shard_map/pallas_call | solution.py:37
  19.6 2.8 %collective-permute-start.3 = (f32[256,256]{1,0:T(8,128)S(1)}, f32[256,256]{1,0:T(8,128)S(1)}, u32[]{:S(2)}, u32[]{:S(2)}) collective-permute-start(f32[256,256]{1,0:T(8,128)S(1)} %get-tuple-element.7.sent), channel_id=1, source_target_pairs={{0,16},{4,20},{8,24},{12,28},{16,0},{20,4},{24,8},{28,12},{1,17},{... | collective-permute-start | bytes 786440 | tf_op jit(solution)/shard_map/ppermute | solution.py:127
  22.4 0.0 copy-done.3
  22.4 0.1 copy.5.kept
  22.5 0.0 copy-done.1
  22.5 0.0 copy-start.2
  22.5 1.4 %copy-done.2 = f32[2,3,1,256,256]{4,3,2,1,0:T(8,128)S(1)} copy-done((f32[2,3,1,256,256]{4,3,2,1,0:T(8,128)S(1)}, f32[2,3,1,256,256]{4,3,2,1,0:T(8,128)}, u32[]{:S(2)}) %copy-start.2) | copy-done | bytes 1572888
  23.9 3.5 %shard_map.52 = (f32[2,256,256]{2,1,0:T(8,128)S(1)}, f32[2,3,256,256]{3,2,1,0:T(8,128)S(1)}, f32[256,256]{1,0:T(8,128)S(1)}) custom-call(s32[3]{0:T(128)S(1)} %pad_add_fusion.place, s32[2,1]{1,0:T(2,128)S(1)} %copy.5.kept, f32[2,1,256,256]{3,2,1,0:T(8,128)S(1)} %copy-done.1, f32[256,256]{1,0:T(8,128)S(1)} %collective-permute-done.near, ...), custom_call_target="tpu_custom_call" | custom-call | flops 2415919104 | bytes 1048576 | tf_op jit(solution)/shard_map/pallas_call | solution.py:37
  27.5 5.9 %collective-permute-done.3.x = f32[256,256]{1,0:T(8,128)S(1)} collective-permute-done((f32[256,256]{1,0:T(8,128)S(1)}, f32[256,256]{1,0:T(8,128)S(1)}, u32[]{:S(2)}, u32[]{:S(2)}) %collective-permute-start.3) | collective-permute-done | bytes 262176 | tf_op jit(solution)/shard_map/ppermute | solution.py:127
  33.4 0.4 shard_map.54
  33.8 0.1 collective-permute-start.4
  33.9 1.4 %collective-permute-start.5 = (f32[8,256]{1,0:T(8,128)S(1)}, f32[8,256]{1,0:T(8,128)S(1)}, u32[]{:S(2)}, u32[]{:S(2)}) collective-permute-start(f32[8,256]{1,0:T(8,128)S(1)} %shard_map.54), channel_id=1, source_target_pairs={{0,2},{1,3},{2,0},{3,1},{4,6},{5,7},{6,4},{7,5},{8,10},{9,11},{10,... | collective-permute-start | bytes 24584 | tf_op jit(solution)/shard_map/ppermute | solution.py:149
  35.3 0.5 %collective-permute-start.6 = (f32[8,256]{1,0:T(8,128)S(1)}, f32[8,256]{1,0:T(8,128)S(1)}, u32[]{:S(2)}, u32[]{:S(2)}) collective-permute-start(f32[8,256]{1,0:T(8,128)S(1)} %shard_map.54), channel_id=1, source_target_pairs={{0,3},{1,2},{2,1},{3,0},{4,7},{5,6},{6,5},{7,4},{8,11},{9,10},{10,... | collective-permute-start | bytes 24584 | tf_op jit(solution)/shard_map/ppermute | solution.py:149
  35.7 1.4 %shard_map.53 = f32[2,1,256,256]{3,2,1,0:T(8,128)} custom-call(s32[3]{0:T(128)S(1)} %pad_add_fusion.place, f32[256,256]{1,0:T(8,128)S(1)} %collective-permute-done.3.x, f32[2,256,256]{2,1,0:T(8,128)S(1)} %get-tuple-element.9.lefts), custom_call_target="tpu_custom_call" | custom-call | flops 201326592 | bytes 1048576 | tf_op jit(solution)/shard_map/pallas_call | solution.py:37
  37.1 0.0 collective-permute-done.4
  37.1 0.5 %collective-permute-done.5 = f32[8,256]{1,0:T(8,128)S(1)} collective-permute-done((f32[8,256]{1,0:T(8,128)S(1)}, f32[8,256]{1,0:T(8,128)S(1)}, u32[]{:S(2)}, u32[]{:S(2)}) %collective-permute-start.5) | collective-permute-done | bytes 8224 | tf_op jit(solution)/shard_map/ppermute | solution.py:149
  37.6 0.7 %collective-permute-done.6 = f32[8,256]{1,0:T(8,128)S(1)} collective-permute-done((f32[8,256]{1,0:T(8,128)S(1)}, f32[8,256]{1,0:T(8,128)S(1)}, u32[]{:S(2)}, u32[]{:S(2)}) %collective-permute-start.6) | collective-permute-done | bytes 8224 | tf_op jit(solution)/shard_map/ppermute | solution.py:149
  38.3 0.1 add_reduce_fusion
  38.4 0.6 %slice.7 = f32[1]{0:T(128)} slice(f32[8]{0:T(128)S(1)} %add_reduce_fusion), slice={[6:7]} | slice | bytes 8 | tf_op jit(solution)/shard_map/slice | solution.py:158
  39.0 0.6 %multiply_divide_fusion = f32[6]{0:T(128)S(1)} fusion(f32[8]{0:T(128)S(1)} %add_reduce_fusion, f32[]{:T(128)} %bitcast.3), kind=kLoop, calls=%fused_computation.2 | loop fusion | flops 12 | bytes 52 | tf_op jit(solution)/shard_map/div | solution.py:158
  39.7 0.6 %div.22 = f32[2,3]{1,0:T(2,128)} reshape(f32[6]{0:T(128)S(1)} %multiply_divide_fusion) | data formatting | bytes 48 | tf_op jit(solution)/shard_map/div | solution.py:158
Async XLA Ops:
  0.6 1.0 %copy-start = (f32[2,1,256,256]{3,2,1,0:T(8,128)S(1)}, f32[2,1,256,256]{3,2,1,0:T(8,128)}, u32[]{:S(2)}) copy-start(f32[2,1,256,256]{3,2,1,0:T(8,128)} %transfer.3) | copy-start | bytes 1572868
  1.7 20.8 %copy-start.3 = (s32[2,1]{0,1:T(1,128)S(1)}, s32[2,1]{0,1:T(1,128)}, u32[]{:S(2)}) copy-start(s32[2,1]{0,1:T(1,128)} %param.5) | copy-start | bytes 28
  1.7 20.9 %copy-start.1 = (f32[2,1,256,256]{3,2,1,0:T(8,128)S(1)}, f32[2,1,256,256]{3,2,1,0:T(8,128)}, u32[]{:S(2)}) copy-start(f32[2,1,256,256]{3,2,1,0:T(8,128)} %transfer.3) | copy-start | bytes 1572868
  2.0 9.3 %collective-permute-start = (f32[256,256]{1,0:T(8,128)S(1)}, f32[256,256]{1,0:T(8,128)S(1)}, u32[]{:S(2)}, u32[]{:S(2)}) collective-permute-start(f32[256,256]{1,0:T(8,128)S(1)} %shard_map.50.own), channel_id=1, source_target_pairs={{0,4},{4,0},{8,12},{12,8},{16,20},{20,16},{24,28},{28,24},{1,5},{5... | collective-permute-start | bytes 786440 | tf_op jit(solution)/shard_map/ppermute | solution.py:127
  5.0 9.2 %collective-permute-start.1 = (f32[256,256]{1,0:T(8,128)S(1)}, f32[256,256]{1,0:T(8,128)S(1)}, u32[]{:S(2)}, u32[]{:S(2)}) collective-permute-start(f32[256,256]{1,0:T(8,128)S(1)} %shard_map.50.own), channel_id=1, source_target_pairs={{0,8},{4,12},{8,0},{12,4},{16,24},{20,28},{24,16},{28,20},{1,9},{5... | collective-permute-start | bytes 786440 | tf_op jit(solution)/shard_map/ppermute | solution.py:127
  6.6 11.6 %collective-permute-start.2 = (f32[256,256]{1,0:T(8,128)S(1)}, f32[256,256]{1,0:T(8,128)S(1)}, u32[]{:S(2)}, u32[]{:S(2)}) collective-permute-start(f32[256,256]{1,0:T(8,128)S(1)} %shard_map.50.own), channel_id=1, source_target_pairs={{0,12},{4,8},{8,4},{12,0},{16,28},{20,24},{24,20},{28,16},{1,13},{... | collective-permute-start | bytes 786440 | tf_op jit(solution)/shard_map/ppermute | solution.py:127
  19.6 13.8 %collective-permute-start.3 = (f32[256,256]{1,0:T(8,128)S(1)}, f32[256,256]{1,0:T(8,128)S(1)}, u32[]{:S(2)}, u32[]{:S(2)}) collective-permute-start(f32[256,256]{1,0:T(8,128)S(1)} %get-tuple-element.7.sent), channel_id=1, source_target_pairs={{0,16},{4,20},{8,24},{12,28},{16,0},{20,4},{24,8},{28,12},{1,17},{... | collective-permute-start | bytes 786440 | tf_op jit(solution)/shard_map/ppermute | solution.py:127
  22.5 1.4 %copy-start.2 = (f32[2,3,1,256,256]{4,3,2,1,0:T(8,128)S(1)}, f32[2,3,1,256,256]{4,3,2,1,0:T(8,128)}, u32[]{:S(2)}) copy-start(f32[2,3,1,256,256]{4,3,2,1,0:T(8,128)} %hamiltonian.1) | copy-start | bytes 4718596
  33.8 3.3 %collective-permute-start.4 = (f32[8,256]{1,0:T(8,128)S(1)}, f32[8,256]{1,0:T(8,128)S(1)}, u32[]{:S(2)}, u32[]{:S(2)}) collective-permute-start(f32[8,256]{1,0:T(8,128)S(1)} %shard_map.54), channel_id=1, source_target_pairs={{0,1},{1,0},{2,3},{3,2},{4,5},{5,4},{6,7},{7,6},{8,9},{9,8},{10,11... | collective-permute-start | bytes 24584 | tf_op jit(solution)/shard_map/ppermute | solution.py:149
  33.9 3.7 %collective-permute-start.5 = (f32[8,256]{1,0:T(8,128)S(1)}, f32[8,256]{1,0:T(8,128)S(1)}, u32[]{:S(2)}, u32[]{:S(2)}) collective-permute-start(f32[8,256]{1,0:T(8,128)S(1)} %shard_map.54), channel_id=1, source_target_pairs={{0,2},{1,3},{2,0},{3,1},{4,6},{5,7},{6,4},{7,5},{8,10},{9,11},{10,... | collective-permute-start | bytes 24584 | tf_op jit(solution)/shard_map/ppermute | solution.py:149
  35.3 3.1 %collective-permute-start.6 = (f32[8,256]{1,0:T(8,128)S(1)}, f32[8,256]{1,0:T(8,128)S(1)}, u32[]{:S(2)}, u32[]{:S(2)}) collective-permute-start(f32[8,256]{1,0:T(8,128)S(1)} %shard_map.54), channel_id=1, source_target_pairs={{0,3},{1,2},{2,1},{3,0},{4,7},{5,6},{6,5},{7,4},{8,11},{9,10},{10,... | collective-permute-start | bytes 24584 | tf_op jit(solution)/shard_map/ppermute | solution.py:149

commit v2 on v0

v2 whole, which is shorter than its diff:
```python
import jax
import jax.numpy as jnp
from jax import lax
from jax.experimental import pallas as pl
from jax.experimental.pallas import tpu as pltpu
from jax.sharding import PartitionSpec as P

F32 = jnp.float32
BF16 = jnp.bfloat16
VMEM = pl.BlockSpec(memory_space=pltpu.VMEM)
SMEM = pl.BlockSpec(memory_space=pltpu.SMEM)
LIMIT = 40 * 1024 * 1024
LANES = 128
TN = ((0,), (0,))


def split(a):
    high = a.astype(BF16)
    return high, (a - high.astype(F32)).astype(BF16)


def dot(a, b, over):
    return lax.dot_general(a, b, (over, ((), ())), preferred_element_type=F32)


def multiply(a, b, over=((1,), (0,))):
    return dot(a[0], b[0], over) + (dot(a[0], b[1], over) + dot(a[1], b[0], over))


def product(a, b):
    return multiply(split(a), split(b))


def bit(k):
    return (lax.axis_index("col") // k) % 2 == 1


def eye(width):
    rows = lax.broadcasted_iota(jnp.int32, (width, width), 0)
    return (rows == lax.broadcasted_iota(jnp.int32, (width, width), 1)).astype(F32)


def group_kernel(transfer, out):
    out[...] = product(transfer[0, 0], transfer[1, 0])


def quad_kernel(own, near, far, cross, whole, other_out):
    odd, high = bit(1), bit(2)
    own, near, far, cross = own[...], near[...], far[...], cross[...]
    mine = product(jnp.where(odd, near, own), jnp.where(odd, own, near))
    other = product(jnp.where(odd, cross, far), jnp.where(odd, far, cross))
    other_out[...] = other
    whole[...] = product(jnp.where(high, other, mine), jnp.where(high, mine, other))


def sides_kernel(near, other, left_out, right_out):
    odd, high = bit(1), bit(2)
    near, other = near[...], other[...]
    one = eye(near.shape[0])
    left_out[...] = product(jnp.where(high, other, one), jnp.where(odd, near, one))
    right_out[...] = product(jnp.where(odd, one, near), jnp.where(high, one, other))


def level_kernel(k, whole, left, right, x, whole_out, left_out, right_out):
    after = bit(k)
    whole, left, right, x = whole[...], left[...], right[...], x[...]
    one = eye(whole.shape[0])
    whole_out[...] = product(jnp.where(after, x, whole), jnp.where(after, whole, x))
    left_out[...] = product(jnp.where(after, x, one), left)
    right_out[...] = product(right, jnp.where(after, one, x))


def shares_kernel(k, whole, sent, share, rest):
    @pl.when(bit(k))
    def _():
        sent[...] = whole[...].T

    @pl.when(jnp.logical_not(bit(k)))
    def _():
        sent[...] = whole[...]

    rows = share.shape[0]
    share[...] = sent[pl.ds(pl.multiple_of(bit(1).astype(jnp.int32) * rows, rows), rows)]
    rest[...] = sent[2 * rows :]


def terms_kernel(k, kept, transfer, left, right, sent, hamiltonian, lefts_out, terms_out, norm_out):
    upper = bit(k)
    columns, terms, width = terms_out.shape[0], terms_out.shape[1], left.shape[0]
    lefts = [left[...], product(left[...], transfer[0, 0])]
    rights = [product(transfer[1, 0], right[...]), right[...]]
    y = split(sent[...])
    norm_out[...] = multiply(y, y, TN)
    column = lax.broadcasted_iota(jnp.int32, (width, width), 1)
    for c in range(columns):
        masked = jnp.where(column < kept[c, 0], lefts[c], 0.0)
        lefts_out[c] = masked
        a = split(jnp.where(upper, masked, multiply(y, split(masked), TN)))
        b = split(jnp.where(upper, multiply(split(rights[c]), y), rights[c]))
        for t in range(terms):
            inner = multiply(a, split(hamiltonian[c, t, 0]))
            terms_out[c, t] = multiply(split(inner), b)


def finish_kernel(share, swapped, rest, terms, norm, out, x):
    rows = share.shape[0]
    at = bit(1).astype(jnp.int32) * rows
    x[pl.ds(pl.multiple_of(at, rows), rows)] = share[...]
    x[pl.ds(pl.multiple_of(rows - at, rows), rows)] = swapped[...]
    x[2 * rows :] = rest[...]
    xs = split(x[...])
    z = multiply(xs, xs, TN)
    columns, count = terms.shape[0], terms.shape[1]

    def total(m):
        s = jnp.sum(z * m, axis=0, keepdims=True)
        return sum(s[:, i : i + LANES] for i in range(0, s.shape[1], LANES))

    sums = [total(terms[c, t]) for c in range(columns) for t in range(count)] + [total(norm[...])]
    sums += [jnp.zeros_like(sums[0])] * (out.shape[0] - len(sums))
    out[...] = jnp.concatenate(sums, axis=0)


def left_kernel(k, x, lefts, out):
    @pl.when(bit(k))
    def _():
        xs = split(x[...])
        for c in range(out.shape[0]):
            out[c, 0] = multiply(xs, split(lefts[c]))

    @pl.when(jnp.logical_not(bit(k)))
    def _():
        out[:, 0] = lefts[...]


def energy_kernel(scale, *refs):
    parts, out = [r[...] for r in refs[:-1]], refs[-1]
    while len(parts) > 1:
        parts = [a + b for a, b in zip(parts[::2], parts[1::2])]
    columns, terms = out.shape
    s = jnp.sum(parts[0], axis=1, keepdims=True)
    s = jnp.broadcast_to(scale * s / s[columns * terms : columns * terms + 1], parts[0].shape)
    row = lax.broadcasted_iota(jnp.int32, s.shape, 0)
    lane = lax.broadcasted_iota(jnp.int32, s.shape, 1)
    for c in range(columns):
        out[c : c + 1] = jnp.sum(jnp.where(row == c * terms + lane, s, 0.0), axis=0, keepdims=True)[:, :terms]


def call(kernel, outs, flops, *args, smem=0):
    return pl.pallas_call(
        kernel,
        out_shape=outs,
        in_specs=[SMEM] * smem + [VMEM] * (len(args) - smem),
        out_specs=jax.tree.map(lambda _: VMEM, outs),
        compiler_params=pltpu.CompilerParams(vmem_limit_bytes=LIMIT),
        cost_estimate=pl.CostEstimate(flops=flops, bytes_accessed=1 << 20, transcendentals=0),
    )(*args)


def per_device(transfer, hamiltonian, kept):
    columns, width, terms = transfer.shape[0], transfer.shape[2], hamiltonian.shape[1]
    total, sectors = lax.axis_size("col"), lax.axis_size("sec")
    half = total // 2
    one = 6 * width**3

    def array(*shape):
        return jax.ShapeDtypeStruct(shape, F32)

    matrix = array(width, width)

    def swap(a, k):
        return lax.ppermute(a, "col", [(i, i ^ k) for i in range(total)])

    group = call(group_kernel, matrix, one, transfer)
    near, far, cross = swap(group, 1), swap(group, 2), swap(group, 3)
    whole, other = call(quad_kernel, (matrix, matrix), 3 * one, group, near, far, cross)
    if total > 8:
        left, right = call(sides_kernel, (matrix, matrix), 2 * one, near, other)
        k = 4
        while k < half:
            x = swap(whole, k)
            whole, left, right = call(
                lambda *refs, k=k: level_kernel(k, *refs), (matrix,) * 3, 3 * one, whole, left, right, x
            )
            k *= 2
    rows = width // 4
    sent, share, rest = call(
        lambda *refs: shares_kernel(half, *refs), (matrix, array(rows, width), array(width - 2 * rows, width)), one, whole
    )
    share = swap(share, half)
    rest = swap(rest, half)
    swapped = swap(share, 1)
    if total <= 8:
        left, right = call(sides_kernel, (matrix, matrix), 2 * one, near, other)
    lefts, products, norm = call(
        lambda *refs: terms_kernel(half, *refs),
        (array(columns, width, width), array(columns, terms, width, width), matrix),
        24 * one,
        kept, transfer, left, right, sent, hamiltonian,
        smem=1,
    )
    table_rows = -(-(columns * terms + 1) // 8) * 8
    table, x = call(
        finish_kernel, (array(table_rows, LANES), matrix), 2 * one, share, swapped, rest, products, norm
    )
    parts = [table] + [lax.ppermute(table, "sec", [(i, i ^ k) for i in range(sectors)]) for k in range(1, sectors)]
    left_env = call(
        lambda *refs: left_kernel(half, *refs), array(columns, 1, width, width), 2 * one, x, lefts
    )
    scale = float(width * sectors)
    energy = call(lambda *refs: energy_kernel(scale, *refs), array(columns, terms), 1000, *parts)
    return left_env, energy


def solution(mesh):
    in_specs = (P("col", "sec", None, None), P("col", None, "sec", None, None), P("col", "sec"))
    out_specs = (P("col", "sec", None, None), P("col", None))
    return jax.shard_map(
        per_device, mesh=mesh, in_specs=in_specs, out_specs=out_specs, check_vma=False
    )
```

time: 104 us -> 37.7 us (0.36)
  waiting for transfers between devices: 49.4 us -> 15.6 us
  matrix products: 26.1 us -> 0 us
  between operations: 14.2 us -> 0.72 us
  starting transfers between devices: 0.04 us -> 13.5 us
  Pallas kernels: 0 us -> 6.61 us
  blocking collectives: 6.3 us -> 0 us
  other arithmetic: 3.41 us -> 0 us
  local copies, waits for them, and re-layouts: 3.77 us -> 1.14 us
    all_gather x1 -> x0, waiting for transfers between devices: 49.3 us -> none  [per_device(): groups = lax.all_gather(group[None], 'col', axis=0, tiled=True)]
    dot_general x18 -> x0, matrix products: 26.1 us -> none  [the longest x12 14.4 us: matmul(): jnp.einsum('sij,sjk->sik', first, second, precision=lax.Precision.HIGHEST)]
    ppermute x0 -> x9, waiting for transfers between devices: none -> 15.6 us  [the longest x6 13.7 us: swap(): return lax.ppermute(a, 'col', [(i, i ^ k) for i in range(total)])]
    ppermute x0 -> x9, starting transfers between devices: none -> 13.5 us  [the longest x6 11.5 us: swap(): return lax.ppermute(a, 'col', [(i, i ^ k) for i in range(total)])]
    pallas_call x0 -> x8, Pallas kernels: none -> 6.61 us  [call(): pl.pallas_call(kernel, out_shape=outs, in_specs=[SMEM] * smem + [VMEM] *...]
    psum x1 -> x0, blocking collectives: 6.3 us -> none  [per_device(): partial_value, norm = lax.psum((partial_value, norm), 'sec')]
    slice x1 -> x0, local copies, waits for them, and re-layouts: 1.38 us -> none  [per_device(): kept[column][:, None]]
    convert_element_type x3 -> x0, other arithmetic: 1.33 us -> none  [the longest x2 1.32 us: per_device(): (column_positions[None, :] < kept[column][:, None]).astype(jnp.float32)]
  transfers between devices with their start and end apart: 1 -> 9, of which waited for: 1 -> 6; matrix products, arithmetic and copies ran while one was open for 4% -> 0% of each run, Pallas kernels for 0% -> 12%
where the time goes in v2:
time: 37.7 us; the launch traced here: 37.5 us
  waiting for transfers between devices  15.6 us (41%)
  starting transfers between devices  13.5 us (36%)
  Pallas kernels  6.61 us (18%)
  local copies, waits for them, and re-layouts  1.14 us (3%)
  between operations  0.72 us (2%)
    ppermute x6, waiting for transfers between devices, swap(): return lax.ppermute(a, 'col', [(i, i ^ k) for i in range(total)])  13.7 us
    ppermute x6, starting transfers between devices, swap(): return lax.ppermute(a, 'col', [(i, i ^ k) for i in range(total)])  11.5 us
    pallas_call x8, Pallas kernels, call(): pl.pallas_call(kernel, out_shape=outs, in_specs=[SMEM] * smem + [VMEM] *...  6.61 us
    ppermute x3, starting transfers between devices, per_device(): lax.ppermute(table, 'sec', [(i, i ^ k) for i in range(sectors)])  1.93 us
    ppermute x3, waiting for transfers between devices, per_device(): lax.ppermute(table, 'sec', [(i, i ^ k) for i in range(sectors)])  1.91 us
    unnamed x9, local copies, waits for them, and re-layouts  1.14 us
  transfers between devices with their start and end apart: 9, of which 6 were waited for; matrix products, arithmetic and copies ran while one was open for 0% of the time, Pallas kernels for 12%

profile of v2, /device:TPU:0, one launch (start us, length us, event | category | flops | bytes accessed | tf_op | source)
XLA Modules:
  0.0 37.5 jit_solution(8288202602742148286)
XLA Ops:
  0.6 0.0 copy-start
  0.6 1.0 %copy-done = f32[2,1,256,256]{3,2,1,0:T(8,128)S(1)} copy-done((f32[2,1,256,256]{3,2,1,0:T(8,128)S(1)}, f32[2,1,256,256]{3,2,1,0:T(8,128)}, u32[]{:S(2)}) %copy-start) | copy-done | bytes 524312
  1.7 0.0 copy-start.3
  1.7 0.0 copy-start.1
  1.7 0.0 copy-start.2
  1.7 0.3 shard_map.50.own
  2.0 3.0 %collective-permute-start = (f32[256,256]{1,0:T(8,128)S(1)}, f32[256,256]{1,0:T(8,128)S(1)}, u32[]{:S(2)}, u32[]{:S(2)}) collective-permute-start(f32[256,256]{1,0:T(8,128)S(1)} %shard_map.50.own), channel_id=1, source_target_pairs={{0,4},{4,0},{8,12},{12,8},{16,20},{20,16},{24,28},{28,24},{1,5},{5... | collective-permute-start | bytes 786440 | tf_op jit(solution)/shard_map/ppermute | solution.py:172
  5.0 1.6 %collective-permute-start.1 = (f32[256,256]{1,0:T(8,128)S(1)}, f32[256,256]{1,0:T(8,128)S(1)}, u32[]{:S(2)}, u32[]{:S(2)}) collective-permute-start(f32[256,256]{1,0:T(8,128)S(1)} %shard_map.50.own), channel_id=1, source_target_pairs={{0,8},{4,12},{8,0},{12,4},{16,24},{20,28},{24,16},{28,20},{1,9},{5... | collective-permute-start | bytes 786440 | tf_op jit(solution)/shard_map/ppermute | solution.py:172
  6.6 0.0 collective-permute-start.2
  6.6 4.7 %collective-permute-done.near = f32[256,256]{1,0:T(8,128)S(1)} collective-permute-done((f32[256,256]{1,0:T(8,128)S(1)}, f32[256,256]{1,0:T(8,128)S(1)}, u32[]{:S(2)}, u32[]{:S(2)}) %collective-permute-start) | collective-permute-done | bytes 262176 | tf_op jit(solution)/shard_map/ppermute | solution.py:172
  11.3 2.9 %collective-permute-done.1.far = f32[256,256]{1,0:T(8,128)S(1)} collective-permute-done((f32[256,256]{1,0:T(8,128)S(1)}, f32[256,256]{1,0:T(8,128)S(1)}, u32[]{:S(2)}, u32[]{:S(2)}) %collective-permute-start.1) | collective-permute-done | bytes 262176 | tf_op jit(solution)/shard_map/ppermute | solution.py:172
  14.2 3.9 %collective-permute-done.2.cross = f32[256,256]{1,0:T(8,128)S(1)} collective-permute-done((f32[256,256]{1,0:T(8,128)S(1)}, f32[256,256]{1,0:T(8,128)S(1)}, u32[]{:S(2)}, u32[]{:S(2)}) %collective-permute-start.2) | collective-permute-done | bytes 262176 | tf_op jit(solution)/shard_map/ppermute | solution.py:172
  18.2 0.8 %shard_map.51 = (f32[256,256]{1,0:T(8,128)S(1)}, f32[256,256]{1,0:T(8,128)S(1)}) custom-call(f32[256,256]{1,0:T(8,128)S(1)} %shard_map.50.own, f32[256,256]{1,0:T(8,128)S(1)} %collective-permute-done.near, f32[256,256]{1,0:T(8,128)S(1)} %collective-permute-done.1.far, f32[256,256]{1,0:T(8,128)S(1)} %collective-permute-done.2.cross), custom_call_target="tpu_custom_call" | custom-call | flops 301989888 | bytes 1048576 | tf_op jit(solution)/shard_map/pallas_call | solution.py:150
  19.0 0.1 shard_map.52
  19.1 2.9 %collective-permute-start.3 = (f32[64,256]{1,0:T(8,128)S(1)}, f32[64,256]{1,0:T(8,128)S(1)}, u32[]{:S(2)}, u32[]{:S(2)}) collective-permute-start(f32[64,256]{1,0:T(8,128)S(1)} %get-tuple-element.15), channel_id=1, source_target_pairs={{0,16},{4,20},{8,24},{12,28},{16,0},{20,4},{24,8},{28,12},{1,17},{... | collective-permute-start | bytes 196616 | tf_op jit(solution)/shard_map/ppermute | solution.py:172
  22.0 0.0 copy-done.3
  22.0 0.1 copy.5.refs_0_
  22.1 0.1 collective-permute-start.5
  22.2 0.4 %shard_map.53 = (f32[256,256]{1,0:T(8,128)S(1)}, f32[256,256]{1,0:T(8,128)S(1)}) custom-call(f32[256,256]{1,0:T(8,128)S(1)} %collective-permute-done.near, f32[256,256]{1,0:T(8,128)S(1)} %get-tuple-element.17.other), custom_call_target="tpu_custom_call" | custom-call | flops 201326592 | bytes 1048576 | tf_op jit(solution)/shard_map/pallas_call | solution.py:150
  22.6 2.1 %collective-permute-done.3.share = f32[64,256]{1,0:T(8,128)S(1)} collective-permute-done((f32[64,256]{1,0:T(8,128)S(1)}, f32[64,256]{1,0:T(8,128)S(1)}, u32[]{:S(2)}, u32[]{:S(2)}) %collective-permute-start.3) | collective-permute-done | bytes 65568 | tf_op jit(solution)/shard_map/ppermute | solution.py:172
  24.7 3.9 %collective-permute-start.4 = (f32[64,256]{1,0:T(8,128)S(1)}, f32[64,256]{1,0:T(8,128)S(1)}, u32[]{:S(2)}, u32[]{:S(2)}) collective-permute-start(f32[64,256]{1,0:T(8,128)S(1)} %collective-permute-done.3.share), channel_id=1, source_target_pairs={{0,4},{4,0},{8,12},{12,8},{16,20},{20,16},{24,28},{28,24},{1,5},{5... | collective-permute-start | bytes 196616 | tf_op jit(solution)/shard_map/ppermute | solution.py:172
  28.6 0.0 copy-done.1
  28.6 0.0 copy-done.2
  28.6 3.1 %shard_map.54 = (f32[2,256,256]{2,1,0:T(8,128)S(1)}, f32[2,3,256,256]{3,2,1,0:T(8,128)S(1)}, f32[256,256]{1,0:T(8,128)S(1)}) custom-call(s32[2,1]{1,0:T(2,128)S(1)} %copy.5.refs_0_, f32[2,1,256,256]{3,2,1,0:T(8,128)S(1)} %copy-done.1, f32[256,256]{1,0:T(8,128)S(1)} %get-tuple-element.18.refs_2_, f32[256,256]{1,0:T(8,128)S(1)} %get-tuple-element.19.refs_3_, ...), custom_call_target="tpu_custom_call" | custom-call | flops 2415919104 | bytes 1048576 | tf_op jit(solution)/shard_map/pallas_call | solution.py:150
  31.7 0.0 collective-permute-done.5.rest
  31.7 0.0 collective-permute-done.4.swapped
  31.7 0.4 %shard_map.55 = (f32[8,128]{1,0:T(8,128)S(1)}, f32[256,256]{1,0:T(8,128)S(1)}) custom-call(f32[64,256]{1,0:T(8,128)S(1)} %collective-permute-done.3.share, f32[64,256]{1,0:T(8,128)S(1)} %collective-permute-done.4.swapped, f32[128,256]{1,0:T(8,128)S(1)} %collective-permute-done.5.rest, f32[2,3,256,256]{3,2,1,0:T(8,128)S(1)} %get-tuple-element.21.terms, ...), custom_call_target="tpu_custom_call" | custom-call | flops 201326592 | bytes 1048576 | tf_op jit(solution)/shard_map/pallas_call | solution.py:150
  32.2 0.1 collective-permute-start.6
  32.2 1.6 %collective-permute-start.7 = (f32[8,128]{1,0:T(8,128)S(1)}, f32[8,128]{1,0:T(8,128)S(1)}, u32[]{:S(2)}, u32[]{:S(2)}) collective-permute-start(f32[8,128]{1,0:T(8,128)S(1)} %get-tuple-element.25.refs_0_), channel_id=1, source_target_pairs={{0,2},{1,3},{2,0},{3,1},{4,6},{5,7},{6,4},{7,5},{8,10},{9,11},{10,... | collective-permute-start | bytes 12296 | tf_op jit(solution)/shard_map/ppermute | solution.py:206
  33.8 0.3 collective-permute-start.8
  34.1 0.8 %shard_map.56 = f32[2,1,256,256]{3,2,1,0:T(8,128)} custom-call(f32[256,256]{1,0:T(8,128)S(1)} %get-tuple-element.23.refs_0_, f32[2,256,256]{2,1,0:T(8,128)S(1)} %get-tuple-element.24.refs_1_), custom_call_target="tpu_custom_call" | custom-call | flops 201326592 | bytes 1048576 | tf_op jit(solution)/shard_map/pallas_call | solution.py:150
  34.9 0.0 collective-permute-done.6.refs_1_
  34.9 1.0 %collective-permute-done.7.refs_2_ = f32[8,128]{1,0:T(8,128)S(1)} collective-permute-done((f32[8,128]{1,0:T(8,128)S(1)}, f32[8,128]{1,0:T(8,128)S(1)}, u32[]{:S(2)}, u32[]{:S(2)}) %collective-permute-start.7) | collective-permute-done | bytes 4128 | tf_op jit(solution)/shard_map/ppermute | solution.py:206
  35.9 0.9 %collective-permute-done.8.refs_3_ = f32[8,128]{1,0:T(8,128)S(1)} collective-permute-done((f32[8,128]{1,0:T(8,128)S(1)}, f32[8,128]{1,0:T(8,128)S(1)}, u32[]{:S(2)}, u32[]{:S(2)}) %collective-permute-start.8) | collective-permute-done | bytes 4128 | tf_op jit(solution)/shard_map/ppermute | solution.py:206
  36.8 0.7 %shard_map.57 = f32[2,3]{1,0:T(2,128)} custom-call(f32[8,128]{1,0:T(8,128)S(1)} %get-tuple-element.25.refs_0_, f32[8,128]{1,0:T(8,128)S(1)} %collective-permute-done.6.refs_1_, f32[8,128]{1,0:T(8,128)S(1)} %collective-permute-done.7.refs_2_, f32[8,128]{1,0:T(8,128)S(1)} %collective-permute-done.8.refs_3_), custom_call_target="tpu_custom_call" | custom-call | flops 1000 | bytes 1048576 | tf_op jit(solution)/shard_map/pallas_call | solution.py:150
Async XLA Ops:
  0.6 1.0 %copy-start = (f32[2,1,256,256]{3,2,1,0:T(8,128)S(1)}, f32[2,1,256,256]{3,2,1,0:T(8,128)}, u32[]{:S(2)}) copy-start(f32[2,1,256,256]{3,2,1,0:T(8,128)} %refs_1_.1) | copy-start | bytes 1572868
  1.7 20.3 %copy-start.3 = (s32[2,1]{0,1:T(1,128)S(1)}, s32[2,1]{0,1:T(1,128)}, u32[]{:S(2)}) copy-start(s32[2,1]{0,1:T(1,128)} %param.5) | copy-start | bytes 28
  1.7 26.9 %copy-start.1 = (f32[2,1,256,256]{3,2,1,0:T(8,128)S(1)}, f32[2,1,256,256]{3,2,1,0:T(8,128)}, u32[]{:S(2)}) copy-start(f32[2,1,256,256]{3,2,1,0:T(8,128)} %refs_1_.1) | copy-start | bytes 1572868
  1.7 26.9 %copy-start.2 = (f32[2,3,1,256,256]{4,3,2,1,0:T(8,128)S(1)}, f32[2,3,1,256,256]{4,3,2,1,0:T(8,128)}, u32[]{:S(2)}) copy-start(f32[2,3,1,256,256]{4,3,2,1,0:T(8,128)} %refs_5_.1) | copy-start | bytes 4718596
  2.0 9.3 %collective-permute-start = (f32[256,256]{1,0:T(8,128)S(1)}, f32[256,256]{1,0:T(8,128)S(1)}, u32[]{:S(2)}, u32[]{:S(2)}) collective-permute-start(f32[256,256]{1,0:T(8,128)S(1)} %shard_map.50.own), channel_id=1, source_target_pairs={{0,4},{4,0},{8,12},{12,8},{16,20},{20,16},{24,28},{28,24},{1,5},{5... | collective-permute-start | bytes 786440 | tf_op jit(solution)/shard_map/ppermute | solution.py:172
  5.0 9.2 %collective-permute-start.1 = (f32[256,256]{1,0:T(8,128)S(1)}, f32[256,256]{1,0:T(8,128)S(1)}, u32[]{:S(2)}, u32[]{:S(2)}) collective-permute-start(f32[256,256]{1,0:T(8,128)S(1)} %shard_map.50.own), channel_id=1, source_target_pairs={{0,8},{4,12},{8,0},{12,4},{16,24},{20,28},{24,16},{28,20},{1,9},{5... | collective-permute-start | bytes 786440 | tf_op jit(solution)/shard_map/ppermute | solution.py:172
  6.6 11.6 %collective-permute-start.2 = (f32[256,256]{1,0:T(8,128)S(1)}, f32[256,256]{1,0:T(8,128)S(1)}, u32[]{:S(2)}, u32[]{:S(2)}) collective-permute-start(f32[256,256]{1,0:T(8,128)S(1)} %shard_map.50.own), channel_id=1, source_target_pairs={{0,12},{4,8},{8,4},{12,0},{16,28},{20,24},{24,20},{28,16},{1,13},{... | collective-permute-start | bytes 786440 | tf_op jit(solution)/shard_map/ppermute | solution.py:172
  19.1 5.6 %collective-permute-start.3 = (f32[64,256]{1,0:T(8,128)S(1)}, f32[64,256]{1,0:T(8,128)S(1)}, u32[]{:S(2)}, u32[]{:S(2)}) collective-permute-start(f32[64,256]{1,0:T(8,128)S(1)} %get-tuple-element.15), channel_id=1, source_target_pairs={{0,16},{4,20},{8,24},{12,28},{16,0},{20,4},{24,8},{28,12},{1,17},{... | collective-permute-start | bytes 196616 | tf_op jit(solution)/shard_map/ppermute | solution.py:172
  22.1 9.6 %collective-permute-start.5 = (f32[128,256]{1,0:T(8,128)S(1)}, f32[128,256]{1,0:T(8,128)S(1)}, u32[]{:S(2)}, u32[]{:S(2)}) collective-permute-start(f32[128,256]{1,0:T(8,128)S(1)} %get-tuple-element.16), channel_id=1, source_target_pairs={{0,16},{4,20},{8,24},{12,28},{16,0},{20,4},{24,8},{28,12},{1,17},{... | collective-permute-start | bytes 393224 | tf_op jit(solution)/shard_map/ppermute | solution.py:172
  24.7 7.1 %collective-permute-start.4 = (f32[64,256]{1,0:T(8,128)S(1)}, f32[64,256]{1,0:T(8,128)S(1)}, u32[]{:S(2)}, u32[]{:S(2)}) collective-permute-start(f32[64,256]{1,0:T(8,128)S(1)} %collective-permute-done.3.share), channel_id=1, source_target_pairs={{0,4},{4,0},{8,12},{12,8},{16,20},{20,16},{24,28},{28,24},{1,5},{5... | collective-permute-start | bytes 196616 | tf_op jit(solution)/shard_map/ppermute | solution.py:172
  32.2 2.8 %collective-permute-start.6 = (f32[8,128]{1,0:T(8,128)S(1)}, f32[8,128]{1,0:T(8,128)S(1)}, u32[]{:S(2)}, u32[]{:S(2)}) collective-permute-start(f32[8,128]{1,0:T(8,128)S(1)} %get-tuple-element.25.refs_0_), channel_id=1, source_target_pairs={{0,1},{1,0},{2,3},{3,2},{4,5},{5,4},{6,7},{7,6},{8,9},{9,8},{10,11... | collective-permute-start | bytes 12296 | tf_op jit(solution)/shard_map/ppermute | solution.py:206
  32.2 3.7 %collective-permute-start.7 = (f32[8,128]{1,0:T(8,128)S(1)}, f32[8,128]{1,0:T(8,128)S(1)}, u32[]{:S(2)}, u32[]{:S(2)}) collective-permute-start(f32[8,128]{1,0:T(8,128)S(1)} %get-tuple-element.25.refs_0_), channel_id=1, source_target_pairs={{0,2},{1,3},{2,0},{3,1},{4,6},{5,7},{6,4},{7,5},{8,10},{9,11},{10,... | collective-permute-start | bytes 12296 | tf_op jit(solution)/shard_map/ppermute | solution.py:206
  33.8 3.0 %collective-permute-start.8 = (f32[8,128]{1,0:T(8,128)S(1)}, f32[8,128]{1,0:T(8,128)S(1)}, u32[]{:S(2)}, u32[]{:S(2)}) collective-permute-start(f32[8,128]{1,0:T(8,128)S(1)} %get-tuple-element.25.refs_0_), channel_id=1, source_target_pairs={{0,3},{1,2},{2,1},{3,0},{4,7},{5,6},{6,5},{7,4},{8,11},{9,10},{10,... | collective-permute-start | bytes 12296 | tf_op jit(solution)/shard_map/ppermute | solution.py:206

commit v3 on v2

--- a/solution.py
+++ b/solution.py
@@ -11,6 +11,7 @@
 SMEM = pl.BlockSpec(memory_space=pltpu.SMEM)
 LIMIT = 40 * 1024 * 1024
 LANES = 128
+FIRST = 10
 TN = ((0,), (0,))
 
 
@@ -40,25 +41,103 @@
     return (rows == lax.broadcasted_iota(jnp.int32, (width, width), 1)).astype(F32)
 
 
-def group_kernel(transfer, out):
-    out[...] = product(transfer[0, 0], transfer[1, 0])
-
-
-def quad_kernel(own, near, far, cross, whole, other_out):
+def group_kernel(transfer, whole, *parts):
+    group = product(transfer[0, 0], transfer[1, 0])
+
+    @pl.when(bit(1))
+    def _():
+        whole[...] = group.T
+
+    @pl.when(jnp.logical_not(bit(1)))
+    def _():
+        whole[...] = group
+
+    at = 0
+    for part in parts:
+        part[...] = whole[at : at + part.shape[0]]
+        at += part.shape[0]
+
+
+def pair_kernel(near, own, out):
+    out[...] = multiply(split(near[...]), split(own[...]), ((1,), (1,)))
+
+
+def whole_of(parts):
+    return jnp.concatenate([part[...] for part in parts], axis=0)
+
+
+def begin_kernel(n, *refs):
+    pairs, fars, out = refs[:n], refs[n:-1], refs[-1]
+    pair, far = whole_of(pairs), whole_of(fars)
+    rows = far.shape[0]
+
+    @pl.when(bit(1) == bit(2))
+    def _():
+        out[:rows] = product(far, pair)
+        out[rows:] = jnp.zeros_like(out[rows:])
+
+    @pl.when(bit(1) != bit(2))
+    def _():
+        out[...] = product(pair[:, :rows], far)
+
+
+def end_quad(begun, pairs, far, room):
+    pair, far = whole_of(pairs), far[...]
+    at = pair.shape[0] - far.shape[0]
+
+    @pl.when(bit(1) == bit(2))
+    def _():
+        room[:at] = begun[:at]
+        room[at:] = product(far, pair)
+
+    @pl.when(bit(1) != bit(2))
+    def _():
+        room[...] = begun[...] + product(pair[:, at:], far)
+
+    return room[...]
+
+
+def quad_kernel(n, begun, *refs):
+    pairs, (far, whole, room) = refs[:n], refs[n:]
+    value = end_quad(begun, pairs, far, room)
+    whole[...] = jnp.where(bit(1), value, value.T)
+
+
+def spread(value, flip, sent, share, rest):
+    @pl.when(flip)
+    def _():
+        sent[...] = value.T
+
+    @pl.when(jnp.logical_not(flip))
+    def _():
+        sent[...] = value
+
+    rows = share.shape[0]
+    share[...] = sent[pl.ds(pl.multiple_of(bit(1).astype(jnp.int32) * rows, rows), rows)]
+    rest[...] = sent[2 * rows :]
+
+
+def quad_shares_kernel(n, k, begun, *refs):
+    pairs, (far, sent, share, rest, room) = refs[:n], refs[n:]
+    spread(end_quad(begun, pairs, far, room), bit(1) == bit(k), sent, share, rest)
+
+
+def shares_kernel(k, whole, sent, share, rest):
+    spread(whole[...], bit(k), sent, share, rest)
+
+
+def sides(nears, fars):
     odd, high = bit(1), bit(2)
-    own, near, far, cross = own[...], near[...], far[...], cross[...]
-    mine = product(jnp.where(odd, near, own), jnp.where(odd, own, near))
-    other = product(jnp.where(odd, cross, far), jnp.where(odd, far, cross))
-    other_out[...] = other
-    whole[...] = product(jnp.where(high, other, mine), jnp.where(high, mine, other))
-
-
-def sides_kernel(near, other, left_out, right_out):
-    odd, high = bit(1), bit(2)
-    near, other = near[...], other[...]
+    near, other = whole_of(nears), whole_of(fars)
+    near, other = jnp.where(odd, near, near.T), jnp.where(odd, other, other.T)
     one = eye(near.shape[0])
-    left_out[...] = product(jnp.where(high, other, one), jnp.where(odd, near, one))
-    right_out[...] = product(jnp.where(odd, one, near), jnp.where(high, one, other))
+    left = product(jnp.where(high, other, one), jnp.where(odd, near, one))
+    right = product(jnp.where(odd, one, near), jnp.where(high, one, other))
+    return left, right
+
+
+def sides_kernel(n, *refs):
+    refs[2 * n][...], refs[2 * n + 1][...] = sides(refs[:n], refs[n : 2 * n])
 
 
 def level_kernel(k, whole, left, right, x, whole_out, left_out, right_out):
@@ -70,36 +149,35 @@
     right_out[...] = product(right, jnp.where(after, one, x))
 
 
-def shares_kernel(k, whole, sent, share, rest):
-    @pl.when(bit(k))
-    def _():
-        sent[...] = whole[...].T
-
-    @pl.when(jnp.logical_not(bit(k)))
-    def _():
-        sent[...] = whole[...]
-
-    rows = share.shape[0]
-    share[...] = sent[pl.ds(pl.multiple_of(bit(1).astype(jnp.int32) * rows, rows), rows)]
-    rest[...] = sent[2 * rows :]
-
-
-def terms_kernel(k, kept, transfer, left, right, sent, hamiltonian, lefts_out, terms_out, norm_out):
+def prepare(k, kept, transfer, left, right, sent, lefts_out, norm_out, a_out, b_out):
     upper = bit(k)
-    columns, terms, width = terms_out.shape[0], terms_out.shape[1], left.shape[0]
-    lefts = [left[...], product(left[...], transfer[0, 0])]
-    rights = [product(transfer[1, 0], right[...]), right[...]]
+    width = left.shape[0]
+    lefts = [left, product(left, transfer[0, 0])]
+    rights = [product(transfer[1, 0], right), right]
     y = split(sent[...])
     norm_out[...] = multiply(y, y, TN)
     column = lax.broadcasted_iota(jnp.int32, (width, width), 1)
-    for c in range(columns):
+    for c in range(len(lefts)):
         masked = jnp.where(column < kept[c, 0], lefts[c], 0.0)
         lefts_out[c] = masked
-        a = split(jnp.where(upper, masked, multiply(y, split(masked), TN)))
-        b = split(jnp.where(upper, multiply(split(rights[c]), y), rights[c]))
-        for t in range(terms):
-            inner = multiply(a, split(hamiltonian[c, t, 0]))
-            terms_out[c, t] = multiply(split(inner), b)
+        a_out[c, 0], a_out[c, 1] = split(jnp.where(upper, masked, multiply(y, split(masked), TN)))
+        b_out[c, 0], b_out[c, 1] = split(jnp.where(upper, multiply(split(rights[c]), y), rights[c]))
+
+
+def prepare_quad_kernel(n, k, kept, transfer, sent, *refs):
+    left, right = sides(refs[:n], refs[n : 2 * n])
+    prepare(k, kept, transfer, left, right, sent, *refs[2 * n :])
+
+
+def prepare_kernel(k, kept, transfer, sent, left, right, *outs):
+    prepare(k, kept, transfer, left[...], right[...], sent, *outs)
+
+
+def terms_kernel(a, b, hamiltonian, out):
+    for c in range(out.shape[0]):
+        for t in range(out.shape[1]):
+            inner = multiply((a[c, 0], a[c, 1]), split(hamiltonian[c, t, 0]))
+            out[c, t] = multiply(split(inner), (b[c, 0], b[c, 1]))
 
 
 def finish_kernel(share, swapped, rest, terms, norm, out, x):
@@ -146,12 +224,13 @@
         out[c : c + 1] = jnp.sum(jnp.where(row == c * terms + lane, s, 0.0), axis=0, keepdims=True)[:, :terms]
 
 
-def call(kernel, outs, flops, *args, smem=0):
+def call(kernel, outs, flops, *args, smem=0, scratch=()):
     return pl.pallas_call(
         kernel,
         out_shape=outs,
         in_specs=[SMEM] * smem + [VMEM] * (len(args) - smem),
         out_specs=jax.tree.map(lambda _: VMEM, outs),
+        scratch_shapes=list(scratch),
         compiler_params=pltpu.CompilerParams(vmem_limit_bytes=LIMIT),
         cost_estimate=pl.CostEstimate(flops=flops, bytes_accessed=1 << 20, transcendentals=0),
     )(*args)
@@ -163,19 +242,34 @@
     half = total // 2
     one = 6 * width**3
 
-    def array(*shape):
-        return jax.ShapeDtypeStruct(shape, F32)
+    def array(*shape, dtype=F32):
+        return jax.ShapeDtypeStruct(shape, dtype)
 
     matrix = array(width, width)
+    room = (pltpu.VMEM((width, width), F32),)
 
     def swap(a, k):
         return lax.ppermute(a, "col", [(i, i ^ k) for i in range(total)])
 
-    group = call(group_kernel, matrix, one, transfer)
-    near, far, cross = swap(group, 1), swap(group, 2), swap(group, 3)
-    whole, other = call(quad_kernel, (matrix, matrix), 3 * one, group, near, far, cross)
-    if total > 8:
-        left, right = call(sides_kernel, (matrix, matrix), 2 * one, near, other)
+    first = width * FIRST // 16
+    heights = (first, width - first)
+    n = len(heights)
+    own, *parts = call(group_kernel, (matrix,) + tuple(array(h, width) for h in heights), one, transfer)
+    nears = [swap(part, 1) for part in parts]
+    pairs, fars = [], []
+    for near, h in zip(nears, heights):
+        pairs.append(call(pair_kernel, array(h, width), one // n, near, own))
+        fars.append(swap(pairs[-1], 2))
+    begun = call(lambda *refs: begin_kernel(n, *refs), matrix, one, *pairs, *fars[:-1])
+    rows = width // 4
+    shared = (matrix, array(rows, width), array(width - 2 * rows, width))
+    if total <= 8:
+        sent, share, rest = call(
+            lambda *refs: quad_shares_kernel(n, half, *refs), shared, one, begun, *pairs, fars[-1], scratch=room
+        )
+    else:
+        whole = call(lambda *refs: quad_kernel(n, *refs), matrix, one, begun, *pairs, fars[-1], scratch=room)
+        left, right = call(lambda *refs: sides_kernel(n, *refs), (matrix, matrix), 2 * one, *nears, *fars)
         k = 4
         while k < half:
             x = swap(whole, k)
@@ -183,22 +277,23 @@
                 lambda *refs, k=k: level_kernel(k, *refs), (matrix,) * 3, 3 * one, whole, left, right, x
             )
             k *= 2
-    rows = width // 4
-    sent, share, rest = call(
-        lambda *refs: shares_kernel(half, *refs), (matrix, array(rows, width), array(width - 2 * rows, width)), one, whole
-    )
+        sent, share, rest = call(lambda *refs: shares_kernel(half, *refs), shared, one, whole)
     share = swap(share, half)
     rest = swap(rest, half)
+    halves = array(columns, 2, width, width, dtype=BF16)
+    prepared = (array(columns, width, width), matrix, halves, halves)
+    if total <= 8:
+        lefts, norm, a, b = call(
+            lambda *refs: prepare_quad_kernel(n, half, *refs), prepared, 9 * one, kept, transfer, sent, *nears, *fars,
+            smem=1,
+        )
+    else:
+        lefts, norm, a, b = call(
+            lambda *refs: prepare_kernel(half, *refs), prepared, 9 * one, kept, transfer, sent, left, right, smem=1
+        )
+    share, norm = lax.optimization_barrier((share, norm))
     swapped = swap(share, 1)
-    if total <= 8:
-        left, right = call(sides_kernel, (matrix, matrix), 2 * one, near, other)
-    lefts, products, norm = call(
-        lambda *refs: terms_kernel(half, *refs),
-        (array(columns, width, width), array(columns, terms, width, width), matrix),
-        24 * one,
-        kept, transfer, left, right, sent, hamiltonian,
-        smem=1,
-    )
+    products = call(terms_kernel, array(columns, terms, width, width), 12 * one, a, b, hamiltonian)
     table_rows = -(-(columns * terms + 1) // 8) * 8
     table, x = call(
         finish_kernel, (array(table_rows, LANES), matrix), 2 * one, share, swapped, rest, products, norm

time: 37.7 us -> 35.2 us (0.934)
  waiting for transfers between devices: 15.6 us -> 13.6 us
  starting transfers between devices: 13.5 us -> 12.7 us
    ppermute x6 -> x7, waiting for transfers between devices: 13.7 us -> 11.7 us  [swap(): return lax.ppermute(a, 'col', [(i, i ^ k) for i in range(total)])]
    ppermute x6 -> x7, starting transfers between devices: 11.5 us -> 10.7 us  [swap(): return lax.ppermute(a, 'col', [(i, i ^ k) for i in range(total)])]
    pallas_call x8 -> x10, Pallas kernels: 6.61 us -> 6.92 us  [call(): pl.pallas_call(kernel, out_shape=outs, in_specs=[SMEM] * smem + [VMEM] *...]
  transfers between devices with their start and end apart: 9 -> 10, of which waited for: 6 -> 7; matrix products, arithmetic and copies ran while one was open for 0% -> 0% of each run, Pallas kernels for 12% -> 15%
where the time goes in v3:
time: 35.2 us; the launch traced here: 35.1 us
  waiting for transfers between devices  13.6 us (39%)
  starting transfers between devices  12.7 us (36%)
  Pallas kernels  6.92 us (20%)
  local copies, waits for them, and re-layouts  1.14 us (3%)
  between operations  0.71 us (2%)
    ppermute x7, waiting for transfers between devices, swap(): return lax.ppermute(a, 'col', [(i, i ^ k) for i in range(total)])  11.7 us
    ppermute x7, starting transfers between devices, swap(): return lax.ppermute(a, 'col', [(i, i ^ k) for i in range(total)])  10.7 us
    pallas_call x10, Pallas kernels, call(): pl.pallas_call(kernel, out_shape=outs, in_specs=[SMEM] * smem + [VMEM] *...  6.92 us
    ppermute x3, starting transfers between devices, per_device(): lax.ppermute(table, 'sec', [(i, i ^ k) for i in range(sectors)])  1.93 us
    ppermute x3, waiting for transfers between devices, per_device(): lax.ppermute(table, 'sec', [(i, i ^ k) for i in range(sectors)])  1.9 us
    unnamed x9, local copies, waits for them, and re-layouts  1.14 us
  transfers between devices with their start and end apart: 10, of which 7 were waited for; matrix products, arithmetic and copies ran while one was open for 0% of the time, Pallas kernels for 15%

profile of v3, /device:TPU:0, one launch (start us, length us, event | category | flops | bytes accessed | tf_op | source)
XLA Modules:
  0.0 35.1 jit_solution(5194056801687462029)
XLA Ops:
  0.6 0.0 copy-start
  0.6 1.0 %copy-done = f32[2,1,256,256]{3,2,1,0:T(8,128)S(1)} copy-done((f32[2,1,256,256]{3,2,1,0:T(8,128)S(1)}, f32[2,1,256,256]{3,2,1,0:T(8,128)}, u32[]{:S(2)}) %copy-start) | copy-done | bytes 524312
  1.7 0.0 copy-start.3
  1.7 0.0 copy-start.1
  1.7 0.3 shard_map.50
  2.0 3.1 %collective-permute-start = (f32[160,256]{1,0:T(8,128)S(1)}, f32[160,256]{1,0:T(8,128)S(1)}, u32[]{:S(2)}, u32[]{:S(2)}) collective-permute-start(f32[160,256]{1,0:T(8,128)S(1)} %get-tuple-element.16), channel_id=1, source_target_pairs={{0,4},{4,0},{8,12},{12,8},{16,20},{20,16},{24,28},{28,24},{1,5},{5... | collective-permute-start | bytes 491528 | tf_op jit(solution)/shard_map/ppermute | solution.py:252
  5.1 0.1 collective-permute-start.1
  5.2 5.0 %collective-permute-done.near.refs_3_ = f32[160,256]{1,0:T(8,128)S(1)} collective-permute-done((f32[160,256]{1,0:T(8,128)S(1)}, f32[160,256]{1,0:T(8,128)S(1)}, u32[]{:S(2)}, u32[]{:S(2)}) %collective-permute-start) | collective-permute-done | bytes 163872 | tf_op jit(solution)/shard_map/ppermute | solution.py:252
  10.1 0.3 shard_map.51.refs_0_.refs_1_
  10.4 2.0 %collective-permute-start.2 = (f32[160,256]{1,0:T(8,128)S(1)}, f32[160,256]{1,0:T(8,128)S(1)}, u32[]{:S(2)}, u32[]{:S(2)}) collective-permute-start(f32[160,256]{1,0:T(8,128)S(1)} %shard_map.51.refs_0_.refs_1_), channel_id=1, source_target_pairs={{0,8},{4,12},{8,0},{12,4},{16,24},{20,28},{24,16},{28,20},{1,9},{5... | collective-permute-start | bytes 491528 | tf_op jit(solution)/shard_map/ppermute | solution.py:252
  12.4 0.0 collective-permute-done.1.near.refs_4_
  12.4 0.3 shard_map.52.refs_1_.refs_2_
  12.7 0.8 %collective-permute-start.3 = (f32[96,256]{1,0:T(8,128)S(1)}, f32[96,256]{1,0:T(8,128)S(1)}, u32[]{:S(2)}, u32[]{:S(2)}) collective-permute-start(f32[96,256]{1,0:T(8,128)S(1)} %shard_map.52.refs_1_.refs_2_), channel_id=1, source_target_pairs={{0,8},{4,12},{8,0},{12,4},{16,24},{20,28},{24,16},{28,20},{1,9},{5... | collective-permute-start | bytes 294920 | tf_op jit(solution)/shard_map/ppermute | solution.py:252
  13.5 0.0 copy-done.3
  13.5 0.1 copy.5.refs_0_
  13.6 2.9 %collective-permute-done.2.refs_2_.refs_5_ = f32[160,256]{1,0:T(8,128)S(1)} collective-permute-done((f32[160,256]{1,0:T(8,128)S(1)}, f32[160,256]{1,0:T(8,128)S(1)}, u32[]{:S(2)}, u32[]{:S(2)}) %collective-permute-start.2) | collective-permute-done | bytes 163872 | tf_op jit(solution)/shard_map/ppermute | solution.py:252
  16.4 0.3 shard_map.53.refs_0_
  16.7 0.8 %collective-permute-done.3.refs_3_.refs_6_ = f32[96,256]{1,0:T(8,128)S(1)} collective-permute-done((f32[96,256]{1,0:T(8,128)S(1)}, f32[96,256]{1,0:T(8,128)S(1)}, u32[]{:S(2)}, u32[]{:S(2)}) %collective-permute-start.3) | collective-permute-done | bytes 98336 | tf_op jit(solution)/shard_map/ppermute | solution.py:252
  17.5 0.4 %shard_map.54 = (f32[256,256]{1,0:T(8,128)S(1)}, f32[64,256]{1,0:T(8,128)S(1)}, f32[128,256]{1,0:T(8,128)S(1)}) custom-call(f32[256,256]{1,0:T(8,128)S(1)} %shard_map.53.refs_0_, f32[160,256]{1,0:T(8,128)S(1)} %shard_map.51.refs_0_.refs_1_, f32[96,256]{1,0:T(8,128)S(1)} %shard_map.52.refs_1_.refs_2_, f32[96,256]{1,0:T(8,128)S(1)} %collective-permute-done.3.refs_3_.refs_6_), custom_call_target="tpu_custom_call" | custom-call | flops 100663296 | bytes 1048576 | tf_op jit(solution)/shard_map/pallas_call | solution.py:228
  17.9 2.5 %collective-permute-start.4 = (f32[64,256]{1,0:T(8,128)S(1)}, f32[64,256]{1,0:T(8,128)S(1)}, u32[]{:S(2)}, u32[]{:S(2)}) collective-permute-start(f32[64,256]{1,0:T(8,128)S(1)} %get-tuple-element.19), channel_id=1, source_target_pairs={{0,16},{4,20},{8,24},{12,28},{16,0},{20,4},{24,8},{28,12},{1,17},{... | collective-permute-start | bytes 196616 | tf_op jit(solution)/shard_map/ppermute | solution.py:252
  20.3 0.5 %collective-permute-start.6 = (f32[128,256]{1,0:T(8,128)S(1)}, f32[128,256]{1,0:T(8,128)S(1)}, u32[]{:S(2)}, u32[]{:S(2)}) collective-permute-start(f32[128,256]{1,0:T(8,128)S(1)} %get-tuple-element.23), channel_id=1, source_target_pairs={{0,16},{4,20},{8,24},{12,28},{16,0},{20,4},{24,8},{28,12},{1,17},{... | collective-permute-start | bytes 393224 | tf_op jit(solution)/shard_map/ppermute | solution.py:252
  20.9 0.0 copy-done.1
  20.9 0.0 copy-start.2
  20.9 1.9 %shard_map.55 = (f32[2,256,256]{2,1,0:T(8,128)S(1)}, f32[256,256]{1,0:T(8,128)S(1)}, bf16[2,2,256,256]{3,2,1,0:T(8,128)(2,1)S(1)}, bf16[2,2,256,256]{3,2,1,0:T(8,128)(2,1)S(1)}) custom-call(s32[2,1]{1,0:T(2,128)S(1)} %copy.5.refs_0_, f32[2,1,256,256]{3,2,1,0:T(8,128)S(1)} %copy-done.1, f32[256,256]{1,0:T(8,128)S(1)} %get-tuple-element.20.refs_2_, ...), custom_call_target="tpu_custom_call" | custom-call | flops 905969664 | bytes 1048576 | tf_op jit(solution)/shard_map/pallas_call | solution.py:228
  22.8 2.3 %collective-permute-done.4.share = f32[64,256]{1,0:T(8,128)S(1)} collective-permute-done((f32[64,256]{1,0:T(8,128)S(1)}, f32[64,256]{1,0:T(8,128)S(1)}, u32[]{:S(2)}, u32[]{:S(2)}) %collective-permute-start.4) | collective-permute-done | bytes 65568 | tf_op jit(solution)/shard_map/ppermute | solution.py:252
  25.1 1.8 %collective-permute-start.5 = (f32[64,256]{1,0:T(8,128)S(1)}, f32[64,256]{1,0:T(8,128)S(1)}, u32[]{:S(2)}, u32[]{:S(2)}) collective-permute-start(f32[64,256]{1,0:T(8,128)S(1)} %collective-permute-done.4.share), channel_id=1, source_target_pairs={{0,4},{4,0},{8,12},{12,8},{16,20},{20,16},{24,28},{28,24},{1,5},{5... | collective-permute-start | bytes 196616 | tf_op jit(solution)/shard_map/ppermute | solution.py:252
  26.9 0.0 copy-done.2
  26.9 1.6 %shard_map.56.terms = f32[2,3,256,256]{3,2,1,0:T(8,128)S(1)} custom-call(bf16[2,2,256,256]{3,2,1,0:T(8,128)(2,1)S(1)} %get-tuple-element.24.a, bf16[2,2,256,256]{3,2,1,0:T(8,128)(2,1)S(1)} %get-tuple-element.25.b, f32[2,3,1,256,256]{4,3,2,1,0:T(8,128)S(1)} %copy-done.2), custom_call_target="tpu_custom_call" | custom-call | flops 1207959552 | bytes 1048576 | tf_op jit(solution)/shard_map/pallas_call | solution.py:228
  28.5 0.8 %collective-permute-done.5.swapped = f32[64,256]{1,0:T(8,128)S(1)} collective-permute-done((f32[64,256]{1,0:T(8,128)S(1)}, f32[64,256]{1,0:T(8,128)S(1)}, u32[]{:S(2)}, u32[]{:S(2)}) %collective-permute-start.5) | collective-permute-done | bytes 65568 | tf_op jit(solution)/shard_map/ppermute | solution.py:252
  29.3 0.0 collective-permute-done.6.rest
  29.3 0.4 %shard_map.57 = (f32[8,128]{1,0:T(8,128)S(1)}, f32[256,256]{1,0:T(8,128)S(1)}) custom-call(f32[64,256]{1,0:T(8,128)S(1)} %collective-permute-done.4.share, f32[64,256]{1,0:T(8,128)S(1)} %collective-permute-done.5.swapped, f32[128,256]{1,0:T(8,128)S(1)} %collective-permute-done.6.rest, f32[2,3,256,256]{3,2,1,0:T(8,128)S(1)} %shard_map.56.terms, ...), custom_call_target="tpu_custom_call" | custom-call | flops 201326592 | bytes 1048576 | tf_op jit(solution)/shard_map/pallas_call | solution.py:228
  29.7 0.1 collective-permute-start.7
  29.8 1.6 %collective-permute-start.8 = (f32[8,128]{1,0:T(8,128)S(1)}, f32[8,128]{1,0:T(8,128)S(1)}, u32[]{:S(2)}, u32[]{:S(2)}) collective-permute-start(f32[8,128]{1,0:T(8,128)S(1)} %get-tuple-element.29.refs_0_), channel_id=1, source_target_pairs={{0,2},{1,3},{2,0},{3,1},{4,6},{5,7},{6,4},{7,5},{8,10},{9,11},{10,... | collective-permute-start | bytes 12296 | tf_op jit(solution)/shard_map/ppermute | solution.py:301
  31.4 0.3 collective-permute-start.9
  31.7 0.8 %shard_map.58 = f32[2,1,256,256]{3,2,1,0:T(8,128)} custom-call(f32[256,256]{1,0:T(8,128)S(1)} %get-tuple-element.27.refs_0_, f32[2,256,256]{2,1,0:T(8,128)S(1)} %get-tuple-element.28.refs_1_), custom_call_target="tpu_custom_call" | custom-call | flops 201326592 | bytes 1048576 | tf_op jit(solution)/shard_map/pallas_call | solution.py:228
  32.5 0.0 collective-permute-done.7.refs_1_
  32.5 1.0 %collective-permute-done.8.refs_2_ = f32[8,128]{1,0:T(8,128)S(1)} collective-permute-done((f32[8,128]{1,0:T(8,128)S(1)}, f32[8,128]{1,0:T(8,128)S(1)}, u32[]{:S(2)}, u32[]{:S(2)}) %collective-permute-start.8) | collective-permute-done | bytes 4128 | tf_op jit(solution)/shard_map/ppermute | solution.py:301
  33.5 0.9 %collective-permute-done.9.refs_3_ = f32[8,128]{1,0:T(8,128)S(1)} collective-permute-done((f32[8,128]{1,0:T(8,128)S(1)}, f32[8,128]{1,0:T(8,128)S(1)}, u32[]{:S(2)}, u32[]{:S(2)}) %collective-permute-start.9) | collective-permute-done | bytes 4128 | tf_op jit(solution)/shard_map/ppermute | solution.py:301
  34.4 0.7 %shard_map.59 = f32[2,3]{1,0:T(2,128)} custom-call(f32[8,128]{1,0:T(8,128)S(1)} %get-tuple-element.29.refs_0_, f32[8,128]{1,0:T(8,128)S(1)} %collective-permute-done.7.refs_1_, f32[8,128]{1,0:T(8,128)S(1)} %collective-permute-done.8.refs_2_, f32[8,128]{1,0:T(8,128)S(1)} %collective-permute-done.9.refs_3_), custom_call_target="tpu_custom_call" | custom-call | flops 1000 | bytes 1048576 | tf_op jit(solution)/shard_map/pallas_call | solution.py:228
Async XLA Ops:
  0.6 1.0 %copy-start = (f32[2,1,256,256]{3,2,1,0:T(8,128)S(1)}, f32[2,1,256,256]{3,2,1,0:T(8,128)}, u32[]{:S(2)}) copy-start(f32[2,1,256,256]{3,2,1,0:T(8,128)} %refs_1_.1) | copy-start | bytes 1572868
  1.7 11.8 %copy-start.3 = (s32[2,1]{0,1:T(1,128)S(1)}, s32[2,1]{0,1:T(1,128)}, u32[]{:S(2)}) copy-start(s32[2,1]{0,1:T(1,128)} %param.5) | copy-start | bytes 28
  1.7 19.2 %copy-start.1 = (f32[2,1,256,256]{3,2,1,0:T(8,128)S(1)}, f32[2,1,256,256]{3,2,1,0:T(8,128)}, u32[]{:S(2)}) copy-start(f32[2,1,256,256]{3,2,1,0:T(8,128)} %refs_1_.1) | copy-start | bytes 1572868
  2.0 8.1 %collective-permute-start = (f32[160,256]{1,0:T(8,128)S(1)}, f32[160,256]{1,0:T(8,128)S(1)}, u32[]{:S(2)}, u32[]{:S(2)}) collective-permute-start(f32[160,256]{1,0:T(8,128)S(1)} %get-tuple-element.16), channel_id=1, source_target_pairs={{0,4},{4,0},{8,12},{12,8},{16,20},{20,16},{24,28},{28,24},{1,5},{5... | collective-permute-start | bytes 491528 | tf_op jit(solution)/shard_map/ppermute | solution.py:252
  5.1 7.3 %collective-permute-start.1 = (f32[96,256]{1,0:T(8,128)S(1)}, f32[96,256]{1,0:T(8,128)S(1)}, u32[]{:S(2)}, u32[]{:S(2)}) collective-permute-start(f32[96,256]{1,0:T(8,128)S(1)} %get-tuple-element.18), channel_id=1, source_target_pairs={{0,4},{4,0},{8,12},{12,8},{16,20},{20,16},{24,28},{28,24},{1,5},{5... | collective-permute-start | bytes 294920 | tf_op jit(solution)/shard_map/ppermute | solution.py:252
  10.4 6.0 %collective-permute-start.2 = (f32[160,256]{1,0:T(8,128)S(1)}, f32[160,256]{1,0:T(8,128)S(1)}, u32[]{:S(2)}, u32[]{:S(2)}) collective-permute-start(f32[160,256]{1,0:T(8,128)S(1)} %shard_map.51.refs_0_.refs_1_), channel_id=1, source_target_pairs={{0,8},{4,12},{8,0},{12,4},{16,24},{20,28},{24,16},{28,20},{1,9},{5... | collective-permute-start | bytes 491528 | tf_op jit(solution)/shard_map/ppermute | solution.py:252
  12.7 4.8 %collective-permute-start.3 = (f32[96,256]{1,0:T(8,128)S(1)}, f32[96,256]{1,0:T(8,128)S(1)}, u32[]{:S(2)}, u32[]{:S(2)}) collective-permute-start(f32[96,256]{1,0:T(8,128)S(1)} %shard_map.52.refs_1_.refs_2_), channel_id=1, source_target_pairs={{0,8},{4,12},{8,0},{12,4},{16,24},{20,28},{24,16},{28,20},{1,9},{5... | collective-permute-start | bytes 294920 | tf_op jit(solution)/shard_map/ppermute | solution.py:252
  17.9 7.2 %collective-permute-start.4 = (f32[64,256]{1,0:T(8,128)S(1)}, f32[64,256]{1,0:T(8,128)S(1)}, u32[]{:S(2)}, u32[]{:S(2)}) collective-permute-start(f32[64,256]{1,0:T(8,128)S(1)} %get-tuple-element.19), channel_id=1, source_target_pairs={{0,16},{4,20},{8,24},{12,28},{16,0},{20,4},{24,8},{28,12},{1,17},{... | collective-permute-start | bytes 196616 | tf_op jit(solution)/shard_map/ppermute | solution.py:252
  20.3 9.0 %collective-permute-start.6 = (f32[128,256]{1,0:T(8,128)S(1)}, f32[128,256]{1,0:T(8,128)S(1)}, u32[]{:S(2)}, u32[]{:S(2)}) collective-permute-start(f32[128,256]{1,0:T(8,128)S(1)} %get-tuple-element.23), channel_id=1, source_target_pairs={{0,16},{4,20},{8,24},{12,28},{16,0},{20,4},{24,8},{28,12},{1,17},{... | collective-permute-start | bytes 393224 | tf_op jit(solution)/shard_map/ppermute | solution.py:252
  20.9 6.0 %copy-start.2 = (f32[2,3,1,256,256]{4,3,2,1,0:T(8,128)S(1)}, f32[2,3,1,256,256]{4,3,2,1,0:T(8,128)}, u32[]{:S(2)}) copy-start(f32[2,3,1,256,256]{4,3,2,1,0:T(8,128)} %hamiltonian.1) | copy-start | bytes 4718596
  25.1 4.3 %collective-permute-start.5 = (f32[64,256]{1,0:T(8,128)S(1)}, f32[64,256]{1,0:T(8,128)S(1)}, u32[]{:S(2)}, u32[]{:S(2)}) collective-permute-start(f32[64,256]{1,0:T(8,128)S(1)} %collective-permute-done.4.share), channel_id=1, source_target_pairs={{0,4},{4,0},{8,12},{12,8},{16,20},{20,16},{24,28},{28,24},{1,5},{5... | collective-permute-start | bytes 196616 | tf_op jit(solution)/shard_map/ppermute | solution.py:252
  29.7 2.8 %collective-permute-start.7 = (f32[8,128]{1,0:T(8,128)S(1)}, f32[8,128]{1,0:T(8,128)S(1)}, u32[]{:S(2)}, u32[]{:S(2)}) collective-permute-start(f32[8,128]{1,0:T(8,128)S(1)} %get-tuple-element.29.refs_0_), channel_id=1, source_target_pairs={{0,1},{1,0},{2,3},{3,2},{4,5},{5,4},{6,7},{7,6},{8,9},{9,8},{10,11... | collective-permute-start | bytes 12296 | tf_op jit(solution)/shard_map/ppermute | solution.py:301
  29.8 3.7 %collective-permute-start.8 = (f32[8,128]{1,0:T(8,128)S(1)}, f32[8,128]{1,0:T(8,128)S(1)}, u32[]{:S(2)}, u32[]{:S(2)}) collective-permute-start(f32[8,128]{1,0:T(8,128)S(1)} %get-tuple-element.29.refs_0_), channel_id=1, source_target_pairs={{0,2},{1,3},{2,0},{3,1},{4,6},{5,7},{6,4},{7,5},{8,10},{9,11},{10,... | collective-permute-start | bytes 12296 | tf_op jit(solution)/shard_map/ppermute | solution.py:301
  31.4 3.0 %collective-permute-start.9 = (f32[8,128]{1,0:T(8,128)S(1)}, f32[8,128]{1,0:T(8,128)S(1)}, u32[]{:S(2)}, u32[]{:S(2)}) collective-permute-start(f32[8,128]{1,0:T(8,128)S(1)} %get-tuple-element.29.refs_0_), channel_id=1, source_target_pairs={{0,3},{1,2},{2,1},{3,0},{4,7},{5,6},{6,5},{7,4},{8,11},{9,10},{10,... | collective-permute-start | bytes 12296 | tf_op jit(solution)/shard_map/ppermute | solution.py:301

commit v4 on v3

--- a/solution.py
+++ b/solution.py
@@ -11,8 +11,8 @@
 SMEM = pl.BlockSpec(memory_space=pltpu.SMEM)
 LIMIT = 40 * 1024 * 1024
 LANES = 128
-FIRST = 10
-TN = ((0,), (0,))
+FIRST = (21, 11)
+SHARE = 10
 
 
 def split(a):
@@ -113,31 +113,60 @@
         sent[...] = value
 
     rows = share.shape[0]
-    share[...] = sent[pl.ds(pl.multiple_of(bit(1).astype(jnp.int32) * rows, rows), rows)]
+    share[...] = sent[pl.ds(pl.multiple_of(bit(1).astype(jnp.int32) * rows, 8), rows)]
     rest[...] = sent[2 * rows :]
 
 
-def quad_shares_kernel(n, k, begun, *refs):
+def quad_sent_kernel(n, k, begun, *refs):
     pairs, (far, sent, share, rest, room) = refs[:n], refs[n:]
     spread(end_quad(begun, pairs, far, room), bit(1) == bit(k), sent, share, rest)
 
 
-def shares_kernel(k, whole, sent, share, rest):
+def sent_kernel(k, whole, sent, share, rest):
     spread(whole[...], bit(k), sent, share, rest)
 
 
-def sides(nears, fars):
-    odd, high = bit(1), bit(2)
-    near, other = whole_of(nears), whole_of(fars)
-    near, other = jnp.where(odd, near, near.T), jnp.where(odd, other, other.T)
-    one = eye(near.shape[0])
-    left = product(jnp.where(high, other, one), jnp.where(odd, near, one))
-    right = product(jnp.where(odd, one, near), jnp.where(high, one, other))
-    return left, right
-
-
-def sides_kernel(n, *refs):
-    refs[2 * n][...], refs[2 * n + 1][...] = sides(refs[:n], refs[n : 2 * n])
+def near_kernel(n, transfer, *refs):
+    nears, (left, right) = refs[:n], refs[n:]
+    odd = bit(1)
+    near = whole_of(nears)
+
+    @pl.when(odd)
+    def _():
+        left[0] = near
+        left[1] = product(near, transfer[0, 0])
+        right[0] = transfer[1, 0]
+        right[1] = eye(near.shape[0])
+
+    @pl.when(jnp.logical_not(odd))
+    def _():
+        value = near.T
+        left[0] = eye(near.shape[0])
+        left[1] = transfer[0, 0]
+        right[0] = product(transfer[1, 0], value)
+        right[1] = value
+
+
+def sides(left, right, fars, lefts, rights):
+    high = bit(2)
+    other = whole_of(fars)
+    other = split(jnp.where(bit(1), other, other.T))
+
+    @pl.when(high)
+    def _():
+        rights[...] = right[...]
+        for c in range(lefts.shape[0]):
+            lefts[c] = multiply(other, split(left[c]))
+
+    @pl.when(jnp.logical_not(high))
+    def _():
+        lefts[...] = left[...]
+        for c in range(lefts.shape[0]):
+            rights[c] = multiply(split(right[c]), other)
+
+
+def sides_kernel(n, left, right, *refs):
+    sides(left, right, refs[:n], *refs[n:])
 
 
 def level_kernel(k, whole, left, right, x, whole_out, left_out, right_out):
@@ -145,32 +174,39 @@
     whole, left, right, x = whole[...], left[...], right[...], x[...]
     one = eye(whole.shape[0])
     whole_out[...] = product(jnp.where(after, x, whole), jnp.where(after, whole, x))
-    left_out[...] = product(jnp.where(after, x, one), left)
-    right_out[...] = product(right, jnp.where(after, one, x))
-
-
-def prepare(k, kept, transfer, left, right, sent, lefts_out, norm_out, a_out, b_out):
-    upper = bit(k)
-    width = left.shape[0]
-    lefts = [left, product(left, transfer[0, 0])]
-    rights = [product(transfer[1, 0], right), right]
-    y = split(sent[...])
-    norm_out[...] = multiply(y, y, TN)
-    column = lax.broadcasted_iota(jnp.int32, (width, width), 1)
-    for c in range(len(lefts)):
-        masked = jnp.where(column < kept[c, 0], lefts[c], 0.0)
-        lefts_out[c] = masked
-        a_out[c, 0], a_out[c, 1] = split(jnp.where(upper, masked, multiply(y, split(masked), TN)))
-        b_out[c, 0], b_out[c, 1] = split(jnp.where(upper, multiply(split(rights[c]), y), rights[c]))
-
-
-def prepare_quad_kernel(n, k, kept, transfer, sent, *refs):
-    left, right = sides(refs[:n], refs[n : 2 * n])
-    prepare(k, kept, transfer, left, right, sent, *refs[2 * n :])
-
-
-def prepare_kernel(k, kept, transfer, sent, left, right, *outs):
-    prepare(k, kept, transfer, left[...], right[...], sent, *outs)
+    for c in range(left.shape[0]):
+        left_out[c] = product(jnp.where(after, x, one), left[c])
+        right_out[c] = product(right[c], jnp.where(after, one, x))
+
+
+def prepare(k, kept, sent, lefts, rights, lefts_out, norm_out, a_out, b_out):
+    y, transposed = split(sent[...]), split(sent[...].T)
+    norm_out[...] = multiply(transposed, y)
+    column = lax.broadcasted_iota(jnp.int32, lefts.shape[1:], 1)
+    for c in range(lefts.shape[0]):
+        lefts_out[c] = jnp.where(column < kept[c : c + 1], lefts[c], 0.0)
+
+    @pl.when(bit(k))
+    def _():
+        for c in range(lefts.shape[0]):
+            a_out[c, 0], a_out[c, 1] = split(lefts_out[c])
+            b_out[c, 0], b_out[c, 1] = split(multiply(split(rights[c]), y))
+
+    @pl.when(jnp.logical_not(bit(k)))
+    def _():
+        for c in range(lefts.shape[0]):
+            a_out[c, 0], a_out[c, 1] = split(multiply(transposed, split(lefts_out[c])))
+            b_out[c, 0], b_out[c, 1] = split(rights[c])
+
+
+def prepare_quad_kernel(n, k, kept, sent, left, right, *refs):
+    fars, outs, (lefts, rights) = refs[:n], refs[n:-2], refs[-2:]
+    sides(left, right, fars, lefts, rights)
+    prepare(k, kept, sent, lefts, rights, *outs)
+
+
+def prepare_kernel(k, kept, sent, lefts, rights, *outs):
+    prepare(k, kept, sent, lefts, rights, *outs)
 
 
 def terms_kernel(a, b, hamiltonian, out):
@@ -180,14 +216,13 @@
             out[c, t] = multiply(split(inner), (b[c, 0], b[c, 1]))
 
 
-def finish_kernel(share, swapped, rest, terms, norm, out, x):
+def finish_kernel(share, passed, rest, terms, norm, out, x):
     rows = share.shape[0]
     at = bit(1).astype(jnp.int32) * rows
-    x[pl.ds(pl.multiple_of(at, rows), rows)] = share[...]
-    x[pl.ds(pl.multiple_of(rows - at, rows), rows)] = swapped[...]
+    x[pl.ds(pl.multiple_of(at, 8), rows)] = share[...]
+    x[pl.ds(pl.multiple_of(rows - at, 8), rows)] = passed[...]
     x[2 * rows :] = rest[...]
-    xs = split(x[...])
-    z = multiply(xs, xs, TN)
+    z = product(x[...].T, x[...])
     columns, count = terms.shape[0], terms.shape[1]
 
     def total(m):
@@ -212,7 +247,7 @@
 
 
 def energy_kernel(scale, *refs):
-    parts, out = [r[...] for r in refs[:-1]], refs[-1]
+    parts, out = [refs[0][...]] + [r[...] for r in refs[-2:0:-1]], refs[-1]
     while len(parts) > 1:
         parts = [a + b for a, b in zip(parts[::2], parts[1::2])]
     columns, terms = out.shape
@@ -251,8 +286,7 @@
     def swap(a, k):
         return lax.ppermute(a, "col", [(i, i ^ k) for i in range(total)])
 
-    first = width * FIRST // 16
-    heights = (first, width - first)
+    heights = [8 * h for h in FIRST]
     n = len(heights)
     own, *parts = call(group_kernel, (matrix,) + tuple(array(h, width) for h in heights), one, transfer)
     nears = [swap(part, 1) for part in parts]
@@ -260,45 +294,48 @@
     for near, h in zip(nears, heights):
         pairs.append(call(pair_kernel, array(h, width), one // n, near, own))
         fars.append(swap(pairs[-1], 2))
+    both = array(columns, width, width)
+    left, right = call(lambda *refs: near_kernel(n, *refs), (both, both), 2 * one, transfer, *nears)
+    fars[0], left = lax.optimization_barrier((fars[0], left))
     begun = call(lambda *refs: begin_kernel(n, *refs), matrix, one, *pairs, *fars[:-1])
-    rows = width // 4
+    rows = 8 * SHARE
     shared = (matrix, array(rows, width), array(width - 2 * rows, width))
     if total <= 8:
         sent, share, rest = call(
-            lambda *refs: quad_shares_kernel(n, half, *refs), shared, one, begun, *pairs, fars[-1], scratch=room
+            lambda *refs: quad_sent_kernel(n, half, *refs), shared, one, begun, *pairs, fars[-1], scratch=room
         )
     else:
         whole = call(lambda *refs: quad_kernel(n, *refs), matrix, one, begun, *pairs, fars[-1], scratch=room)
-        left, right = call(lambda *refs: sides_kernel(n, *refs), (matrix, matrix), 2 * one, *nears, *fars)
+        left, right = call(lambda *refs: sides_kernel(n, *refs), (both, both), 2 * one, left, right, *fars)
         k = 4
         while k < half:
             x = swap(whole, k)
             whole, left, right = call(
-                lambda *refs, k=k: level_kernel(k, *refs), (matrix,) * 3, 3 * one, whole, left, right, x
+                lambda *refs, k=k: level_kernel(k, *refs), (matrix, both, both), 5 * one, whole, left, right, x
             )
             k *= 2
-        sent, share, rest = call(lambda *refs: shares_kernel(half, *refs), shared, one, whole)
+        sent, share, rest = call(lambda *refs: sent_kernel(half, *refs), shared, one, whole)
     share = swap(share, half)
     rest = swap(rest, half)
     halves = array(columns, 2, width, width, dtype=BF16)
     prepared = (array(columns, width, width), matrix, halves, halves)
     if total <= 8:
         lefts, norm, a, b = call(
-            lambda *refs: prepare_quad_kernel(n, half, *refs), prepared, 9 * one, kept, transfer, sent, *nears, *fars,
-            smem=1,
+            lambda *refs: prepare_quad_kernel(n, half, *refs), prepared, 5 * one, kept, sent, left, right, *fars,
+            scratch=(pltpu.VMEM((columns, width, width), F32),) * 2,
         )
     else:
         lefts, norm, a, b = call(
-            lambda *refs: prepare_kernel(half, *refs), prepared, 9 * one, kept, transfer, sent, left, right, smem=1
+            lambda *refs: prepare_kernel(half, *refs), prepared, 3 * one, kept, sent, left, right
         )
     share, norm = lax.optimization_barrier((share, norm))
-    swapped = swap(share, 1)
+    passed = swap(share, 1)
     products = call(terms_kernel, array(columns, terms, width, width), 12 * one, a, b, hamiltonian)
     table_rows = -(-(columns * terms + 1) // 8) * 8
     table, x = call(
-        finish_kernel, (array(table_rows, LANES), matrix), 2 * one, share, swapped, rest, products, norm
+        finish_kernel, (array(table_rows, LANES), matrix), 2 * one, share, passed, rest, products, norm
     )
-    parts = [table] + [lax.ppermute(table, "sec", [(i, i ^ k) for i in range(sectors)]) for k in range(1, sectors)]
+    parts = [table] + [lax.ppermute(table, "sec", [(i, i ^ k) for i in range(sectors)]) for k in range(sectors - 1, 0, -1)]
     left_env = call(
         lambda *refs: left_kernel(half, *refs), array(columns, 1, width, width), 2 * one, x, lefts
     )

time: 35.2 us -> 34.1 us (0.969)
  starting transfers between devices: 12.7 us -> 12.1 us
  waiting for transfers between devices: 13.6 us -> 13.1 us
    ppermute x3, waiting for transfers between devices: 1.9 us -> 1 us  [per_device(): lax.ppermute(table, 'sec', [(i, i ^ k) for i in range(sectors)])]
    ppermute x7, starting transfers between devices: 10.7 us -> 10.2 us  [swap(): return lax.ppermute(a, 'col', [(i, i ^ k) for i in range(total)])]
    ppermute x7, waiting for transfers between devices: 11.7 us -> 12.1 us  [swap(): return lax.ppermute(a, 'col', [(i, i ^ k) for i in range(total)])]
    pallas_call x10 -> x11, Pallas kernels: 6.92 us -> 6.81 us  [call(): pl.pallas_call(kernel, out_shape=outs, in_specs=[SMEM] * smem + [VMEM] *...]
where the time goes in v4:
time: 34.1 us; the launch traced here: 33.9 us
  waiting for transfers between devices  13.1 us (38%)
  starting transfers between devices  12.1 us (35%)
  Pallas kernels  6.81 us (20%)
  local copies, waits for them, and re-layouts  1.14 us (3%)
  between operations  0.74 us (2%)
    ppermute x7, waiting for transfers between devices, swap(): return lax.ppermute(a, 'col', [(i, i ^ k) for i in range(total)])  12.1 us
    ppermute x7, starting transfers between devices, swap(): return lax.ppermute(a, 'col', [(i, i ^ k) for i in range(total)])  10.2 us
    pallas_call x11, Pallas kernels, call(): pl.pallas_call(kernel, out_shape=outs, in_specs=[SMEM] * smem + [VMEM] *...  6.81 us
    ppermute x3, starting transfers between devices, per_device(): lax.ppermute(table, 'sec', [(i, i ^ k) for i in range(sectors)])  1.92 us
    unnamed x9, local copies, waits for them, and re-layouts  1.14 us
    ppermute x3, waiting for transfers between devices, per_device(): lax.ppermute(table, 'sec', [(i, i ^ k) for i in range(sectors)])  1 us
  transfers between devices with their start and end apart: 10, of which 7 were waited for; matrix products, arithmetic and copies ran while one was open for 0% of the time, Pallas kernels for 15%

profile of v4, /device:TPU:0, one launch (start us, length us, event | category | flops | bytes accessed | tf_op | source)
XLA Modules:
  0.0 33.9 jit_solution(9981280010379956737)
XLA Ops:
  0.6 0.0 copy-start
  0.6 1.0 %copy-done = f32[2,1,256,256]{3,2,1,0:T(8,128)S(1)} copy-done((f32[2,1,256,256]{3,2,1,0:T(8,128)S(1)}, f32[2,1,256,256]{3,2,1,0:T(8,128)}, u32[]{:S(2)}) %copy-start) | copy-done | bytes 524312
  1.7 0.0 copy-start.1
  1.7 0.3 shard_map.50
  2.0 3.1 %collective-permute-start = (f32[168,256]{1,0:T(8,128)S(1)}, f32[168,256]{1,0:T(8,128)S(1)}, u32[]{:S(2)}, u32[]{:S(2)}) collective-permute-start(f32[168,256]{1,0:T(8,128)S(1)} %get-tuple-element.20), channel_id=1, source_target_pairs={{0,4},{4,0},{8,12},{12,8},{16,20},{20,16},{24,28},{28,24},{1,5},{5... | collective-permute-start | bytes 516104 | tf_op jit(solution)/shard_map/ppermute | solution.py:287
  5.1 0.1 collective-permute-start.1
  5.2 5.1 %collective-permute-done.near.refs_1_ = f32[168,256]{1,0:T(8,128)S(1)} collective-permute-done((f32[168,256]{1,0:T(8,128)S(1)}, f32[168,256]{1,0:T(8,128)S(1)}, u32[]{:S(2)}, u32[]{:S(2)}) %collective-permute-start) | collective-permute-done | bytes 172064 | tf_op jit(solution)/shard_map/ppermute | solution.py:287
  10.3 0.0 copy-start.3
  10.3 0.3 shard_map.51.refs_0_.refs_1_
  10.6 1.9 %collective-permute-start.2 = (f32[168,256]{1,0:T(8,128)S(1)}, f32[168,256]{1,0:T(8,128)S(1)}, u32[]{:S(2)}, u32[]{:S(2)}) collective-permute-start(f32[168,256]{1,0:T(8,128)S(1)} %shard_map.51.refs_0_.refs_1_), channel_id=1, source_target_pairs={{0,8},{4,12},{8,0},{12,4},{16,24},{20,28},{24,16},{28,20},{1,9},{5... | collective-permute-start | bytes 516104 | tf_op jit(solution)/shard_map/ppermute | solution.py:287
  12.5 0.0 collective-permute-done.1.near.refs_2_
  12.5 0.3 shard_map.52.refs_1_.refs_2_
  12.8 0.6 %collective-permute-start.3 = (f32[88,256]{1,0:T(8,128)S(1)}, f32[88,256]{1,0:T(8,128)S(1)}, u32[]{:S(2)}, u32[]{:S(2)}) collective-permute-start(f32[88,256]{1,0:T(8,128)S(1)} %shard_map.52.refs_1_.refs_2_), channel_id=1, source_target_pairs={{0,8},{4,12},{8,0},{12,4},{16,24},{20,28},{24,16},{28,20},{1,9},{5... | collective-permute-start | bytes 270344 | tf_op jit(solution)/shard_map/ppermute | solution.py:287
  13.5 0.0 copy-done.1
  13.5 0.4 %shard_map.53 = (f32[2,256,256]{2,1,0:T(8,128)S(1)}, f32[2,256,256]{2,1,0:T(8,128)S(1)}) custom-call(f32[2,1,256,256]{3,2,1,0:T(8,128)S(1)} %copy-done.1, f32[168,256]{1,0:T(8,128)S(1)} %collective-permute-done.near.refs_1_, f32[88,256]{1,0:T(8,128)S(1)} %collective-permute-done.1.near.refs_2_), custom_call_target="tpu_custom_call" | custom-call | flops 201326592 | bytes 1048576 | tf_op jit(solution)/shard_map/pallas_call | solution.py:263
  13.9 2.5 %collective-permute-done.2.refs_2_.refs_4_ = f32[168,256]{1,0:T(8,128)S(1)} collective-permute-done((f32[168,256]{1,0:T(8,128)S(1)}, f32[168,256]{1,0:T(8,128)S(1)}, u32[]{:S(2)}, u32[]{:S(2)}) %collective-permute-start.2) | collective-permute-done | bytes 172064 | tf_op jit(solution)/shard_map/ppermute | solution.py:287
  16.4 0.0 copy-start.2
  16.4 0.3 shard_map.54.refs_0_
  16.7 0.7 %collective-permute-done.3.refs_3_.refs_5_ = f32[88,256]{1,0:T(8,128)S(1)} collective-permute-done((f32[88,256]{1,0:T(8,128)S(1)}, f32[88,256]{1,0:T(8,128)S(1)}, u32[]{:S(2)}, u32[]{:S(2)}) %collective-permute-start.3) | collective-permute-done | bytes 90144 | tf_op jit(solution)/shard_map/ppermute | solution.py:287
  17.4 0.4 %shard_map.55 = (f32[256,256]{1,0:T(8,128)S(1)}, f32[80,256]{1,0:T(8,128)S(1)}, f32[96,256]{1,0:T(8,128)S(1)}) custom-call(f32[256,256]{1,0:T(8,128)S(1)} %shard_map.54.refs_0_, f32[168,256]{1,0:T(8,128)S(1)} %shard_map.51.refs_0_.refs_1_, f32[88,256]{1,0:T(8,128)S(1)} %shard_map.52.refs_1_.refs_2_, f32[88,256]{1,0:T(8,128)S(1)} %collective-permute-done.3.refs_3_.refs_5_), custom_call_target="tpu_custom_call" | custom-call | flops 100663296 | bytes 1048576 | tf_op jit(solution)/shard_map/pallas_call | solution.py:263
  17.8 2.7 %collective-permute-start.4 = (f32[80,256]{1,0:T(8,128)S(1)}, f32[80,256]{1,0:T(8,128)S(1)}, u32[]{:S(2)}, u32[]{:S(2)}) collective-permute-start(f32[80,256]{1,0:T(8,128)S(1)} %get-tuple-element.25), channel_id=1, source_target_pairs={{0,16},{4,20},{8,24},{12,28},{16,0},{20,4},{24,8},{28,12},{1,17},{... | collective-permute-start | bytes 245768 | tf_op jit(solution)/shard_map/ppermute | solution.py:287
  20.5 0.0 copy-done.3
  20.5 0.1 copy.5.refs_0_
  20.6 0.3 collective-permute-start.6
  20.9 1.3 %shard_map.56 = (f32[2,256,256]{2,1,0:T(8,128)S(1)}, f32[256,256]{1,0:T(8,128)S(1)}, bf16[2,2,256,256]{3,2,1,0:T(8,128)(2,1)S(1)}, bf16[2,2,256,256]{3,2,1,0:T(8,128)(2,1)S(1)}) custom-call(s32[2,1]{1,0:T(2,128)S(1)} %copy.5.refs_0_, f32[256,256]{1,0:T(8,128)S(1)} %get-tuple-element.26.refs_1_, f32[2,256,256]{2,1,0:T(8,128)S(1)} %get-tuple-element.27.refs_2_, ...), custom_call_target="tpu_custom_call" | custom-call | flops 503316480 | bytes 1048576 | tf_op jit(solution)/shard_map/pallas_call | solution.py:263
  22.2 2.4 %collective-permute-done.4.share = f32[80,256]{1,0:T(8,128)S(1)} collective-permute-done((f32[80,256]{1,0:T(8,128)S(1)}, f32[80,256]{1,0:T(8,128)S(1)}, u32[]{:S(2)}, u32[]{:S(2)}) %collective-permute-start.4) | collective-permute-done | bytes 81952 | tf_op jit(solution)/shard_map/ppermute | solution.py:287
  24.7 1.5 %collective-permute-start.5 = (f32[80,256]{1,0:T(8,128)S(1)}, f32[80,256]{1,0:T(8,128)S(1)}, u32[]{:S(2)}, u32[]{:S(2)}) collective-permute-start(f32[80,256]{1,0:T(8,128)S(1)} %collective-permute-done.4.share), channel_id=1, source_target_pairs={{0,4},{4,0},{8,12},{12,8},{16,20},{20,16},{24,28},{28,24},{1,5},{5... | collective-permute-start | bytes 245768 | tf_op jit(solution)/shard_map/ppermute | solution.py:287
  26.1 0.0 copy-done.2
  26.1 1.6 %shard_map.57.terms = f32[2,3,256,256]{3,2,1,0:T(8,128)S(1)} custom-call(bf16[2,2,256,256]{3,2,1,0:T(8,128)(2,1)S(1)} %get-tuple-element.32.a, bf16[2,2,256,256]{3,2,1,0:T(8,128)(2,1)S(1)} %get-tuple-element.33.b, f32[2,3,1,256,256]{4,3,2,1,0:T(8,128)S(1)} %copy-done.2), custom_call_target="tpu_custom_call" | custom-call | flops 1207959552 | bytes 1048576 | tf_op jit(solution)/shard_map/pallas_call | solution.py:263
  27.8 0.0 collective-permute-done.6.rest
  27.8 1.3 %collective-permute-done.5.passed = f32[80,256]{1,0:T(8,128)S(1)} collective-permute-done((f32[80,256]{1,0:T(8,128)S(1)}, f32[80,256]{1,0:T(8,128)S(1)}, u32[]{:S(2)}, u32[]{:S(2)}) %collective-permute-start.5) | collective-permute-done | bytes 81952 | tf_op jit(solution)/shard_map/ppermute | solution.py:287
  29.1 0.4 %shard_map.58 = (f32[8,128]{1,0:T(8,128)S(1)}, f32[256,256]{1,0:T(8,128)S(1)}) custom-call(f32[80,256]{1,0:T(8,128)S(1)} %collective-permute-done.4.share, f32[80,256]{1,0:T(8,128)S(1)} %collective-permute-done.5.passed, f32[96,256]{1,0:T(8,128)S(1)} %collective-permute-done.6.rest, f32[2,3,256,256]{3,2,1,0:T(8,128)S(1)} %shard_map.57.terms, ...), custom_call_target="tpu_custom_call" | custom-call | flops 201326592 | bytes 1048576 | tf_op jit(solution)/shard_map/pallas_call | solution.py:263
  29.5 0.1 collective-permute-start.7
  29.6 1.3 %collective-permute-start.8 = (f32[8,128]{1,0:T(8,128)S(1)}, f32[8,128]{1,0:T(8,128)S(1)}, u32[]{:S(2)}, u32[]{:S(2)}) collective-permute-start(f32[8,128]{1,0:T(8,128)S(1)} %get-tuple-element.37.refs_0_), channel_id=1, source_target_pairs={{0,2},{1,3},{2,0},{3,1},{4,6},{5,7},{6,4},{7,5},{8,10},{9,11},{10,... | collective-permute-start | bytes 12296 | tf_op jit(solution)/shard_map/ppermute | solution.py:338
  30.9 0.6 %collective-permute-start.9 = (f32[8,128]{1,0:T(8,128)S(1)}, f32[8,128]{1,0:T(8,128)S(1)}, u32[]{:S(2)}, u32[]{:S(2)}) collective-permute-start(f32[8,128]{1,0:T(8,128)S(1)} %get-tuple-element.37.refs_0_), channel_id=1, source_target_pairs={{0,1},{1,0},{2,3},{3,2},{4,5},{5,4},{6,7},{7,6},{8,9},{9,8},{10,11... | collective-permute-start | bytes 12296 | tf_op jit(solution)/shard_map/ppermute | solution.py:338
  31.5 0.8 %shard_map.59 = f32[2,1,256,256]{3,2,1,0:T(8,128)} custom-call(f32[256,256]{1,0:T(8,128)S(1)} %get-tuple-element.35.refs_0_, f32[2,256,256]{2,1,0:T(8,128)S(1)} %get-tuple-element.36.refs_1_), custom_call_target="tpu_custom_call" | custom-call | flops 201326592 | bytes 1048576 | tf_op jit(solution)/shard_map/pallas_call | solution.py:263
  32.3 0.3 %collective-permute-done.7.refs_1_ = f32[8,128]{1,0:T(8,128)S(1)} collective-permute-done((f32[8,128]{1,0:T(8,128)S(1)}, f32[8,128]{1,0:T(8,128)S(1)}, u32[]{:S(2)}, u32[]{:S(2)}) %collective-permute-start.7) | collective-permute-done | bytes 4128 | tf_op jit(solution)/shard_map/ppermute | solution.py:338
  32.6 0.7 %collective-permute-done.8.refs_2_ = f32[8,128]{1,0:T(8,128)S(1)} collective-permute-done((f32[8,128]{1,0:T(8,128)S(1)}, f32[8,128]{1,0:T(8,128)S(1)}, u32[]{:S(2)}, u32[]{:S(2)}) %collective-permute-start.8) | collective-permute-done | bytes 4128 | tf_op jit(solution)/shard_map/ppermute | solution.py:338
  33.3 0.0 collective-permute-done.9.refs_3_
  33.3 0.7 %shard_map.60 = f32[2,3]{1,0:T(2,128)} custom-call(f32[8,128]{1,0:T(8,128)S(1)} %get-tuple-element.37.refs_0_, f32[8,128]{1,0:T(8,128)S(1)} %collective-permute-done.7.refs_1_, f32[8,128]{1,0:T(8,128)S(1)} %collective-permute-done.8.refs_2_, f32[8,128]{1,0:T(8,128)S(1)} %collective-permute-done.9.refs_3_), custom_call_target="tpu_custom_call" | custom-call | flops 1000 | bytes 1048576 | tf_op jit(solution)/shard_map/pallas_call | solution.py:263
Async XLA Ops:
  0.6 1.0 %copy-start = (f32[2,1,256,256]{3,2,1,0:T(8,128)S(1)}, f32[2,1,256,256]{3,2,1,0:T(8,128)}, u32[]{:S(2)}) copy-start(f32[2,1,256,256]{3,2,1,0:T(8,128)} %refs_0_.2) | copy-start | bytes 1572868
  1.7 11.8 %copy-start.1 = (f32[2,1,256,256]{3,2,1,0:T(8,128)S(1)}, f32[2,1,256,256]{3,2,1,0:T(8,128)}, u32[]{:S(2)}) copy-start(f32[2,1,256,256]{3,2,1,0:T(8,128)} %refs_0_.2) | copy-start | bytes 1572868
  2.0 8.3 %collective-permute-start = (f32[168,256]{1,0:T(8,128)S(1)}, f32[168,256]{1,0:T(8,128)S(1)}, u32[]{:S(2)}, u32[]{:S(2)}) collective-permute-start(f32[168,256]{1,0:T(8,128)S(1)} %get-tuple-element.20), channel_id=1, source_target_pairs={{0,4},{4,0},{8,12},{12,8},{16,20},{20,16},{24,28},{28,24},{1,5},{5... | collective-permute-start | bytes 516104 | tf_op jit(solution)/shard_map/ppermute | solution.py:287
  5.1 7.4 %collective-permute-start.1 = (f32[88,256]{1,0:T(8,128)S(1)}, f32[88,256]{1,0:T(8,128)S(1)}, u32[]{:S(2)}, u32[]{:S(2)}) collective-permute-start(f32[88,256]{1,0:T(8,128)S(1)} %get-tuple-element.22), channel_id=1, source_target_pairs={{0,4},{4,0},{8,12},{12,8},{16,20},{20,16},{24,28},{28,24},{1,5},{5... | collective-permute-start | bytes 270344 | tf_op jit(solution)/shard_map/ppermute | solution.py:287
  10.3 10.2 %copy-start.3 = (s32[2,1]{0,1:T(1,128)S(1)}, s32[2,1]{0,1:T(1,128)}, u32[]{:S(2)}) copy-start(s32[2,1]{0,1:T(1,128)} %param.5) | copy-start | bytes 28
  10.6 5.8 %collective-permute-start.2 = (f32[168,256]{1,0:T(8,128)S(1)}, f32[168,256]{1,0:T(8,128)S(1)}, u32[]{:S(2)}, u32[]{:S(2)}) collective-permute-start(f32[168,256]{1,0:T(8,128)S(1)} %shard_map.51.refs_0_.refs_1_), channel_id=1, source_target_pairs={{0,8},{4,12},{8,0},{12,4},{16,24},{20,28},{24,16},{28,20},{1,9},{5... | collective-permute-start | bytes 516104 | tf_op jit(solution)/shard_map/ppermute | solution.py:287
  12.8 4.6 %collective-permute-start.3 = (f32[88,256]{1,0:T(8,128)S(1)}, f32[88,256]{1,0:T(8,128)S(1)}, u32[]{:S(2)}, u32[]{:S(2)}) collective-permute-start(f32[88,256]{1,0:T(8,128)S(1)} %shard_map.52.refs_1_.refs_2_), channel_id=1, source_target_pairs={{0,8},{4,12},{8,0},{12,4},{16,24},{20,28},{24,16},{28,20},{1,9},{5... | collective-permute-start | bytes 270344 | tf_op jit(solution)/shard_map/ppermute | solution.py:287
  16.4 9.7 %copy-start.2 = (f32[2,3,1,256,256]{4,3,2,1,0:T(8,128)S(1)}, f32[2,3,1,256,256]{4,3,2,1,0:T(8,128)}, u32[]{:S(2)}) copy-start(f32[2,3,1,256,256]{4,3,2,1,0:T(8,128)} %hamiltonian.1) | copy-start | bytes 4718596
  17.8 6.8 %collective-permute-start.4 = (f32[80,256]{1,0:T(8,128)S(1)}, f32[80,256]{1,0:T(8,128)S(1)}, u32[]{:S(2)}, u32[]{:S(2)}) collective-permute-start(f32[80,256]{1,0:T(8,128)S(1)} %get-tuple-element.25), channel_id=1, source_target_pairs={{0,16},{4,20},{8,24},{12,28},{16,0},{20,4},{24,8},{28,12},{1,17},{... | collective-permute-start | bytes 245768 | tf_op jit(solution)/shard_map/ppermute | solution.py:287
  20.6 7.2 %collective-permute-start.6 = (f32[96,256]{1,0:T(8,128)S(1)}, f32[96,256]{1,0:T(8,128)S(1)}, u32[]{:S(2)}, u32[]{:S(2)}) collective-permute-start(f32[96,256]{1,0:T(8,128)S(1)} %get-tuple-element.31), channel_id=1, source_target_pairs={{0,16},{4,20},{8,24},{12,28},{16,0},{20,4},{24,8},{28,12},{1,17},{... | collective-permute-start | bytes 294920 | tf_op jit(solution)/shard_map/ppermute | solution.py:287
  24.7 4.4 %collective-permute-start.5 = (f32[80,256]{1,0:T(8,128)S(1)}, f32[80,256]{1,0:T(8,128)S(1)}, u32[]{:S(2)}, u32[]{:S(2)}) collective-permute-start(f32[80,256]{1,0:T(8,128)S(1)} %collective-permute-done.4.share), channel_id=1, source_target_pairs={{0,4},{4,0},{8,12},{12,8},{16,20},{20,16},{24,28},{28,24},{1,5},{5... | collective-permute-start | bytes 245768 | tf_op jit(solution)/shard_map/ppermute | solution.py:287
  29.5 3.1 %collective-permute-start.7 = (f32[8,128]{1,0:T(8,128)S(1)}, f32[8,128]{1,0:T(8,128)S(1)}, u32[]{:S(2)}, u32[]{:S(2)}) collective-permute-start(f32[8,128]{1,0:T(8,128)S(1)} %get-tuple-element.37.refs_0_), channel_id=1, source_target_pairs={{0,3},{1,2},{2,1},{3,0},{4,7},{5,6},{6,5},{7,4},{8,11},{9,10},{10,... | collective-permute-start | bytes 12296 | tf_op jit(solution)/shard_map/ppermute | solution.py:338
  29.6 3.7 %collective-permute-start.8 = (f32[8,128]{1,0:T(8,128)S(1)}, f32[8,128]{1,0:T(8,128)S(1)}, u32[]{:S(2)}, u32[]{:S(2)}) collective-permute-start(f32[8,128]{1,0:T(8,128)S(1)} %get-tuple-element.37.refs_0_), channel_id=1, source_target_pairs={{0,2},{1,3},{2,0},{3,1},{4,6},{5,7},{6,4},{7,5},{8,10},{9,11},{10,... | collective-permute-start | bytes 12296 | tf_op jit(solution)/shard_map/ppermute | solution.py:338
  30.9 2.4 %collective-permute-start.9 = (f32[8,128]{1,0:T(8,128)S(1)}, f32[8,128]{1,0:T(8,128)S(1)}, u32[]{:S(2)}, u32[]{:S(2)}) collective-permute-start(f32[8,128]{1,0:T(8,128)S(1)} %get-tuple-element.37.refs_0_), channel_id=1, source_target_pairs={{0,1},{1,0},{2,3},{3,2},{4,5},{5,4},{6,7},{7,6},{8,9},{9,8},{10,11... | collective-permute-start | bytes 12296 | tf_op jit(solution)/shard_map/ppermute | solution.py:338

commit v5 on v4

--- a/solution.py
+++ b/solution.py
@@ -12,7 +12,7 @@
 LIMIT = 40 * 1024 * 1024
 LANES = 128
 FIRST = (21, 11)
-SHARE = 10
+SHARE = 8
 
 
 def split(a):
@@ -315,7 +315,7 @@
             )
             k *= 2
         sent, share, rest = call(lambda *refs: sent_kernel(half, *refs), shared, one, whole)
-    share = swap(share, half)
+    share = swap(share, half | 2)
     rest = swap(rest, half)
     halves = array(columns, 2, width, width, dtype=BF16)
     prepared = (array(columns, width, width), matrix, halves, halves)

time: 34.1 us -> 33.3 us (0.977)
  waiting for transfers between devices: 13.1 us -> 11.6 us
  starting transfers between devices: 12.1 us -> 12.8 us
    ppermute x7, waiting for transfers between devices: 12.1 us -> 10.6 us  [swap(): return lax.ppermute(a, 'col', [(i, i ^ k) for i in range(total)])]
    ppermute x7, starting transfers between devices: 10.2 us -> 10.9 us  [swap(): return lax.ppermute(a, 'col', [(i, i ^ k) for i in range(total)])]
where the time goes in v5:
time: 33.3 us; the launch traced here: 33.1 us
  starting transfers between devices  12.8 us (38%)
  waiting for transfers between devices  11.6 us (35%)
  Pallas kernels  6.82 us (20%)
  local copies, waits for them, and re-layouts  1.14 us (3%)
  between operations  0.73 us (2%)
    ppermute x7, starting transfers between devices, swap(): return lax.ppermute(a, 'col', [(i, i ^ k) for i in range(total)])  10.9 us
    ppermute x7, waiting for transfers between devices, swap(): return lax.ppermute(a, 'col', [(i, i ^ k) for i in range(total)])  10.6 us
    pallas_call x11, Pallas kernels, call(): pl.pallas_call(kernel, out_shape=outs, in_specs=[SMEM] * smem + [VMEM] *...  6.82 us
    ppermute x3, starting transfers between devices, per_device(): lax.ppermute(table, 'sec', [(i, i ^ k) for i in range(sectors)])  1.92 us
    unnamed x9, local copies, waits for them, and re-layouts  1.14 us
    ppermute x3, waiting for transfers between devices, per_device(): lax.ppermute(table, 'sec', [(i, i ^ k) for i in range(sectors)])  1 us
  transfers between devices with their start and end apart: 10, of which 7 were waited for; matrix products, arithmetic and copies ran while one was open for 0% of the time, Pallas kernels for 15%

profile of v5, /device:TPU:0, one launch (start us, length us, event | category | flops | bytes accessed | tf_op | source)
XLA Modules:
  0.0 33.1 jit_solution(18204733016898720907)
XLA Ops:
  0.6 0.0 copy-start
  0.6 1.0 %copy-done = f32[2,1,256,256]{3,2,1,0:T(8,128)S(1)} copy-done((f32[2,1,256,256]{3,2,1,0:T(8,128)S(1)}, f32[2,1,256,256]{3,2,1,0:T(8,128)}, u32[]{:S(2)}) %copy-start) | copy-done | bytes 524312
  1.7 0.0 copy-start.1
  1.7 0.3 shard_map.50
  2.0 3.1 %collective-permute-start = (f32[168,256]{1,0:T(8,128)S(1)}, f32[168,256]{1,0:T(8,128)S(1)}, u32[]{:S(2)}, u32[]{:S(2)}) collective-permute-start(f32[168,256]{1,0:T(8,128)S(1)} %get-tuple-element.20), channel_id=1, source_target_pairs={{0,4},{4,0},{8,12},{12,8},{16,20},{20,16},{24,28},{28,24},{1,5},{5... | collective-permute-start | bytes 516104 | tf_op jit(solution)/shard_map/ppermute | solution.py:287
  5.1 0.1 collective-permute-start.1
  5.2 5.1 %collective-permute-done.near.refs_1_ = f32[168,256]{1,0:T(8,128)S(1)} collective-permute-done((f32[168,256]{1,0:T(8,128)S(1)}, f32[168,256]{1,0:T(8,128)S(1)}, u32[]{:S(2)}, u32[]{:S(2)}) %collective-permute-start) | collective-permute-done | bytes 172064 | tf_op jit(solution)/shard_map/ppermute | solution.py:287
  10.3 0.0 copy-start.3
  10.3 0.3 shard_map.51.refs_0_.refs_1_
  10.6 1.9 %collective-permute-start.2 = (f32[168,256]{1,0:T(8,128)S(1)}, f32[168,256]{1,0:T(8,128)S(1)}, u32[]{:S(2)}, u32[]{:S(2)}) collective-permute-start(f32[168,256]{1,0:T(8,128)S(1)} %shard_map.51.refs_0_.refs_1_), channel_id=1, source_target_pairs={{0,8},{4,12},{8,0},{12,4},{16,24},{20,28},{24,16},{28,20},{1,9},{5... | collective-permute-start | bytes 516104 | tf_op jit(solution)/shard_map/ppermute | solution.py:287
  12.5 0.0 collective-permute-done.1.near.refs_2_
  12.5 0.3 shard_map.52.refs_1_.refs_2_
  12.8 0.6 %collective-permute-start.3 = (f32[88,256]{1,0:T(8,128)S(1)}, f32[88,256]{1,0:T(8,128)S(1)}, u32[]{:S(2)}, u32[]{:S(2)}) collective-permute-start(f32[88,256]{1,0:T(8,128)S(1)} %shard_map.52.refs_1_.refs_2_), channel_id=1, source_target_pairs={{0,8},{4,12},{8,0},{12,4},{16,24},{20,28},{24,16},{28,20},{1,9},{5... | collective-permute-start | bytes 270344 | tf_op jit(solution)/shard_map/ppermute | solution.py:287
  13.5 0.0 copy-done.1
  13.5 0.4 %shard_map.53 = (f32[2,256,256]{2,1,0:T(8,128)S(1)}, f32[2,256,256]{2,1,0:T(8,128)S(1)}) custom-call(f32[2,1,256,256]{3,2,1,0:T(8,128)S(1)} %copy-done.1, f32[168,256]{1,0:T(8,128)S(1)} %collective-permute-done.near.refs_1_, f32[88,256]{1,0:T(8,128)S(1)} %collective-permute-done.1.near.refs_2_), custom_call_target="tpu_custom_call" | custom-call | flops 201326592 | bytes 1048576 | tf_op jit(solution)/shard_map/pallas_call | solution.py:263
  13.9 2.5 %collective-permute-done.2.refs_2_.refs_4_ = f32[168,256]{1,0:T(8,128)S(1)} collective-permute-done((f32[168,256]{1,0:T(8,128)S(1)}, f32[168,256]{1,0:T(8,128)S(1)}, u32[]{:S(2)}, u32[]{:S(2)}) %collective-permute-start.2) | collective-permute-done | bytes 172064 | tf_op jit(solution)/shard_map/ppermute | solution.py:287
  16.4 0.0 copy-start.2
  16.4 0.3 shard_map.54.refs_0_
  16.7 0.7 %collective-permute-done.3.refs_3_.refs_5_ = f32[88,256]{1,0:T(8,128)S(1)} collective-permute-done((f32[88,256]{1,0:T(8,128)S(1)}, f32[88,256]{1,0:T(8,128)S(1)}, u32[]{:S(2)}, u32[]{:S(2)}) %collective-permute-start.3) | collective-permute-done | bytes 90144 | tf_op jit(solution)/shard_map/ppermute | solution.py:287
  17.4 0.4 %shard_map.55 = (f32[256,256]{1,0:T(8,128)S(1)}, f32[64,256]{1,0:T(8,128)S(1)}, f32[128,256]{1,0:T(8,128)S(1)}) custom-call(f32[256,256]{1,0:T(8,128)S(1)} %shard_map.54.refs_0_, f32[168,256]{1,0:T(8,128)S(1)} %shard_map.51.refs_0_.refs_1_, f32[88,256]{1,0:T(8,128)S(1)} %shard_map.52.refs_1_.refs_2_, f32[88,256]{1,0:T(8,128)S(1)} %collective-permute-done.3.refs_3_.refs_5_), custom_call_target="tpu_custom_call" | custom-call | flops 100663296 | bytes 1048576 | tf_op jit(solution)/shard_map/pallas_call | solution.py:263
  17.8 3.6 %collective-permute-start.4 = (f32[64,256]{1,0:T(8,128)S(1)}, f32[64,256]{1,0:T(8,128)S(1)}, u32[]{:S(2)}, u32[]{:S(2)}) collective-permute-start(f32[64,256]{1,0:T(8,128)S(1)} %get-tuple-element.25), channel_id=1, source_target_pairs={{0,24},{4,28},{8,16},{12,20},{16,8},{20,12},{24,0},{28,4},{1,25},{... | collective-permute-start | bytes 196616 | tf_op jit(solution)/shard_map/ppermute | solution.py:287
  21.4 0.0 copy-done.3
  21.4 0.1 copy.5.refs_0_
  21.5 0.0 collective-permute-start.6
  21.5 1.3 %shard_map.56 = (f32[2,256,256]{2,1,0:T(8,128)S(1)}, f32[256,256]{1,0:T(8,128)S(1)}, bf16[2,2,256,256]{3,2,1,0:T(8,128)(2,1)S(1)}, bf16[2,2,256,256]{3,2,1,0:T(8,128)(2,1)S(1)}) custom-call(s32[2,1]{1,0:T(2,128)S(1)} %copy.5.refs_0_, f32[256,256]{1,0:T(8,128)S(1)} %get-tuple-element.26.refs_1_, f32[2,256,256]{2,1,0:T(8,128)S(1)} %get-tuple-element.27.refs_2_, ...), custom_call_target="tpu_custom_call" | custom-call | flops 503316480 | bytes 1048576 | tf_op jit(solution)/shard_map/pallas_call | solution.py:263
  22.8 1.2 %collective-permute-done.4.share = f32[64,256]{1,0:T(8,128)S(1)} collective-permute-done((f32[64,256]{1,0:T(8,128)S(1)}, f32[64,256]{1,0:T(8,128)S(1)}, u32[]{:S(2)}, u32[]{:S(2)}) %collective-permute-start.4) | collective-permute-done | bytes 65568 | tf_op jit(solution)/shard_map/ppermute | solution.py:287
  24.0 1.6 %collective-permute-start.5 = (f32[64,256]{1,0:T(8,128)S(1)}, f32[64,256]{1,0:T(8,128)S(1)}, u32[]{:S(2)}, u32[]{:S(2)}) collective-permute-start(f32[64,256]{1,0:T(8,128)S(1)} %collective-permute-done.4.share), channel_id=1, source_target_pairs={{0,4},{4,0},{8,12},{12,8},{16,20},{20,16},{24,28},{28,24},{1,5},{5... | collective-permute-start | bytes 196616 | tf_op jit(solution)/shard_map/ppermute | solution.py:287
  25.6 0.0 copy-done.2
  25.6 1.6 %shard_map.57.terms = f32[2,3,256,256]{3,2,1,0:T(8,128)S(1)} custom-call(bf16[2,2,256,256]{3,2,1,0:T(8,128)(2,1)S(1)} %get-tuple-element.32.a, bf16[2,2,256,256]{3,2,1,0:T(8,128)(2,1)S(1)} %get-tuple-element.33.b, f32[2,3,1,256,256]{4,3,2,1,0:T(8,128)S(1)} %copy-done.2), custom_call_target="tpu_custom_call" | custom-call | flops 1207959552 | bytes 1048576 | tf_op jit(solution)/shard_map/pallas_call | solution.py:263
  27.3 1.0 %collective-permute-done.5.passed = f32[64,256]{1,0:T(8,128)S(1)} collective-permute-done((f32[64,256]{1,0:T(8,128)S(1)}, f32[64,256]{1,0:T(8,128)S(1)}, u32[]{:S(2)}, u32[]{:S(2)}) %collective-permute-start.5) | collective-permute-done | bytes 65568 | tf_op jit(solution)/shard_map/ppermute | solution.py:287
  28.3 0.0 collective-permute-done.6.rest
  28.3 0.4 %shard_map.58 = (f32[8,128]{1,0:T(8,128)S(1)}, f32[256,256]{1,0:T(8,128)S(1)}) custom-call(f32[64,256]{1,0:T(8,128)S(1)} %collective-permute-done.4.share, f32[64,256]{1,0:T(8,128)S(1)} %collective-permute-done.5.passed, f32[128,256]{1,0:T(8,128)S(1)} %collective-permute-done.6.rest, f32[2,3,256,256]{3,2,1,0:T(8,128)S(1)} %shard_map.57.terms, ...), custom_call_target="tpu_custom_call" | custom-call | flops 201326592 | bytes 1048576 | tf_op jit(solution)/shard_map/pallas_call | solution.py:263
  28.7 0.1 collective-permute-start.7
  28.8 1.6 %collective-permute-start.8 = (f32[8,128]{1,0:T(8,128)S(1)}, f32[8,128]{1,0:T(8,128)S(1)}, u32[]{:S(2)}, u32[]{:S(2)}) collective-permute-start(f32[8,128]{1,0:T(8,128)S(1)} %get-tuple-element.37.refs_0_), channel_id=1, source_target_pairs={{0,2},{1,3},{2,0},{3,1},{4,6},{5,7},{6,4},{7,5},{8,10},{9,11},{10,... | collective-permute-start | bytes 12296 | tf_op jit(solution)/shard_map/ppermute | solution.py:338
  30.4 0.3 collective-permute-start.9
  30.7 0.8 %shard_map.59 = f32[2,1,256,256]{3,2,1,0:T(8,128)} custom-call(f32[256,256]{1,0:T(8,128)S(1)} %get-tuple-element.35.refs_0_, f32[2,256,256]{2,1,0:T(8,128)S(1)} %get-tuple-element.36.refs_1_), custom_call_target="tpu_custom_call" | custom-call | flops 201326592 | bytes 1048576 | tf_op jit(solution)/shard_map/pallas_call | solution.py:263
  31.5 0.3 %collective-permute-done.7.refs_1_ = f32[8,128]{1,0:T(8,128)S(1)} collective-permute-done((f32[8,128]{1,0:T(8,128)S(1)}, f32[8,128]{1,0:T(8,128)S(1)}, u32[]{:S(2)}, u32[]{:S(2)}) %collective-permute-start.7) | collective-permute-done | bytes 4128 | tf_op jit(solution)/shard_map/ppermute | solution.py:338
  31.8 0.7 %collective-permute-done.8.refs_2_ = f32[8,128]{1,0:T(8,128)S(1)} collective-permute-done((f32[8,128]{1,0:T(8,128)S(1)}, f32[8,128]{1,0:T(8,128)S(1)}, u32[]{:S(2)}, u32[]{:S(2)}) %collective-permute-start.8) | collective-permute-done | bytes 4128 | tf_op jit(solution)/shard_map/ppermute | solution.py:338
  32.5 0.0 collective-permute-done.9.refs_3_
  32.5 0.7 %shard_map.60 = f32[2,3]{1,0:T(2,128)} custom-call(f32[8,128]{1,0:T(8,128)S(1)} %get-tuple-element.37.refs_0_, f32[8,128]{1,0:T(8,128)S(1)} %collective-permute-done.7.refs_1_, f32[8,128]{1,0:T(8,128)S(1)} %collective-permute-done.8.refs_2_, f32[8,128]{1,0:T(8,128)S(1)} %collective-permute-done.9.refs_3_), custom_call_target="tpu_custom_call" | custom-call | flops 1000 | bytes 1048576 | tf_op jit(solution)/shard_map/pallas_call | solution.py:263
Async XLA Ops:
  0.6 1.0 %copy-start = (f32[2,1,256,256]{3,2,1,0:T(8,128)S(1)}, f32[2,1,256,256]{3,2,1,0:T(8,128)}, u32[]{:S(2)}) copy-start(f32[2,1,256,256]{3,2,1,0:T(8,128)} %refs_0_.2) | copy-start | bytes 1572868
  1.7 11.8 %copy-start.1 = (f32[2,1,256,256]{3,2,1,0:T(8,128)S(1)}, f32[2,1,256,256]{3,2,1,0:T(8,128)}, u32[]{:S(2)}) copy-start(f32[2,1,256,256]{3,2,1,0:T(8,128)} %refs_0_.2) | copy-start | bytes 1572868
  2.0 8.3 %collective-permute-start = (f32[168,256]{1,0:T(8,128)S(1)}, f32[168,256]{1,0:T(8,128)S(1)}, u32[]{:S(2)}, u32[]{:S(2)}) collective-permute-start(f32[168,256]{1,0:T(8,128)S(1)} %get-tuple-element.20), channel_id=1, source_target_pairs={{0,4},{4,0},{8,12},{12,8},{16,20},{20,16},{24,28},{28,24},{1,5},{5... | collective-permute-start | bytes 516104 | tf_op jit(solution)/shard_map/ppermute | solution.py:287
  5.1 7.4 %collective-permute-start.1 = (f32[88,256]{1,0:T(8,128)S(1)}, f32[88,256]{1,0:T(8,128)S(1)}, u32[]{:S(2)}, u32[]{:S(2)}) collective-permute-start(f32[88,256]{1,0:T(8,128)S(1)} %get-tuple-element.22), channel_id=1, source_target_pairs={{0,4},{4,0},{8,12},{12,8},{16,20},{20,16},{24,28},{28,24},{1,5},{5... | collective-permute-start | bytes 270344 | tf_op jit(solution)/shard_map/ppermute | solution.py:287
  10.3 11.1 %copy-start.3 = (s32[2,1]{0,1:T(1,128)S(1)}, s32[2,1]{0,1:T(1,128)}, u32[]{:S(2)}) copy-start(s32[2,1]{0,1:T(1,128)} %param.5) | copy-start | bytes 28
  10.6 5.8 %collective-permute-start.2 = (f32[168,256]{1,0:T(8,128)S(1)}, f32[168,256]{1,0:T(8,128)S(1)}, u32[]{:S(2)}, u32[]{:S(2)}) collective-permute-start(f32[168,256]{1,0:T(8,128)S(1)} %shard_map.51.refs_0_.refs_1_), channel_id=1, source_target_pairs={{0,8},{4,12},{8,0},{12,4},{16,24},{20,28},{24,16},{28,20},{1,9},{5... | collective-permute-start | bytes 516104 | tf_op jit(solution)/shard_map/ppermute | solution.py:287
  12.8 4.6 %collective-permute-start.3 = (f32[88,256]{1,0:T(8,128)S(1)}, f32[88,256]{1,0:T(8,128)S(1)}, u32[]{:S(2)}, u32[]{:S(2)}) collective-permute-start(f32[88,256]{1,0:T(8,128)S(1)} %shard_map.52.refs_1_.refs_2_), channel_id=1, source_target_pairs={{0,8},{4,12},{8,0},{12,4},{16,24},{20,28},{24,16},{28,20},{1,9},{5... | collective-permute-start | bytes 270344 | tf_op jit(solution)/shard_map/ppermute | solution.py:287
  16.4 9.2 %copy-start.2 = (f32[2,3,1,256,256]{4,3,2,1,0:T(8,128)S(1)}, f32[2,3,1,256,256]{4,3,2,1,0:T(8,128)}, u32[]{:S(2)}) copy-start(f32[2,3,1,256,256]{4,3,2,1,0:T(8,128)} %hamiltonian.1) | copy-start | bytes 4718596
  17.8 6.2 %collective-permute-start.4 = (f32[64,256]{1,0:T(8,128)S(1)}, f32[64,256]{1,0:T(8,128)S(1)}, u32[]{:S(2)}, u32[]{:S(2)}) collective-permute-start(f32[64,256]{1,0:T(8,128)S(1)} %get-tuple-element.25), channel_id=1, source_target_pairs={{0,24},{4,28},{8,16},{12,20},{16,8},{20,12},{24,0},{28,4},{1,25},{... | collective-permute-start | bytes 196616 | tf_op jit(solution)/shard_map/ppermute | solution.py:287
  21.5 6.8 %collective-permute-start.6 = (f32[128,256]{1,0:T(8,128)S(1)}, f32[128,256]{1,0:T(8,128)S(1)}, u32[]{:S(2)}, u32[]{:S(2)}) collective-permute-start(f32[128,256]{1,0:T(8,128)S(1)} %get-tuple-element.31), channel_id=1, source_target_pairs={{0,16},{4,20},{8,24},{12,28},{16,0},{20,4},{24,8},{28,12},{1,17},{... | collective-permute-start | bytes 393224 | tf_op jit(solution)/shard_map/ppermute | solution.py:287
  24.0 4.3 %collective-permute-start.5 = (f32[64,256]{1,0:T(8,128)S(1)}, f32[64,256]{1,0:T(8,128)S(1)}, u32[]{:S(2)}, u32[]{:S(2)}) collective-permute-start(f32[64,256]{1,0:T(8,128)S(1)} %collective-permute-done.4.share), channel_id=1, source_target_pairs={{0,4},{4,0},{8,12},{12,8},{16,20},{20,16},{24,28},{28,24},{1,5},{5... | collective-permute-start | bytes 196616 | tf_op jit(solution)/shard_map/ppermute | solution.py:287
  28.7 3.1 %collective-permute-start.7 = (f32[8,128]{1,0:T(8,128)S(1)}, f32[8,128]{1,0:T(8,128)S(1)}, u32[]{:S(2)}, u32[]{:S(2)}) collective-permute-start(f32[8,128]{1,0:T(8,128)S(1)} %get-tuple-element.37.refs_0_), channel_id=1, source_target_pairs={{0,3},{1,2},{2,1},{3,0},{4,7},{5,6},{6,5},{7,4},{8,11},{9,10},{10,... | collective-permute-start | bytes 12296 | tf_op jit(solution)/shard_map/ppermute | solution.py:338
  28.8 3.7 %collective-permute-start.8 = (f32[8,128]{1,0:T(8,128)S(1)}, f32[8,128]{1,0:T(8,128)S(1)}, u32[]{:S(2)}, u32[]{:S(2)}) collective-permute-start(f32[8,128]{1,0:T(8,128)S(1)} %get-tuple-element.37.refs_0_), channel_id=1, source_target_pairs={{0,2},{1,3},{2,0},{3,1},{4,6},{5,7},{6,4},{7,5},{8,10},{9,11},{10,... | collective-permute-start | bytes 12296 | tf_op jit(solution)/shard_map/ppermute | solution.py:338
  30.4 2.1 %collective-permute-start.9 = (f32[8,128]{1,0:T(8,128)S(1)}, f32[8,128]{1,0:T(8,128)S(1)}, u32[]{:S(2)}, u32[]{:S(2)}) collective-permute-start(f32[8,128]{1,0:T(8,128)S(1)} %get-tuple-element.37.refs_0_), channel_id=1, source_target_pairs={{0,1},{1,0},{2,3},{3,2},{4,5},{5,4},{6,7},{7,6},{8,9},{9,8},{10,11... | collective-permute-start | bytes 12296 | tf_op jit(solution)/shard_map/ppermute | solution.py:338

commit v6 on v5

--- a/solution.py
+++ b/solution.py
@@ -8,11 +8,8 @@
 F32 = jnp.float32
 BF16 = jnp.bfloat16
 VMEM = pl.BlockSpec(memory_space=pltpu.VMEM)
-SMEM = pl.BlockSpec(memory_space=pltpu.SMEM)
 LIMIT = 40 * 1024 * 1024
 LANES = 128
-FIRST = (21, 11)
-SHARE = 8
 
 
 def split(a):
@@ -42,7 +39,9 @@
 
 
 def group_kernel(transfer, whole, *parts):
-    group = product(transfer[0, 0], transfer[1, 0])
+    group = transfer[0, 0]
+    for c in range(1, transfer.shape[0]):
+        group = product(group, transfer[c, 0])
 
     @pl.when(bit(1))
     def _():
@@ -128,23 +127,30 @@
 
 def near_kernel(n, transfer, *refs):
     nears, (left, right) = refs[:n], refs[n:]
-    odd = bit(1)
+    last = transfer.shape[0] - 1
     near = whole_of(nears)
 
-    @pl.when(odd)
+    @pl.when(bit(1))
     def _():
         left[0] = near
-        left[1] = product(near, transfer[0, 0])
-        right[0] = transfer[1, 0]
-        right[1] = eye(near.shape[0])
-
-    @pl.when(jnp.logical_not(odd))
-    def _():
-        value = near.T
+        for c in range(last):
+            left[c + 1] = product(left[c], transfer[c, 0])
+        right[last] = eye(near.shape[0])
+        if last > 0:
+            right[last - 1] = transfer[last, 0]
+        for c in range(last - 2, -1, -1):
+            right[c] = product(transfer[c + 1, 0], right[c + 1])
+
+    @pl.when(jnp.logical_not(bit(1)))
+    def _():
         left[0] = eye(near.shape[0])
-        left[1] = transfer[0, 0]
-        right[0] = product(transfer[1, 0], value)
-        right[1] = value
+        if last > 0:
+            left[1] = transfer[0, 0]
+        for c in range(1, last):
+            left[c + 1] = product(left[c], transfer[c, 0])
+        right[last] = near.T
+        for c in range(last - 1, -1, -1):
+            right[c] = product(transfer[c + 1, 0], right[c + 1])
 
 
 def sides(left, right, fars, lefts, rights):
@@ -259,11 +265,11 @@
         out[c : c + 1] = jnp.sum(jnp.where(row == c * terms + lane, s, 0.0), axis=0, keepdims=True)[:, :terms]
 
 
-def call(kernel, outs, flops, *args, smem=0, scratch=()):
+def call(kernel, outs, flops, *args, scratch=()):
     return pl.pallas_call(
         kernel,
         out_shape=outs,
-        in_specs=[SMEM] * smem + [VMEM] * (len(args) - smem),
+        in_specs=[VMEM] * len(args),
         out_specs=jax.tree.map(lambda _: VMEM, outs),
         scratch_shapes=list(scratch),
         compiler_params=pltpu.CompilerParams(vmem_limit_bytes=LIMIT),
@@ -286,7 +292,8 @@
     def swap(a, k):
         return lax.ppermute(a, "col", [(i, i ^ k) for i in range(total)])
 
-    heights = [8 * h for h in FIRST]
+    first = width * 21 // 256 * 8
+    heights = [first, width - first]
     n = len(heights)
     own, *parts = call(group_kernel, (matrix,) + tuple(array(h, width) for h in heights), one, transfer)
     nears = [swap(part, 1) for part in parts]
@@ -298,7 +305,7 @@
     left, right = call(lambda *refs: near_kernel(n, *refs), (both, both), 2 * one, transfer, *nears)
     fars[0], left = lax.optimization_barrier((fars[0], left))
     begun = call(lambda *refs: begin_kernel(n, *refs), matrix, one, *pairs, *fars[:-1])
-    rows = 8 * SHARE
+    rows = width // 4
     shared = (matrix, array(rows, width), array(width - 2 * rows, width))
     if total <= 8:
         sent, share, rest = call(

time: 33.3 us -> 33.3 us (level)
  no operation moved by 1% of the time
where the time goes in v6:
time: 33.3 us; the launch traced here: 33.1 us
  starting transfers between devices  12.8 us (38%)
  waiting for transfers between devices  11.6 us (35%)
  Pallas kernels  6.82 us (20%)
  local copies, waits for them, and re-layouts  1.14 us (3%)
  between operations  0.73 us (2%)
    ppermute x7, starting transfers between devices, swap(): return lax.ppermute(a, 'col', [(i, i ^ k) for i in range(total)])  10.9 us
    ppermute x7, waiting for transfers between devices, swap(): return lax.ppermute(a, 'col', [(i, i ^ k) for i in range(total)])  10.6 us
    pallas_call x11, Pallas kernels, call(): pl.pallas_call(kernel, out_shape=outs, in_specs=[VMEM] * len(args), out_s...  6.82 us
    ppermute x3, starting transfers between devices, per_device(): lax.ppermute(table, 'sec', [(i, i ^ k) for i in range(sectors)])  1.92 us
    unnamed x9, local copies, waits for them, and re-layouts  1.14 us
    ppermute x3, waiting for transfers between devices, per_device(): lax.ppermute(table, 'sec', [(i, i ^ k) for i in range(sectors)])  1 us
  transfers between devices with their start and end apart: 10, of which 7 were waited for; matrix products, arithmetic and copies ran while one was open for 0% of the time, Pallas kernels for 15%

profile of v6, /device:TPU:0, one launch (start us, length us, event | category | flops | bytes accessed | tf_op | source)
XLA Modules:
  0.0 33.1 jit_solution(8633185710432383227)
XLA Ops:
  0.6 0.0 copy-start
  0.6 1.0 %copy-done = f32[2,1,256,256]{3,2,1,0:T(8,128)S(1)} copy-done((f32[2,1,256,256]{3,2,1,0:T(8,128)S(1)}, f32[2,1,256,256]{3,2,1,0:T(8,128)}, u32[]{:S(2)}) %copy-start) | copy-done | bytes 524312
  1.7 0.0 copy-start.1
  1.7 0.3 shard_map.50
  2.0 3.1 %collective-permute-start = (f32[168,256]{1,0:T(8,128)S(1)}, f32[168,256]{1,0:T(8,128)S(1)}, u32[]{:S(2)}, u32[]{:S(2)}) collective-permute-start(f32[168,256]{1,0:T(8,128)S(1)} %get-tuple-element.20), channel_id=1, source_target_pairs={{0,4},{4,0},{8,12},{12,8},{16,20},{20,16},{24,28},{28,24},{1,5},{5... | collective-permute-start | bytes 516104 | tf_op jit(solution)/shard_map/ppermute | solution.py:293
  5.1 0.1 collective-permute-start.1
  5.2 5.1 %collective-permute-done.near.refs_1_ = f32[168,256]{1,0:T(8,128)S(1)} collective-permute-done((f32[168,256]{1,0:T(8,128)S(1)}, f32[168,256]{1,0:T(8,128)S(1)}, u32[]{:S(2)}, u32[]{:S(2)}) %collective-permute-start) | collective-permute-done | bytes 172064 | tf_op jit(solution)/shard_map/ppermute | solution.py:293
  10.3 0.0 copy-start.3
  10.3 0.3 shard_map.51.refs_0_.refs_1_
  10.6 1.9 %collective-permute-start.2 = (f32[168,256]{1,0:T(8,128)S(1)}, f32[168,256]{1,0:T(8,128)S(1)}, u32[]{:S(2)}, u32[]{:S(2)}) collective-permute-start(f32[168,256]{1,0:T(8,128)S(1)} %shard_map.51.refs_0_.refs_1_), channel_id=1, source_target_pairs={{0,8},{4,12},{8,0},{12,4},{16,24},{20,28},{24,16},{28,20},{1,9},{5... | collective-permute-start | bytes 516104 | tf_op jit(solution)/shard_map/ppermute | solution.py:293
  12.5 0.0 collective-permute-done.1.near.refs_2_
  12.5 0.3 shard_map.52.refs_1_.refs_2_
  12.8 0.6 %collective-permute-start.3 = (f32[88,256]{1,0:T(8,128)S(1)}, f32[88,256]{1,0:T(8,128)S(1)}, u32[]{:S(2)}, u32[]{:S(2)}) collective-permute-start(f32[88,256]{1,0:T(8,128)S(1)} %shard_map.52.refs_1_.refs_2_), channel_id=1, source_target_pairs={{0,8},{4,12},{8,0},{12,4},{16,24},{20,28},{24,16},{28,20},{1,9},{5... | collective-permute-start | bytes 270344 | tf_op jit(solution)/shard_map/ppermute | solution.py:293
  13.5 0.0 copy-done.1
  13.5 0.4 %shard_map.53 = (f32[2,256,256]{2,1,0:T(8,128)S(1)}, f32[2,256,256]{2,1,0:T(8,128)S(1)}) custom-call(f32[2,1,256,256]{3,2,1,0:T(8,128)S(1)} %copy-done.1, f32[168,256]{1,0:T(8,128)S(1)} %collective-permute-done.near.refs_1_, f32[88,256]{1,0:T(8,128)S(1)} %collective-permute-done.1.near.refs_2_), custom_call_target="tpu_custom_call" | custom-call | flops 201326592 | bytes 1048576 | tf_op jit(solution)/shard_map/pallas_call | solution.py:269
  13.9 2.5 %collective-permute-done.2.refs_2_.refs_4_ = f32[168,256]{1,0:T(8,128)S(1)} collective-permute-done((f32[168,256]{1,0:T(8,128)S(1)}, f32[168,256]{1,0:T(8,128)S(1)}, u32[]{:S(2)}, u32[]{:S(2)}) %collective-permute-start.2) | collective-permute-done | bytes 172064 | tf_op jit(solution)/shard_map/ppermute | solution.py:293
  16.4 0.0 copy-start.2
  16.4 0.3 shard_map.54.refs_0_
  16.7 0.7 %collective-permute-done.3.refs_3_.refs_5_ = f32[88,256]{1,0:T(8,128)S(1)} collective-permute-done((f32[88,256]{1,0:T(8,128)S(1)}, f32[88,256]{1,0:T(8,128)S(1)}, u32[]{:S(2)}, u32[]{:S(2)}) %collective-permute-start.3) | collective-permute-done | bytes 90144 | tf_op jit(solution)/shard_map/ppermute | solution.py:293
  17.4 0.4 %shard_map.55 = (f32[256,256]{1,0:T(8,128)S(1)}, f32[64,256]{1,0:T(8,128)S(1)}, f32[128,256]{1,0:T(8,128)S(1)}) custom-call(f32[256,256]{1,0:T(8,128)S(1)} %shard_map.54.refs_0_, f32[168,256]{1,0:T(8,128)S(1)} %shard_map.51.refs_0_.refs_1_, f32[88,256]{1,0:T(8,128)S(1)} %shard_map.52.refs_1_.refs_2_, f32[88,256]{1,0:T(8,128)S(1)} %collective-permute-done.3.refs_3_.refs_5_), custom_call_target="tpu_custom_call" | custom-call | flops 100663296 | bytes 1048576 | tf_op jit(solution)/shard_map/pallas_call | solution.py:269
  17.8 3.6 %collective-permute-start.4 = (f32[64,256]{1,0:T(8,128)S(1)}, f32[64,256]{1,0:T(8,128)S(1)}, u32[]{:S(2)}, u32[]{:S(2)}) collective-permute-start(f32[64,256]{1,0:T(8,128)S(1)} %get-tuple-element.25), channel_id=1, source_target_pairs={{0,24},{4,28},{8,16},{12,20},{16,8},{20,12},{24,0},{28,4},{1,25},{... | collective-permute-start | bytes 196616 | tf_op jit(solution)/shard_map/ppermute | solution.py:293
  21.4 0.0 copy-done.3
  21.4 0.1 copy.5.refs_0_
  21.5 0.0 collective-permute-start.6
  21.5 1.3 %shard_map.56 = (f32[2,256,256]{2,1,0:T(8,128)S(1)}, f32[256,256]{1,0:T(8,128)S(1)}, bf16[2,2,256,256]{3,2,1,0:T(8,128)(2,1)S(1)}, bf16[2,2,256,256]{3,2,1,0:T(8,128)(2,1)S(1)}) custom-call(s32[2,1]{1,0:T(2,128)S(1)} %copy.5.refs_0_, f32[256,256]{1,0:T(8,128)S(1)} %get-tuple-element.26.refs_1_, f32[2,256,256]{2,1,0:T(8,128)S(1)} %get-tuple-element.27.refs_2_, ...), custom_call_target="tpu_custom_call" | custom-call | flops 503316480 | bytes 1048576 | tf_op jit(solution)/shard_map/pallas_call | solution.py:269
  22.8 1.2 %collective-permute-done.4.share = f32[64,256]{1,0:T(8,128)S(1)} collective-permute-done((f32[64,256]{1,0:T(8,128)S(1)}, f32[64,256]{1,0:T(8,128)S(1)}, u32[]{:S(2)}, u32[]{:S(2)}) %collective-permute-start.4) | collective-permute-done | bytes 65568 | tf_op jit(solution)/shard_map/ppermute | solution.py:293
  24.0 1.6 %collective-permute-start.5 = (f32[64,256]{1,0:T(8,128)S(1)}, f32[64,256]{1,0:T(8,128)S(1)}, u32[]{:S(2)}, u32[]{:S(2)}) collective-permute-start(f32[64,256]{1,0:T(8,128)S(1)} %collective-permute-done.4.share), channel_id=1, source_target_pairs={{0,4},{4,0},{8,12},{12,8},{16,20},{20,16},{24,28},{28,24},{1,5},{5... | collective-permute-start | bytes 196616 | tf_op jit(solution)/shard_map/ppermute | solution.py:293
  25.6 0.0 copy-done.2
  25.6 1.6 %shard_map.57.terms = f32[2,3,256,256]{3,2,1,0:T(8,128)S(1)} custom-call(bf16[2,2,256,256]{3,2,1,0:T(8,128)(2,1)S(1)} %get-tuple-element.32.a, bf16[2,2,256,256]{3,2,1,0:T(8,128)(2,1)S(1)} %get-tuple-element.33.b, f32[2,3,1,256,256]{4,3,2,1,0:T(8,128)S(1)} %copy-done.2), custom_call_target="tpu_custom_call" | custom-call | flops 1207959552 | bytes 1048576 | tf_op jit(solution)/shard_map/pallas_call | solution.py:269
  27.3 1.0 %collective-permute-done.5.passed = f32[64,256]{1,0:T(8,128)S(1)} collective-permute-done((f32[64,256]{1,0:T(8,128)S(1)}, f32[64,256]{1,0:T(8,128)S(1)}, u32[]{:S(2)}, u32[]{:S(2)}) %collective-permute-start.5) | collective-permute-done | bytes 65568 | tf_op jit(solution)/shard_map/ppermute | solution.py:293
  28.3 0.0 collective-permute-done.6.rest
  28.3 0.4 %shard_map.58 = (f32[8,128]{1,0:T(8,128)S(1)}, f32[256,256]{1,0:T(8,128)S(1)}) custom-call(f32[64,256]{1,0:T(8,128)S(1)} %collective-permute-done.4.share, f32[64,256]{1,0:T(8,128)S(1)} %collective-permute-done.5.passed, f32[128,256]{1,0:T(8,128)S(1)} %collective-permute-done.6.rest, f32[2,3,256,256]{3,2,1,0:T(8,128)S(1)} %shard_map.57.terms, ...), custom_call_target="tpu_custom_call" | custom-call | flops 201326592 | bytes 1048576 | tf_op jit(solution)/shard_map/pallas_call | solution.py:269
  28.7 0.1 collective-permute-start.7
  28.8 1.6 %collective-permute-start.8 = (f32[8,128]{1,0:T(8,128)S(1)}, f32[8,128]{1,0:T(8,128)S(1)}, u32[]{:S(2)}, u32[]{:S(2)}) collective-permute-start(f32[8,128]{1,0:T(8,128)S(1)} %get-tuple-element.37.refs_0_), channel_id=1, source_target_pairs={{0,2},{1,3},{2,0},{3,1},{4,6},{5,7},{6,4},{7,5},{8,10},{9,11},{10,... | collective-permute-start | bytes 12296 | tf_op jit(solution)/shard_map/ppermute | solution.py:345
  30.4 0.3 collective-permute-start.9
  30.7 0.8 %shard_map.59 = f32[2,1,256,256]{3,2,1,0:T(8,128)} custom-call(f32[256,256]{1,0:T(8,128)S(1)} %get-tuple-element.35.refs_0_, f32[2,256,256]{2,1,0:T(8,128)S(1)} %get-tuple-element.36.refs_1_), custom_call_target="tpu_custom_call" | custom-call | flops 201326592 | bytes 1048576 | tf_op jit(solution)/shard_map/pallas_call | solution.py:269
  31.5 0.3 %collective-permute-done.7.refs_1_ = f32[8,128]{1,0:T(8,128)S(1)} collective-permute-done((f32[8,128]{1,0:T(8,128)S(1)}, f32[8,128]{1,0:T(8,128)S(1)}, u32[]{:S(2)}, u32[]{:S(2)}) %collective-permute-start.7) | collective-permute-done | bytes 4128 | tf_op jit(solution)/shard_map/ppermute | solution.py:345
  31.8 0.7 %collective-permute-done.8.refs_2_ = f32[8,128]{1,0:T(8,128)S(1)} collective-permute-done((f32[8,128]{1,0:T(8,128)S(1)}, f32[8,128]{1,0:T(8,128)S(1)}, u32[]{:S(2)}, u32[]{:S(2)}) %collective-permute-start.8) | collective-permute-done | bytes 4128 | tf_op jit(solution)/shard_map/ppermute | solution.py:345
  32.5 0.0 collective-permute-done.9.refs_3_
  32.5 0.7 %shard_map.60 = f32[2,3]{1,0:T(2,128)} custom-call(f32[8,128]{1,0:T(8,128)S(1)} %get-tuple-element.37.refs_0_, f32[8,128]{1,0:T(8,128)S(1)} %collective-permute-done.7.refs_1_, f32[8,128]{1,0:T(8,128)S(1)} %collective-permute-done.8.refs_2_, f32[8,128]{1,0:T(8,128)S(1)} %collective-permute-done.9.refs_3_), custom_call_target="tpu_custom_call" | custom-call | flops 1000 | bytes 1048576 | tf_op jit(solution)/shard_map/pallas_call | solution.py:269
Async XLA Ops:
  0.6 1.0 %copy-start = (f32[2,1,256,256]{3,2,1,0:T(8,128)S(1)}, f32[2,1,256,256]{3,2,1,0:T(8,128)}, u32[]{:S(2)}) copy-start(f32[2,1,256,256]{3,2,1,0:T(8,128)} %refs_0_.2) | copy-start | bytes 1572868
  1.7 11.8 %copy-start.1 = (f32[2,1,256,256]{3,2,1,0:T(8,128)S(1)}, f32[2,1,256,256]{3,2,1,0:T(8,128)}, u32[]{:S(2)}) copy-start(f32[2,1,256,256]{3,2,1,0:T(8,128)} %refs_0_.2) | copy-start | bytes 1572868
  2.0 8.3 %collective-permute-start = (f32[168,256]{1,0:T(8,128)S(1)}, f32[168,256]{1,0:T(8,128)S(1)}, u32[]{:S(2)}, u32[]{:S(2)}) collective-permute-start(f32[168,256]{1,0:T(8,128)S(1)} %get-tuple-element.20), channel_id=1, source_target_pairs={{0,4},{4,0},{8,12},{12,8},{16,20},{20,16},{24,28},{28,24},{1,5},{5... | collective-permute-start | bytes 516104 | tf_op jit(solution)/shard_map/ppermute | solution.py:293
  5.1 7.4 %collective-permute-start.1 = (f32[88,256]{1,0:T(8,128)S(1)}, f32[88,256]{1,0:T(8,128)S(1)}, u32[]{:S(2)}, u32[]{:S(2)}) collective-permute-start(f32[88,256]{1,0:T(8,128)S(1)} %get-tuple-element.22), channel_id=1, source_target_pairs={{0,4},{4,0},{8,12},{12,8},{16,20},{20,16},{24,28},{28,24},{1,5},{5... | collective-permute-start | bytes 270344 | tf_op jit(solution)/shard_map/ppermute | solution.py:293
  10.3 11.1 %copy-start.3 = (s32[2,1]{0,1:T(1,128)S(1)}, s32[2,1]{0,1:T(1,128)}, u32[]{:S(2)}) copy-start(s32[2,1]{0,1:T(1,128)} %param.5) | copy-start | bytes 28
  10.6 5.8 %collective-permute-start.2 = (f32[168,256]{1,0:T(8,128)S(1)}, f32[168,256]{1,0:T(8,128)S(1)}, u32[]{:S(2)}, u32[]{:S(2)}) collective-permute-start(f32[168,256]{1,0:T(8,128)S(1)} %shard_map.51.refs_0_.refs_1_), channel_id=1, source_target_pairs={{0,8},{4,12},{8,0},{12,4},{16,24},{20,28},{24,16},{28,20},{1,9},{5... | collective-permute-start | bytes 516104 | tf_op jit(solution)/shard_map/ppermute | solution.py:293
  12.8 4.6 %collective-permute-start.3 = (f32[88,256]{1,0:T(8,128)S(1)}, f32[88,256]{1,0:T(8,128)S(1)}, u32[]{:S(2)}, u32[]{:S(2)}) collective-permute-start(f32[88,256]{1,0:T(8,128)S(1)} %shard_map.52.refs_1_.refs_2_), channel_id=1, source_target_pairs={{0,8},{4,12},{8,0},{12,4},{16,24},{20,28},{24,16},{28,20},{1,9},{5... | collective-permute-start | bytes 270344 | tf_op jit(solution)/shard_map/ppermute | solution.py:293
  16.4 9.2 %copy-start.2 = (f32[2,3,1,256,256]{4,3,2,1,0:T(8,128)S(1)}, f32[2,3,1,256,256]{4,3,2,1,0:T(8,128)}, u32[]{:S(2)}) copy-start(f32[2,3,1,256,256]{4,3,2,1,0:T(8,128)} %hamiltonian.1) | copy-start | bytes 4718596
  17.8 6.2 %collective-permute-start.4 = (f32[64,256]{1,0:T(8,128)S(1)}, f32[64,256]{1,0:T(8,128)S(1)}, u32[]{:S(2)}, u32[]{:S(2)}) collective-permute-start(f32[64,256]{1,0:T(8,128)S(1)} %get-tuple-element.25), channel_id=1, source_target_pairs={{0,24},{4,28},{8,16},{12,20},{16,8},{20,12},{24,0},{28,4},{1,25},{... | collective-permute-start | bytes 196616 | tf_op jit(solution)/shard_map/ppermute | solution.py:293
  21.5 6.8 %collective-permute-start.6 = (f32[128,256]{1,0:T(8,128)S(1)}, f32[128,256]{1,0:T(8,128)S(1)}, u32[]{:S(2)}, u32[]{:S(2)}) collective-permute-start(f32[128,256]{1,0:T(8,128)S(1)} %get-tuple-element.31), channel_id=1, source_target_pairs={{0,16},{4,20},{8,24},{12,28},{16,0},{20,4},{24,8},{28,12},{1,17},{... | collective-permute-start | bytes 393224 | tf_op jit(solution)/shard_map/ppermute | solution.py:293
  24.0 4.3 %collective-permute-start.5 = (f32[64,256]{1,0:T(8,128)S(1)}, f32[64,256]{1,0:T(8,128)S(1)}, u32[]{:S(2)}, u32[]{:S(2)}) collective-permute-start(f32[64,256]{1,0:T(8,128)S(1)} %collective-permute-done.4.share), channel_id=1, source_target_pairs={{0,4},{4,0},{8,12},{12,8},{16,20},{20,16},{24,28},{28,24},{1,5},{5... | collective-permute-start | bytes 196616 | tf_op jit(solution)/shard_map/ppermute | solution.py:293
  28.7 3.1 %collective-permute-start.7 = (f32[8,128]{1,0:T(8,128)S(1)}, f32[8,128]{1,0:T(8,128)S(1)}, u32[]{:S(2)}, u32[]{:S(2)}) collective-permute-start(f32[8,128]{1,0:T(8,128)S(1)} %get-tuple-element.37.refs_0_), channel_id=1, source_target_pairs={{0,3},{1,2},{2,1},{3,0},{4,7},{5,6},{6,5},{7,4},{8,11},{9,10},{10,... | collective-permute-start | bytes 12296 | tf_op jit(solution)/shard_map/ppermute | solution.py:345
  28.8 3.7 %collective-permute-start.8 = (f32[8,128]{1,0:T(8,128)S(1)}, f32[8,128]{1,0:T(8,128)S(1)}, u32[]{:S(2)}, u32[]{:S(2)}) collective-permute-start(f32[8,128]{1,0:T(8,128)S(1)} %get-tuple-element.37.refs_0_), channel_id=1, source_target_pairs={{0,2},{1,3},{2,0},{3,1},{4,6},{5,7},{6,4},{7,5},{8,10},{9,11},{10,... | collective-permute-start | bytes 12296 | tf_op jit(solution)/shard_map/ppermute | solution.py:345
  30.4 2.1 %collective-permute-start.9 = (f32[8,128]{1,0:T(8,128)S(1)}, f32[8,128]{1,0:T(8,128)S(1)}, u32[]{:S(2)}, u32[]{:S(2)}) collective-permute-start(f32[8,128]{1,0:T(8,128)S(1)} %get-tuple-element.37.refs_0_), channel_id=1, source_target_pairs={{0,1},{1,0},{2,3},{3,2},{4,5},{5,4},{6,7},{7,6},{8,9},{9,8},{10,11... | collective-permute-start | bytes 12296 | tf_op jit(solution)/shard_map/ppermute | solution.py:345

commit v7 on v6

--- a/solution.py
+++ b/solution.py
@@ -57,8 +57,12 @@
         at += part.shape[0]
 
 
-def pair_kernel(near, own, out):
-    out[...] = multiply(split(near[...]), split(own[...]), ((1,), (1,)))
+def turn_kernel(whole, turned):
+    turned[0], turned[1] = split(whole[...].T)
+
+
+def pair_kernel(near, turned, out):
+    out[...] = multiply(split(near[...]), (turned[0], turned[1]))
 
 
 def whole_of(parts):
@@ -125,7 +129,7 @@
     spread(whole[...], bit(k), sent, share, rest)
 
 
-def near_kernel(n, transfer, *refs):
+def near_kernel(n, kept, transfer, *refs):
     nears, (left, right) = refs[:n], refs[n:]
     last = transfer.shape[0] - 1
     near = whole_of(nears)
@@ -152,6 +156,10 @@
         for c in range(last - 1, -1, -1):
             right[c] = product(transfer[c + 1, 0], right[c + 1])
 
+    column = lax.broadcasted_iota(jnp.int32, near.shape, 1)
+    for c in range(last + 1):
+        left[c] = jnp.where(column < kept[c : c + 1], left[c], 0.0)
+
 
 def sides(left, right, fars, lefts, rights):
     high = bit(2)
@@ -185,34 +193,32 @@
         right_out[c] = product(right[c], jnp.where(after, one, x))
 
 
-def prepare(k, kept, sent, lefts, rights, lefts_out, norm_out, a_out, b_out):
+def prepare(k, sent, lefts, rights, norm_out, a_out, b_out):
     y, transposed = split(sent[...]), split(sent[...].T)
     norm_out[...] = multiply(transposed, y)
-    column = lax.broadcasted_iota(jnp.int32, lefts.shape[1:], 1)
-    for c in range(lefts.shape[0]):
-        lefts_out[c] = jnp.where(column < kept[c : c + 1], lefts[c], 0.0)
 
     @pl.when(bit(k))
     def _():
         for c in range(lefts.shape[0]):
-            a_out[c, 0], a_out[c, 1] = split(lefts_out[c])
+            a_out[c, 0], a_out[c, 1] = split(lefts[c])
             b_out[c, 0], b_out[c, 1] = split(multiply(split(rights[c]), y))
 
     @pl.when(jnp.logical_not(bit(k)))
     def _():
         for c in range(lefts.shape[0]):
-            a_out[c, 0], a_out[c, 1] = split(multiply(transposed, split(lefts_out[c])))
+            a_out[c, 0], a_out[c, 1] = split(multiply(transposed, split(lefts[c])))
             b_out[c, 0], b_out[c, 1] = split(rights[c])
 
 
-def prepare_quad_kernel(n, k, kept, sent, left, right, *refs):
-    fars, outs, (lefts, rights) = refs[:n], refs[n:-2], refs[-2:]
+def prepare_quad_kernel(n, k, sent, left, right, *refs):
+    fars, (lefts, *outs), rights = refs[:n], refs[n:-1], refs[-1]
     sides(left, right, fars, lefts, rights)
-    prepare(k, kept, sent, lefts, rights, *outs)
-
-
-def prepare_kernel(k, kept, sent, lefts, rights, *outs):
-    prepare(k, kept, sent, lefts, rights, *outs)
+    prepare(k, sent, lefts, rights, *outs)
+
+
+def prepare_kernel(k, sent, left, right, lefts, *outs):
+    lefts[...] = left[...]
+    prepare(k, sent, lefts, right, *outs)
 
 
 def terms_kernel(a, b, hamiltonian, out):
@@ -295,14 +301,15 @@
     first = width * 21 // 256 * 8
     heights = [first, width - first]
     n = len(heights)
-    own, *parts = call(group_kernel, (matrix,) + tuple(array(h, width) for h in heights), one, transfer)
+    whole, *parts = call(group_kernel, (matrix,) + tuple(array(h, width) for h in heights), one, transfer)
+    turned = call(turn_kernel, array(2, width, width, dtype=BF16), one // 4, whole)
     nears = [swap(part, 1) for part in parts]
     pairs, fars = [], []
     for near, h in zip(nears, heights):
-        pairs.append(call(pair_kernel, array(h, width), one // n, near, own))
+        pairs.append(call(pair_kernel, array(h, width), one // n, near, turned))
         fars.append(swap(pairs[-1], 2))
     both = array(columns, width, width)
-    left, right = call(lambda *refs: near_kernel(n, *refs), (both, both), 2 * one, transfer, *nears)
+    left, right = call(lambda *refs: near_kernel(n, *refs), (both, both), 2 * one, kept, transfer, *nears)
     fars[0], left = lax.optimization_barrier((fars[0], left))
     begun = call(lambda *refs: begin_kernel(n, *refs), matrix, one, *pairs, *fars[:-1])
     rows = width // 4
@@ -328,12 +335,12 @@
     prepared = (array(columns, width, width), matrix, halves, halves)
     if total <= 8:
         lefts, norm, a, b = call(
-            lambda *refs: prepare_quad_kernel(n, half, *refs), prepared, 5 * one, kept, sent, left, right, *fars,
-            scratch=(pltpu.VMEM((columns, width, width), F32),) * 2,
+            lambda *refs: prepare_quad_kernel(n, half, *refs), prepared, 5 * one, sent, left, right, *fars,
+            scratch=(pltpu.VMEM((columns, width, width), F32),),
         )
     else:
         lefts, norm, a, b = call(
-            lambda *refs: prepare_kernel(half, *refs), prepared, 3 * one, kept, sent, left, right
+            lambda *refs: prepare_kernel(half, *refs), prepared, 3 * one, sent, left, right
         )
     share, norm = lax.optimization_barrier((share, norm))
     passed = swap(share, 1)

time: 33.3 us -> 33.2 us (level)
    pallas_call x11 -> x12, Pallas kernels: 6.82 us -> 6.9 us  [call(): pl.pallas_call(kernel, out_shape=outs, in_specs=[VMEM] * len(args), out_s...]
where the time goes in v7:
time: 33.2 us; the launch traced here: 33.1 us
  starting transfers between devices  12.9 us (39%)
  waiting for transfers between devices  11.4 us (34%)
  Pallas kernels  6.9 us (21%)
  local copies, waits for them, and re-layouts  1.14 us (3%)
  between operations  0.74 us (2%)
    ppermute x7, starting transfers between devices, swap(): return lax.ppermute(a, 'col', [(i, i ^ k) for i in range(total)])  10.9 us
    ppermute x7, waiting for transfers between devices, swap(): return lax.ppermute(a, 'col', [(i, i ^ k) for i in range(total)])  10.4 us
    pallas_call x12, Pallas kernels, call(): pl.pallas_call(kernel, out_shape=outs, in_specs=[VMEM] * len(args), out_s...  6.9 us
    ppermute x3, starting transfers between devices, per_device(): lax.ppermute(table, 'sec', [(i, i ^ k) for i in range(sectors)])  1.92 us
    unnamed x9, local copies, waits for them, and re-layouts  1.14 us
    ppermute x3, waiting for transfers between devices, per_device(): lax.ppermute(table, 'sec', [(i, i ^ k) for i in range(sectors)])  1 us
  transfers between devices with their start and end apart: 10, of which 7 were waited for; matrix products, arithmetic and copies ran while one was open for 0% of the time, Pallas kernels for 15%

profile of v7, /device:TPU:0, one launch (start us, length us, event | category | flops | bytes accessed | tf_op | source)
XLA Modules:
  0.0 33.1 jit_solution(17531924392619613683)
XLA Ops:
  0.6 0.0 copy-start
  0.6 1.0 %copy-done = f32[2,1,256,256]{3,2,1,0:T(8,128)S(1)} copy-done((f32[2,1,256,256]{3,2,1,0:T(8,128)S(1)}, f32[2,1,256,256]{3,2,1,0:T(8,128)}, u32[]{:S(2)}) %copy-start) | copy-done | bytes 524312
  1.7 0.0 copy-start.3
  1.7 0.0 copy-start.1
  1.7 0.3 shard_map.50
  2.0 3.1 %collective-permute-start = (f32[168,256]{1,0:T(8,128)S(1)}, f32[168,256]{1,0:T(8,128)S(1)}, u32[]{:S(2)}, u32[]{:S(2)}) collective-permute-start(f32[168,256]{1,0:T(8,128)S(1)} %get-tuple-element.20), channel_id=1, source_target_pairs={{0,4},{4,0},{8,12},{12,8},{16,20},{20,16},{24,28},{28,24},{1,5},{5... | collective-permute-start | bytes 516104 | tf_op jit(solution)/shard_map/ppermute | solution.py:299
  5.1 0.1 collective-permute-start.1
  5.2 0.1 shard_map.51.turned
  5.3 5.0 %collective-permute-done.near.refs_2_ = f32[168,256]{1,0:T(8,128)S(1)} collective-permute-done((f32[168,256]{1,0:T(8,128)S(1)}, f32[168,256]{1,0:T(8,128)S(1)}, u32[]{:S(2)}, u32[]{:S(2)}) %collective-permute-start) | collective-permute-done | bytes 172064 | tf_op jit(solution)/shard_map/ppermute | solution.py:299
  10.3 0.2 shard_map.52.refs_0_.refs_1_
  10.5 1.9 %collective-permute-start.2 = (f32[168,256]{1,0:T(8,128)S(1)}, f32[168,256]{1,0:T(8,128)S(1)}, u32[]{:S(2)}, u32[]{:S(2)}) collective-permute-start(f32[168,256]{1,0:T(8,128)S(1)} %shard_map.52.refs_0_.refs_1_), channel_id=1, source_target_pairs={{0,8},{4,12},{8,0},{12,4},{16,24},{20,28},{24,16},{28,20},{1,9},{5... | collective-permute-start | bytes 516104 | tf_op jit(solution)/shard_map/ppermute | solution.py:299
  12.5 0.0 collective-permute-done.1.near.refs_3_
  12.5 0.2 shard_map.53.refs_1_.refs_2_
  12.7 0.7 %collective-permute-start.3 = (f32[88,256]{1,0:T(8,128)S(1)}, f32[88,256]{1,0:T(8,128)S(1)}, u32[]{:S(2)}, u32[]{:S(2)}) collective-permute-start(f32[88,256]{1,0:T(8,128)S(1)} %shard_map.53.refs_1_.refs_2_), channel_id=1, source_target_pairs={{0,8},{4,12},{8,0},{12,4},{16,24},{20,28},{24,16},{28,20},{1,9},{5... | collective-permute-start | bytes 270344 | tf_op jit(solution)/shard_map/ppermute | solution.py:299
  13.4 0.0 copy-done.3
  13.4 0.1 copy.5.refs_0_
  13.5 0.0 copy-done.1
  13.5 0.5 %shard_map.54 = (f32[2,256,256]{2,1,0:T(8,128)S(1)}, f32[2,256,256]{2,1,0:T(8,128)S(1)}) custom-call(s32[2,1]{1,0:T(2,128)S(1)} %copy.5.refs_0_, f32[2,1,256,256]{3,2,1,0:T(8,128)S(1)} %copy-done.1, f32[168,256]{1,0:T(8,128)S(1)} %collective-permute-done.near.refs_2_, f32[88,256]{1,0:T(8,128)S(1)} %collective-permute-done.1.near.refs_3_), custom_call_target="tpu_custom_call" | custom-call | flops 201326592 | bytes 1048576 | tf_op jit(solution)/shard_map/pallas_call | solution.py:275
  14.0 2.4 %collective-permute-done.2.refs_2_.refs_3_ = f32[168,256]{1,0:T(8,128)S(1)} collective-permute-done((f32[168,256]{1,0:T(8,128)S(1)}, f32[168,256]{1,0:T(8,128)S(1)}, u32[]{:S(2)}, u32[]{:S(2)}) %collective-permute-start.2) | collective-permute-done | bytes 172064 | tf_op jit(solution)/shard_map/ppermute | solution.py:299
  16.4 0.0 copy-start.2
  16.4 0.3 shard_map.55.refs_0_
  16.6 0.7 %collective-permute-done.3.refs_3_.refs_4_ = f32[88,256]{1,0:T(8,128)S(1)} collective-permute-done((f32[88,256]{1,0:T(8,128)S(1)}, f32[88,256]{1,0:T(8,128)S(1)}, u32[]{:S(2)}, u32[]{:S(2)}) %collective-permute-start.3) | collective-permute-done | bytes 90144 | tf_op jit(solution)/shard_map/ppermute | solution.py:299
  17.3 0.4 %shard_map.56 = (f32[256,256]{1,0:T(8,128)S(1)}, f32[64,256]{1,0:T(8,128)S(1)}, f32[128,256]{1,0:T(8,128)S(1)}) custom-call(f32[256,256]{1,0:T(8,128)S(1)} %shard_map.55.refs_0_, f32[168,256]{1,0:T(8,128)S(1)} %shard_map.52.refs_0_.refs_1_, f32[88,256]{1,0:T(8,128)S(1)} %shard_map.53.refs_1_.refs_2_, f32[88,256]{1,0:T(8,128)S(1)} %collective-permute-done.3.refs_3_.refs_4_), custom_call_target="tpu_custom_call" | custom-call | flops 100663296 | bytes 1048576 | tf_op jit(solution)/shard_map/pallas_call | solution.py:275
  17.7 3.6 %collective-permute-start.4 = (f32[64,256]{1,0:T(8,128)S(1)}, f32[64,256]{1,0:T(8,128)S(1)}, u32[]{:S(2)}, u32[]{:S(2)}) collective-permute-start(f32[64,256]{1,0:T(8,128)S(1)} %get-tuple-element.25), channel_id=1, source_target_pairs={{0,24},{4,28},{8,16},{12,20},{16,8},{20,12},{24,0},{28,4},{1,25},{... | collective-permute-start | bytes 196616 | tf_op jit(solution)/shard_map/ppermute | solution.py:299
  21.3 0.0 collective-permute-start.6
  21.3 1.3 %shard_map.57 = (f32[2,256,256]{2,1,0:T(8,128)S(1)}, f32[256,256]{1,0:T(8,128)S(1)}, bf16[2,2,256,256]{3,2,1,0:T(8,128)(2,1)S(1)}, bf16[2,2,256,256]{3,2,1,0:T(8,128)(2,1)S(1)}) custom-call(f32[256,256]{1,0:T(8,128)S(1)} %get-tuple-element.26.refs_0_, f32[2,256,256]{2,1,0:T(8,128)S(1)} %get-tuple-element.27.refs_1_, ...), custom_call_target="tpu_custom_call" | custom-call | flops 503316480 | bytes 1048576 | tf_op jit(solution)/shard_map/pallas_call | solution.py:275
  22.7 1.3 %collective-permute-done.4.share = f32[64,256]{1,0:T(8,128)S(1)} collective-permute-done((f32[64,256]{1,0:T(8,128)S(1)}, f32[64,256]{1,0:T(8,128)S(1)}, u32[]{:S(2)}, u32[]{:S(2)}) %collective-permute-start.4) | collective-permute-done | bytes 65568 | tf_op jit(solution)/shard_map/ppermute | solution.py:299
  24.0 1.5 %collective-permute-start.5 = (f32[64,256]{1,0:T(8,128)S(1)}, f32[64,256]{1,0:T(8,128)S(1)}, u32[]{:S(2)}, u32[]{:S(2)}) collective-permute-start(f32[64,256]{1,0:T(8,128)S(1)} %collective-permute-done.4.share), channel_id=1, source_target_pairs={{0,4},{4,0},{8,12},{12,8},{16,20},{20,16},{24,28},{28,24},{1,5},{5... | collective-permute-start | bytes 196616 | tf_op jit(solution)/shard_map/ppermute | solution.py:299
  25.5 0.0 copy-done.2
  25.5 1.7 %shard_map.58.terms = f32[2,3,256,256]{3,2,1,0:T(8,128)S(1)} custom-call(bf16[2,2,256,256]{3,2,1,0:T(8,128)(2,1)S(1)} %get-tuple-element.32.a, bf16[2,2,256,256]{3,2,1,0:T(8,128)(2,1)S(1)} %get-tuple-element.33.b, f32[2,3,1,256,256]{4,3,2,1,0:T(8,128)S(1)} %copy-done.2), custom_call_target="tpu_custom_call" | custom-call | flops 1207959552 | bytes 1048576 | tf_op jit(solution)/shard_map/pallas_call | solution.py:275
  27.2 1.1 %collective-permute-done.5.passed = f32[64,256]{1,0:T(8,128)S(1)} collective-permute-done((f32[64,256]{1,0:T(8,128)S(1)}, f32[64,256]{1,0:T(8,128)S(1)}, u32[]{:S(2)}, u32[]{:S(2)}) %collective-permute-start.5) | collective-permute-done | bytes 65568 | tf_op jit(solution)/shard_map/ppermute | solution.py:299
  28.2 0.0 collective-permute-done.6.rest
  28.2 0.4 %shard_map.59 = (f32[8,128]{1,0:T(8,128)S(1)}, f32[256,256]{1,0:T(8,128)S(1)}) custom-call(f32[64,256]{1,0:T(8,128)S(1)} %collective-permute-done.4.share, f32[64,256]{1,0:T(8,128)S(1)} %collective-permute-done.5.passed, f32[128,256]{1,0:T(8,128)S(1)} %collective-permute-done.6.rest, f32[2,3,256,256]{3,2,1,0:T(8,128)S(1)} %shard_map.58.terms, ...), custom_call_target="tpu_custom_call" | custom-call | flops 201326592 | bytes 1048576 | tf_op jit(solution)/shard_map/pallas_call | solution.py:275
  28.7 0.1 collective-permute-start.7
  28.7 1.5 %collective-permute-start.8 = (f32[8,128]{1,0:T(8,128)S(1)}, f32[8,128]{1,0:T(8,128)S(1)}, u32[]{:S(2)}, u32[]{:S(2)}) collective-permute-start(f32[8,128]{1,0:T(8,128)S(1)} %get-tuple-element.37.refs_0_), channel_id=1, source_target_pairs={{0,2},{1,3},{2,0},{3,1},{4,6},{5,7},{6,4},{7,5},{8,10},{9,11},{10,... | collective-permute-start | bytes 12296 | tf_op jit(solution)/shard_map/ppermute | solution.py:352
  30.3 0.3 %collective-permute-start.9 = (f32[8,128]{1,0:T(8,128)S(1)}, f32[8,128]{1,0:T(8,128)S(1)}, u32[]{:S(2)}, u32[]{:S(2)}) collective-permute-start(f32[8,128]{1,0:T(8,128)S(1)} %get-tuple-element.37.refs_0_), channel_id=1, source_target_pairs={{0,1},{1,0},{2,3},{3,2},{4,5},{5,4},{6,7},{7,6},{8,9},{9,8},{10,11... | collective-permute-start | bytes 12296 | tf_op jit(solution)/shard_map/ppermute | solution.py:352
  30.6 0.8 %shard_map.60 = f32[2,1,256,256]{3,2,1,0:T(8,128)} custom-call(f32[256,256]{1,0:T(8,128)S(1)} %get-tuple-element.35.refs_0_, f32[2,256,256]{2,1,0:T(8,128)S(1)} %get-tuple-element.36.refs_1_), custom_call_target="tpu_custom_call" | custom-call | flops 201326592 | bytes 1048576 | tf_op jit(solution)/shard_map/pallas_call | solution.py:275
  31.4 0.4 %collective-permute-done.7.refs_1_ = f32[8,128]{1,0:T(8,128)S(1)} collective-permute-done((f32[8,128]{1,0:T(8,128)S(1)}, f32[8,128]{1,0:T(8,128)S(1)}, u32[]{:S(2)}, u32[]{:S(2)}) %collective-permute-start.7) | collective-permute-done | bytes 4128 | tf_op jit(solution)/shard_map/ppermute | solution.py:352
  31.8 0.6 %collective-permute-done.8.refs_2_ = f32[8,128]{1,0:T(8,128)S(1)} collective-permute-done((f32[8,128]{1,0:T(8,128)S(1)}, f32[8,128]{1,0:T(8,128)S(1)}, u32[]{:S(2)}, u32[]{:S(2)}) %collective-permute-start.8) | collective-permute-done | bytes 4128 | tf_op jit(solution)/shard_map/ppermute | solution.py:352
  32.4 0.0 collective-permute-done.9.refs_3_
  32.4 0.7 %shard_map.61 = f32[2,3]{1,0:T(2,128)} custom-call(f32[8,128]{1,0:T(8,128)S(1)} %get-tuple-element.37.refs_0_, f32[8,128]{1,0:T(8,128)S(1)} %collective-permute-done.7.refs_1_, f32[8,128]{1,0:T(8,128)S(1)} %collective-permute-done.8.refs_2_, f32[8,128]{1,0:T(8,128)S(1)} %collective-permute-done.9.refs_3_), custom_call_target="tpu_custom_call" | custom-call | flops 1000 | bytes 1048576 | tf_op jit(solution)/shard_map/pallas_call | solution.py:275
Async XLA Ops:
  0.6 1.0 %copy-start = (f32[2,1,256,256]{3,2,1,0:T(8,128)S(1)}, f32[2,1,256,256]{3,2,1,0:T(8,128)}, u32[]{:S(2)}) copy-start(f32[2,1,256,256]{3,2,1,0:T(8,128)} %refs_1_.1) | copy-start | bytes 1572868
  1.7 11.7 %copy-start.3 = (s32[2,1]{0,1:T(1,128)S(1)}, s32[2,1]{0,1:T(1,128)}, u32[]{:S(2)}) copy-start(s32[2,1]{0,1:T(1,128)} %param.5) | copy-start | bytes 28
  1.7 11.8 %copy-start.1 = (f32[2,1,256,256]{3,2,1,0:T(8,128)S(1)}, f32[2,1,256,256]{3,2,1,0:T(8,128)}, u32[]{:S(2)}) copy-start(f32[2,1,256,256]{3,2,1,0:T(8,128)} %refs_1_.1) | copy-start | bytes 1572868
  2.0 8.3 %collective-permute-start = (f32[168,256]{1,0:T(8,128)S(1)}, f32[168,256]{1,0:T(8,128)S(1)}, u32[]{:S(2)}, u32[]{:S(2)}) collective-permute-start(f32[168,256]{1,0:T(8,128)S(1)} %get-tuple-element.20), channel_id=1, source_target_pairs={{0,4},{4,0},{8,12},{12,8},{16,20},{20,16},{24,28},{28,24},{1,5},{5... | collective-permute-start | bytes 516104 | tf_op jit(solution)/shard_map/ppermute | solution.py:299
  5.1 7.4 %collective-permute-start.1 = (f32[88,256]{1,0:T(8,128)S(1)}, f32[88,256]{1,0:T(8,128)S(1)}, u32[]{:S(2)}, u32[]{:S(2)}) collective-permute-start(f32[88,256]{1,0:T(8,128)S(1)} %get-tuple-element.22), channel_id=1, source_target_pairs={{0,4},{4,0},{8,12},{12,8},{16,20},{20,16},{24,28},{28,24},{1,5},{5... | collective-permute-start | bytes 270344 | tf_op jit(solution)/shard_map/ppermute | solution.py:299
  10.5 5.8 %collective-permute-start.2 = (f32[168,256]{1,0:T(8,128)S(1)}, f32[168,256]{1,0:T(8,128)S(1)}, u32[]{:S(2)}, u32[]{:S(2)}) collective-permute-start(f32[168,256]{1,0:T(8,128)S(1)} %shard_map.52.refs_0_.refs_1_), channel_id=1, source_target_pairs={{0,8},{4,12},{8,0},{12,4},{16,24},{20,28},{24,16},{28,20},{1,9},{5... | collective-permute-start | bytes 516104 | tf_op jit(solution)/shard_map/ppermute | solution.py:299
  12.7 4.6 %collective-permute-start.3 = (f32[88,256]{1,0:T(8,128)S(1)}, f32[88,256]{1,0:T(8,128)S(1)}, u32[]{:S(2)}, u32[]{:S(2)}) collective-permute-start(f32[88,256]{1,0:T(8,128)S(1)} %shard_map.53.refs_1_.refs_2_), channel_id=1, source_target_pairs={{0,8},{4,12},{8,0},{12,4},{16,24},{20,28},{24,16},{28,20},{1,9},{5... | collective-permute-start | bytes 270344 | tf_op jit(solution)/shard_map/ppermute | solution.py:299
  16.4 9.1 %copy-start.2 = (f32[2,3,1,256,256]{4,3,2,1,0:T(8,128)S(1)}, f32[2,3,1,256,256]{4,3,2,1,0:T(8,128)}, u32[]{:S(2)}) copy-start(f32[2,3,1,256,256]{4,3,2,1,0:T(8,128)} %hamiltonian.1) | copy-start | bytes 4718596
  17.7 6.2 %collective-permute-start.4 = (f32[64,256]{1,0:T(8,128)S(1)}, f32[64,256]{1,0:T(8,128)S(1)}, u32[]{:S(2)}, u32[]{:S(2)}) collective-permute-start(f32[64,256]{1,0:T(8,128)S(1)} %get-tuple-element.25), channel_id=1, source_target_pairs={{0,24},{4,28},{8,16},{12,20},{16,8},{20,12},{24,0},{28,4},{1,25},{... | collective-permute-start | bytes 196616 | tf_op jit(solution)/shard_map/ppermute | solution.py:299
  21.3 6.9 %collective-permute-start.6 = (f32[128,256]{1,0:T(8,128)S(1)}, f32[128,256]{1,0:T(8,128)S(1)}, u32[]{:S(2)}, u32[]{:S(2)}) collective-permute-start(f32[128,256]{1,0:T(8,128)S(1)} %get-tuple-element.31), channel_id=1, source_target_pairs={{0,16},{4,20},{8,24},{12,28},{16,0},{20,4},{24,8},{28,12},{1,17},{... | collective-permute-start | bytes 393224 | tf_op jit(solution)/shard_map/ppermute | solution.py:299
  24.0 4.3 %collective-permute-start.5 = (f32[64,256]{1,0:T(8,128)S(1)}, f32[64,256]{1,0:T(8,128)S(1)}, u32[]{:S(2)}, u32[]{:S(2)}) collective-permute-start(f32[64,256]{1,0:T(8,128)S(1)} %collective-permute-done.4.share), channel_id=1, source_target_pairs={{0,4},{4,0},{8,12},{12,8},{16,20},{20,16},{24,28},{28,24},{1,5},{5... | collective-permute-start | bytes 196616 | tf_op jit(solution)/shard_map/ppermute | solution.py:299
  28.7 3.1 %collective-permute-start.7 = (f32[8,128]{1,0:T(8,128)S(1)}, f32[8,128]{1,0:T(8,128)S(1)}, u32[]{:S(2)}, u32[]{:S(2)}) collective-permute-start(f32[8,128]{1,0:T(8,128)S(1)} %get-tuple-element.37.refs_0_), channel_id=1, source_target_pairs={{0,3},{1,2},{2,1},{3,0},{4,7},{5,6},{6,5},{7,4},{8,11},{9,10},{10,... | collective-permute-start | bytes 12296 | tf_op jit(solution)/shard_map/ppermute | solution.py:352
  28.7 3.7 %collective-permute-start.8 = (f32[8,128]{1,0:T(8,128)S(1)}, f32[8,128]{1,0:T(8,128)S(1)}, u32[]{:S(2)}, u32[]{:S(2)}) collective-permute-start(f32[8,128]{1,0:T(8,128)S(1)} %get-tuple-element.37.refs_0_), channel_id=1, source_target_pairs={{0,2},{1,3},{2,0},{3,1},{4,6},{5,7},{6,4},{7,5},{8,10},{9,11},{10,... | collective-permute-start | bytes 12296 | tf_op jit(solution)/shard_map/ppermute | solution.py:352
  30.3 2.2 %collective-permute-start.9 = (f32[8,128]{1,0:T(8,128)S(1)}, f32[8,128]{1,0:T(8,128)S(1)}, u32[]{:S(2)}, u32[]{:S(2)}) collective-permute-start(f32[8,128]{1,0:T(8,128)S(1)} %get-tuple-element.37.refs_0_), channel_id=1, source_target_pairs={{0,1},{1,0},{2,3},{3,2},{4,5},{5,4},{6,7},{7,6},{8,9},{9,8},{10,11... | collective-permute-start | bytes 12296 | tf_op jit(solution)/shard_map/ppermute | solution.py:352

commit v8 on v7

--- a/solution.py
+++ b/solution.py
@@ -312,7 +312,7 @@
     left, right = call(lambda *refs: near_kernel(n, *refs), (both, both), 2 * one, kept, transfer, *nears)
     fars[0], left = lax.optimization_barrier((fars[0], left))
     begun = call(lambda *refs: begin_kernel(n, *refs), matrix, one, *pairs, *fars[:-1])
-    rows = width // 4
+    rows = width * 7 // 256 * 8
     shared = (matrix, array(rows, width), array(width - 2 * rows, width))
     if total <= 8:
         sent, share, rest = call(

time: 33.2 us -> 33.1 us (level)
  transfers between devices with their start and end apart: 10 -> 10, of which waited for: 7 -> 7; matrix products, arithmetic and copies ran while one was open for 0% -> 0% of each run, Pallas kernels for 15% -> 16%
where the time goes in v8:
time: 33.1 us; the launch traced here: 32.9 us
  starting transfers between devices  12.9 us (39%)
  waiting for transfers between devices  11.3 us (34%)
  Pallas kernels  6.88 us (21%)
  local copies, waits for them, and re-layouts  1.14 us (3%)
  between operations  0.74 us (2%)
    ppermute x7, starting transfers between devices, swap(): return lax.ppermute(a, 'col', [(i, i ^ k) for i in range(total)])  10.9 us
    ppermute x7, waiting for transfers between devices, swap(): return lax.ppermute(a, 'col', [(i, i ^ k) for i in range(total)])  10.3 us
    pallas_call x12, Pallas kernels, call(): pl.pallas_call(kernel, out_shape=outs, in_specs=[VMEM] * len(args), out_s...  6.88 us
    ppermute x3, starting transfers between devices, per_device(): lax.ppermute(table, 'sec', [(i, i ^ k) for i in range(sectors)])  1.92 us
    unnamed x9, local copies, waits for them, and re-layouts  1.14 us
    ppermute x3, waiting for transfers between devices, per_device(): lax.ppermute(table, 'sec', [(i, i ^ k) for i in range(sectors)])  1 us
  transfers between devices with their start and end apart: 10, of which 7 were waited for; matrix products, arithmetic and copies ran while one was open for 0% of the time, Pallas kernels for 16%

profile of v8, /device:TPU:0, one launch (start us, length us, event | category | flops | bytes accessed | tf_op | source)
XLA Modules:
  0.0 32.9 jit_solution(15113061265870157276)
XLA Ops:
  0.6 0.0 copy-start
  0.6 1.0 %copy-done = f32[2,1,256,256]{3,2,1,0:T(8,128)S(1)} copy-done((f32[2,1,256,256]{3,2,1,0:T(8,128)S(1)}, f32[2,1,256,256]{3,2,1,0:T(8,128)}, u32[]{:S(2)}) %copy-start) | copy-done | bytes 524312
  1.7 0.0 copy-start.3
  1.7 0.0 copy-start.1
  1.7 0.3 shard_map.50
  2.0 3.1 %collective-permute-start = (f32[168,256]{1,0:T(8,128)S(1)}, f32[168,256]{1,0:T(8,128)S(1)}, u32[]{:S(2)}, u32[]{:S(2)}) collective-permute-start(f32[168,256]{1,0:T(8,128)S(1)} %get-tuple-element.20), channel_id=1, source_target_pairs={{0,4},{4,0},{8,12},{12,8},{16,20},{20,16},{24,28},{28,24},{1,5},{5... | collective-permute-start | bytes 516104 | tf_op jit(solution)/shard_map/ppermute | solution.py:299
  5.1 0.1 collective-permute-start.1
  5.2 0.1 shard_map.51.turned
  5.3 5.0 %collective-permute-done.near.refs_2_ = f32[168,256]{1,0:T(8,128)S(1)} collective-permute-done((f32[168,256]{1,0:T(8,128)S(1)}, f32[168,256]{1,0:T(8,128)S(1)}, u32[]{:S(2)}, u32[]{:S(2)}) %collective-permute-start) | collective-permute-done | bytes 172064 | tf_op jit(solution)/shard_map/ppermute | solution.py:299
  10.3 0.2 shard_map.52.refs_0_.refs_1_
  10.5 1.9 %collective-permute-start.2 = (f32[168,256]{1,0:T(8,128)S(1)}, f32[168,256]{1,0:T(8,128)S(1)}, u32[]{:S(2)}, u32[]{:S(2)}) collective-permute-start(f32[168,256]{1,0:T(8,128)S(1)} %shard_map.52.refs_0_.refs_1_), channel_id=1, source_target_pairs={{0,8},{4,12},{8,0},{12,4},{16,24},{20,28},{24,16},{28,20},{1,9},{5... | collective-permute-start | bytes 516104 | tf_op jit(solution)/shard_map/ppermute | solution.py:299
  12.5 0.0 collective-permute-done.1.near.refs_3_
  12.5 0.2 shard_map.53.refs_1_.refs_2_
  12.7 0.7 %collective-permute-start.3 = (f32[88,256]{1,0:T(8,128)S(1)}, f32[88,256]{1,0:T(8,128)S(1)}, u32[]{:S(2)}, u32[]{:S(2)}) collective-permute-start(f32[88,256]{1,0:T(8,128)S(1)} %shard_map.53.refs_1_.refs_2_), channel_id=1, source_target_pairs={{0,8},{4,12},{8,0},{12,4},{16,24},{20,28},{24,16},{28,20},{1,9},{5... | collective-permute-start | bytes 270344 | tf_op jit(solution)/shard_map/ppermute | solution.py:299
  13.4 0.0 copy-done.3
  13.4 0.1 copy.5.refs_0_
  13.5 0.0 copy-done.1
  13.5 0.5 %shard_map.54 = (f32[2,256,256]{2,1,0:T(8,128)S(1)}, f32[2,256,256]{2,1,0:T(8,128)S(1)}) custom-call(s32[2,1]{1,0:T(2,128)S(1)} %copy.5.refs_0_, f32[2,1,256,256]{3,2,1,0:T(8,128)S(1)} %copy-done.1, f32[168,256]{1,0:T(8,128)S(1)} %collective-permute-done.near.refs_2_, f32[88,256]{1,0:T(8,128)S(1)} %collective-permute-done.1.near.refs_3_), custom_call_target="tpu_custom_call" | custom-call | flops 201326592 | bytes 1048576 | tf_op jit(solution)/shard_map/pallas_call | solution.py:275
  14.0 2.4 %collective-permute-done.2.refs_2_.refs_3_ = f32[168,256]{1,0:T(8,128)S(1)} collective-permute-done((f32[168,256]{1,0:T(8,128)S(1)}, f32[168,256]{1,0:T(8,128)S(1)}, u32[]{:S(2)}, u32[]{:S(2)}) %collective-permute-start.2) | collective-permute-done | bytes 172064 | tf_op jit(solution)/shard_map/ppermute | solution.py:299
  16.4 0.0 copy-start.2
  16.4 0.3 shard_map.55.refs_0_
  16.6 0.7 %collective-permute-done.3.refs_3_.refs_4_ = f32[88,256]{1,0:T(8,128)S(1)} collective-permute-done((f32[88,256]{1,0:T(8,128)S(1)}, f32[88,256]{1,0:T(8,128)S(1)}, u32[]{:S(2)}, u32[]{:S(2)}) %collective-permute-start.3) | collective-permute-done | bytes 90144 | tf_op jit(solution)/shard_map/ppermute | solution.py:299
  17.3 0.4 %shard_map.56 = (f32[256,256]{1,0:T(8,128)S(1)}, f32[56,256]{1,0:T(8,128)S(1)}, f32[144,256]{1,0:T(8,128)S(1)}) custom-call(f32[256,256]{1,0:T(8,128)S(1)} %shard_map.55.refs_0_, f32[168,256]{1,0:T(8,128)S(1)} %shard_map.52.refs_0_.refs_1_, f32[88,256]{1,0:T(8,128)S(1)} %shard_map.53.refs_1_.refs_2_, f32[88,256]{1,0:T(8,128)S(1)} %collective-permute-done.3.refs_3_.refs_4_), custom_call_target="tpu_custom_call" | custom-call | flops 100663296 | bytes 1048576 | tf_op jit(solution)/shard_map/pallas_call | solution.py:275
  17.7 3.6 %collective-permute-start.4 = (f32[56,256]{1,0:T(8,128)S(1)}, f32[56,256]{1,0:T(8,128)S(1)}, u32[]{:S(2)}, u32[]{:S(2)}) collective-permute-start(f32[56,256]{1,0:T(8,128)S(1)} %get-tuple-element.25), channel_id=1, source_target_pairs={{0,24},{4,28},{8,16},{12,20},{16,8},{20,12},{24,0},{28,4},{1,25},{... | collective-permute-start | bytes 172040 | tf_op jit(solution)/shard_map/ppermute | solution.py:299
  21.3 0.0 collective-permute-start.6
  21.3 1.3 %shard_map.57 = (f32[2,256,256]{2,1,0:T(8,128)S(1)}, f32[256,256]{1,0:T(8,128)S(1)}, bf16[2,2,256,256]{3,2,1,0:T(8,128)(2,1)S(1)}, bf16[2,2,256,256]{3,2,1,0:T(8,128)(2,1)S(1)}) custom-call(f32[256,256]{1,0:T(8,128)S(1)} %get-tuple-element.26.refs_0_, f32[2,256,256]{2,1,0:T(8,128)S(1)} %get-tuple-element.27.refs_1_, ...), custom_call_target="tpu_custom_call" | custom-call | flops 503316480 | bytes 1048576 | tf_op jit(solution)/shard_map/pallas_call | solution.py:275
  22.7 1.2 %collective-permute-done.4.share = f32[56,256]{1,0:T(8,128)S(1)} collective-permute-done((f32[56,256]{1,0:T(8,128)S(1)}, f32[56,256]{1,0:T(8,128)S(1)}, u32[]{:S(2)}, u32[]{:S(2)}) %collective-permute-start.4) | collective-permute-done | bytes 57376 | tf_op jit(solution)/shard_map/ppermute | solution.py:299
  23.9 1.5 %collective-permute-start.5 = (f32[56,256]{1,0:T(8,128)S(1)}, f32[56,256]{1,0:T(8,128)S(1)}, u32[]{:S(2)}, u32[]{:S(2)}) collective-permute-start(f32[56,256]{1,0:T(8,128)S(1)} %collective-permute-done.4.share), channel_id=1, source_target_pairs={{0,4},{4,0},{8,12},{12,8},{16,20},{20,16},{24,28},{28,24},{1,5},{5... | collective-permute-start | bytes 172040 | tf_op jit(solution)/shard_map/ppermute | solution.py:299
  25.4 0.0 copy-done.2
  25.4 1.6 %shard_map.58.terms = f32[2,3,256,256]{3,2,1,0:T(8,128)S(1)} custom-call(bf16[2,2,256,256]{3,2,1,0:T(8,128)(2,1)S(1)} %get-tuple-element.32.a, bf16[2,2,256,256]{3,2,1,0:T(8,128)(2,1)S(1)} %get-tuple-element.33.b, f32[2,3,1,256,256]{4,3,2,1,0:T(8,128)S(1)} %copy-done.2), custom_call_target="tpu_custom_call" | custom-call | flops 1207959552 | bytes 1048576 | tf_op jit(solution)/shard_map/pallas_call | solution.py:275
  27.0 1.0 %collective-permute-done.5.passed = f32[56,256]{1,0:T(8,128)S(1)} collective-permute-done((f32[56,256]{1,0:T(8,128)S(1)}, f32[56,256]{1,0:T(8,128)S(1)}, u32[]{:S(2)}, u32[]{:S(2)}) %collective-permute-start.5) | collective-permute-done | bytes 57376 | tf_op jit(solution)/shard_map/ppermute | solution.py:299
  28.1 0.0 collective-permute-done.6.rest
  28.1 0.4 %shard_map.59 = (f32[8,128]{1,0:T(8,128)S(1)}, f32[256,256]{1,0:T(8,128)S(1)}) custom-call(f32[56,256]{1,0:T(8,128)S(1)} %collective-permute-done.4.share, f32[56,256]{1,0:T(8,128)S(1)} %collective-permute-done.5.passed, f32[144,256]{1,0:T(8,128)S(1)} %collective-permute-done.6.rest, f32[2,3,256,256]{3,2,1,0:T(8,128)S(1)} %shard_map.58.terms, ...), custom_call_target="tpu_custom_call" | custom-call | flops 201326592 | bytes 1048576 | tf_op jit(solution)/shard_map/pallas_call | solution.py:275
  28.5 0.1 collective-permute-start.7
  28.6 1.6 %collective-permute-start.8 = (f32[8,128]{1,0:T(8,128)S(1)}, f32[8,128]{1,0:T(8,128)S(1)}, u32[]{:S(2)}, u32[]{:S(2)}) collective-permute-start(f32[8,128]{1,0:T(8,128)S(1)} %get-tuple-element.37.refs_0_), channel_id=1, source_target_pairs={{0,2},{1,3},{2,0},{3,1},{4,6},{5,7},{6,4},{7,5},{8,10},{9,11},{10,... | collective-permute-start | bytes 12296 | tf_op jit(solution)/shard_map/ppermute | solution.py:352
  30.2 0.2 collective-permute-start.9
  30.4 0.8 %shard_map.60 = f32[2,1,256,256]{3,2,1,0:T(8,128)} custom-call(f32[256,256]{1,0:T(8,128)S(1)} %get-tuple-element.35.refs_0_, f32[2,256,256]{2,1,0:T(8,128)S(1)} %get-tuple-element.36.refs_1_), custom_call_target="tpu_custom_call" | custom-call | flops 201326592 | bytes 1048576 | tf_op jit(solution)/shard_map/pallas_call | solution.py:275
  31.2 0.3 %collective-permute-done.7.refs_1_ = f32[8,128]{1,0:T(8,128)S(1)} collective-permute-done((f32[8,128]{1,0:T(8,128)S(1)}, f32[8,128]{1,0:T(8,128)S(1)}, u32[]{:S(2)}, u32[]{:S(2)}) %collective-permute-start.7) | collective-permute-done | bytes 4128 | tf_op jit(solution)/shard_map/ppermute | solution.py:352
  31.6 0.7 %collective-permute-done.8.refs_2_ = f32[8,128]{1,0:T(8,128)S(1)} collective-permute-done((f32[8,128]{1,0:T(8,128)S(1)}, f32[8,128]{1,0:T(8,128)S(1)}, u32[]{:S(2)}, u32[]{:S(2)}) %collective-permute-start.8) | collective-permute-done | bytes 4128 | tf_op jit(solution)/shard_map/ppermute | solution.py:352
  32.2 0.0 collective-permute-done.9.refs_3_
  32.2 0.7 %shard_map.61 = f32[2,3]{1,0:T(2,128)} custom-call(f32[8,128]{1,0:T(8,128)S(1)} %get-tuple-element.37.refs_0_, f32[8,128]{1,0:T(8,128)S(1)} %collective-permute-done.7.refs_1_, f32[8,128]{1,0:T(8,128)S(1)} %collective-permute-done.8.refs_2_, f32[8,128]{1,0:T(8,128)S(1)} %collective-permute-done.9.refs_3_), custom_call_target="tpu_custom_call" | custom-call | flops 1000 | bytes 1048576 | tf_op jit(solution)/shard_map/pallas_call | solution.py:275
Async XLA Ops:
  0.6 1.0 %copy-start = (f32[2,1,256,256]{3,2,1,0:T(8,128)S(1)}, f32[2,1,256,256]{3,2,1,0:T(8,128)}, u32[]{:S(2)}) copy-start(f32[2,1,256,256]{3,2,1,0:T(8,128)} %refs_1_.1) | copy-start | bytes 1572868
  1.7 11.7 %copy-start.3 = (s32[2,1]{0,1:T(1,128)S(1)}, s32[2,1]{0,1:T(1,128)}, u32[]{:S(2)}) copy-start(s32[2,1]{0,1:T(1,128)} %param.5) | copy-start | bytes 28
  1.7 11.8 %copy-start.1 = (f32[2,1,256,256]{3,2,1,0:T(8,128)S(1)}, f32[2,1,256,256]{3,2,1,0:T(8,128)}, u32[]{:S(2)}) copy-start(f32[2,1,256,256]{3,2,1,0:T(8,128)} %refs_1_.1) | copy-start | bytes 1572868
  2.0 8.3 %collective-permute-start = (f32[168,256]{1,0:T(8,128)S(1)}, f32[168,256]{1,0:T(8,128)S(1)}, u32[]{:S(2)}, u32[]{:S(2)}) collective-permute-start(f32[168,256]{1,0:T(8,128)S(1)} %get-tuple-element.20), channel_id=1, source_target_pairs={{0,4},{4,0},{8,12},{12,8},{16,20},{20,16},{24,28},{28,24},{1,5},{5... | collective-permute-start | bytes 516104 | tf_op jit(solution)/shard_map/ppermute | solution.py:299
  5.1 7.4 %collective-permute-start.1 = (f32[88,256]{1,0:T(8,128)S(1)}, f32[88,256]{1,0:T(8,128)S(1)}, u32[]{:S(2)}, u32[]{:S(2)}) collective-permute-start(f32[88,256]{1,0:T(8,128)S(1)} %get-tuple-element.22), channel_id=1, source_target_pairs={{0,4},{4,0},{8,12},{12,8},{16,20},{20,16},{24,28},{28,24},{1,5},{5... | collective-permute-start | bytes 270344 | tf_op jit(solution)/shard_map/ppermute | solution.py:299
  10.5 5.8 %collective-permute-start.2 = (f32[168,256]{1,0:T(8,128)S(1)}, f32[168,256]{1,0:T(8,128)S(1)}, u32[]{:S(2)}, u32[]{:S(2)}) collective-permute-start(f32[168,256]{1,0:T(8,128)S(1)} %shard_map.52.refs_0_.refs_1_), channel_id=1, source_target_pairs={{0,8},{4,12},{8,0},{12,4},{16,24},{20,28},{24,16},{28,20},{1,9},{5... | collective-permute-start | bytes 516104 | tf_op jit(solution)/shard_map/ppermute | solution.py:299
  12.7 4.6 %collective-permute-start.3 = (f32[88,256]{1,0:T(8,128)S(1)}, f32[88,256]{1,0:T(8,128)S(1)}, u32[]{:S(2)}, u32[]{:S(2)}) collective-permute-start(f32[88,256]{1,0:T(8,128)S(1)} %shard_map.53.refs_1_.refs_2_), channel_id=1, source_target_pairs={{0,8},{4,12},{8,0},{12,4},{16,24},{20,28},{24,16},{28,20},{1,9},{5... | collective-permute-start | bytes 270344 | tf_op jit(solution)/shard_map/ppermute | solution.py:299
  16.4 9.0 %copy-start.2 = (f32[2,3,1,256,256]{4,3,2,1,0:T(8,128)S(1)}, f32[2,3,1,256,256]{4,3,2,1,0:T(8,128)}, u32[]{:S(2)}) copy-start(f32[2,3,1,256,256]{4,3,2,1,0:T(8,128)} %hamiltonian.1) | copy-start | bytes 4718596
  17.7 6.1 %collective-permute-start.4 = (f32[56,256]{1,0:T(8,128)S(1)}, f32[56,256]{1,0:T(8,128)S(1)}, u32[]{:S(2)}, u32[]{:S(2)}) collective-permute-start(f32[56,256]{1,0:T(8,128)S(1)} %get-tuple-element.25), channel_id=1, source_target_pairs={{0,24},{4,28},{8,16},{12,20},{16,8},{20,12},{24,0},{28,4},{1,25},{... | collective-permute-start | bytes 172040 | tf_op jit(solution)/shard_map/ppermute | solution.py:299
  21.3 6.7 %collective-permute-start.6 = (f32[144,256]{1,0:T(8,128)S(1)}, f32[144,256]{1,0:T(8,128)S(1)}, u32[]{:S(2)}, u32[]{:S(2)}) collective-permute-start(f32[144,256]{1,0:T(8,128)S(1)} %get-tuple-element.31), channel_id=1, source_target_pairs={{0,16},{4,20},{8,24},{12,28},{16,0},{20,4},{24,8},{28,12},{1,17},{... | collective-permute-start | bytes 442376 | tf_op jit(solution)/shard_map/ppermute | solution.py:299
  23.9 4.2 %collective-permute-start.5 = (f32[56,256]{1,0:T(8,128)S(1)}, f32[56,256]{1,0:T(8,128)S(1)}, u32[]{:S(2)}, u32[]{:S(2)}) collective-permute-start(f32[56,256]{1,0:T(8,128)S(1)} %collective-permute-done.4.share), channel_id=1, source_target_pairs={{0,4},{4,0},{8,12},{12,8},{16,20},{20,16},{24,28},{28,24},{1,5},{5... | collective-permute-start | bytes 172040 | tf_op jit(solution)/shard_map/ppermute | solution.py:299
  28.5 3.1 %collective-permute-start.7 = (f32[8,128]{1,0:T(8,128)S(1)}, f32[8,128]{1,0:T(8,128)S(1)}, u32[]{:S(2)}, u32[]{:S(2)}) collective-permute-start(f32[8,128]{1,0:T(8,128)S(1)} %get-tuple-element.37.refs_0_), channel_id=1, source_target_pairs={{0,3},{1,2},{2,1},{3,0},{4,7},{5,6},{6,5},{7,4},{8,11},{9,10},{10,... | collective-permute-start | bytes 12296 | tf_op jit(solution)/shard_map/ppermute | solution.py:352
  28.6 3.7 %collective-permute-start.8 = (f32[8,128]{1,0:T(8,128)S(1)}, f32[8,128]{1,0:T(8,128)S(1)}, u32[]{:S(2)}, u32[]{:S(2)}) collective-permute-start(f32[8,128]{1,0:T(8,128)S(1)} %get-tuple-element.37.refs_0_), channel_id=1, source_target_pairs={{0,2},{1,3},{2,0},{3,1},{4,6},{5,7},{6,4},{7,5},{8,10},{9,11},{10,... | collective-permute-start | bytes 12296 | tf_op jit(solution)/shard_map/ppermute | solution.py:352
  30.2 2.1 %collective-permute-start.9 = (f32[8,128]{1,0:T(8,128)S(1)}, f32[8,128]{1,0:T(8,128)S(1)}, u32[]{:S(2)}, u32[]{:S(2)}) collective-permute-start(f32[8,128]{1,0:T(8,128)S(1)} %get-tuple-element.37.refs_0_), channel_id=1, source_target_pairs={{0,1},{1,0},{2,3},{3,2},{4,5},{5,4},{6,7},{7,6},{8,9},{9,8},{10,11... | collective-permute-start | bytes 12296 | tf_op jit(solution)/shard_map/ppermute | solution.py:352

commit v9 on v8

--- a/solution.py
+++ b/solution.py
@@ -342,7 +342,6 @@
         lefts, norm, a, b = call(
             lambda *refs: prepare_kernel(half, *refs), prepared, 3 * one, sent, left, right
         )
-    share, norm = lax.optimization_barrier((share, norm))
     passed = swap(share, 1)
     products = call(terms_kernel, array(columns, terms, width, width), 12 * one, a, b, hamiltonian)
     table_rows = -(-(columns * terms + 1) // 8) * 8

time: 33.1 us -> 33.1 us (level)
  no operation moved by 1% of the time
where the time goes in v9:
time: 33.1 us; the launch traced here: 32.9 us
  starting transfers between devices  12.9 us (39%)
  waiting for transfers between devices  11.3 us (34%)
  Pallas kernels  6.88 us (21%)
  local copies, waits for them, and re-layouts  1.14 us (3%)
  between operations  0.74 us (2%)
    ppermute x7, starting transfers between devices, swap(): return lax.ppermute(a, 'col', [(i, i ^ k) for i in range(total)])  10.9 us
    ppermute x7, waiting for transfers between devices, swap(): return lax.ppermute(a, 'col', [(i, i ^ k) for i in range(total)])  10.3 us
    pallas_call x12, Pallas kernels, call(): pl.pallas_call(kernel, out_shape=outs, in_specs=[VMEM] * len(args), out_s...  6.88 us
    ppermute x3, starting transfers between devices, per_device(): lax.ppermute(table, 'sec', [(i, i ^ k) for i in range(sectors)])  1.92 us
    unnamed x9, local copies, waits for them, and re-layouts  1.14 us
    ppermute x3, waiting for transfers between devices, per_device(): lax.ppermute(table, 'sec', [(i, i ^ k) for i in range(sectors)])  1 us
  transfers between devices with their start and end apart: 10, of which 7 were waited for; matrix products, arithmetic and copies ran while one was open for 0% of the time, Pallas kernels for 16%

profile of v9, /device:TPU:0, one launch (start us, length us, event | category | flops | bytes accessed | tf_op | source)
XLA Modules:
  0.0 32.9 jit_solution(15113061265870157276)
XLA Ops:
  0.6 0.0 copy-start
  0.6 1.0 %copy-done = f32[2,1,256,256]{3,2,1,0:T(8,128)S(1)} copy-done((f32[2,1,256,256]{3,2,1,0:T(8,128)S(1)}, f32[2,1,256,256]{3,2,1,0:T(8,128)}, u32[]{:S(2)}) %copy-start) | copy-done | bytes 524312
  1.7 0.0 copy-start.3
  1.7 0.0 copy-start.1
  1.7 0.3 shard_map.50
  2.0 3.1 %collective-permute-start = (f32[168,256]{1,0:T(8,128)S(1)}, f32[168,256]{1,0:T(8,128)S(1)}, u32[]{:S(2)}, u32[]{:S(2)}) collective-permute-start(f32[168,256]{1,0:T(8,128)S(1)} %get-tuple-element.18), channel_id=1, source_target_pairs={{0,4},{4,0},{8,12},{12,8},{16,20},{20,16},{24,28},{28,24},{1,5},{5... | collective-permute-start | bytes 516104 | tf_op jit(solution)/shard_map/ppermute | solution.py:299
  5.1 0.1 collective-permute-start.1
  5.2 0.1 shard_map.51.turned
  5.3 5.0 %collective-permute-done.near.refs_2_ = f32[168,256]{1,0:T(8,128)S(1)} collective-permute-done((f32[168,256]{1,0:T(8,128)S(1)}, f32[168,256]{1,0:T(8,128)S(1)}, u32[]{:S(2)}, u32[]{:S(2)}) %collective-permute-start) | collective-permute-done | bytes 172064 | tf_op jit(solution)/shard_map/ppermute | solution.py:299
  10.3 0.2 shard_map.52.refs_0_.refs_1_
  10.5 1.9 %collective-permute-start.2 = (f32[168,256]{1,0:T(8,128)S(1)}, f32[168,256]{1,0:T(8,128)S(1)}, u32[]{:S(2)}, u32[]{:S(2)}) collective-permute-start(f32[168,256]{1,0:T(8,128)S(1)} %shard_map.52.refs_0_.refs_1_), channel_id=1, source_target_pairs={{0,8},{4,12},{8,0},{12,4},{16,24},{20,28},{24,16},{28,20},{1,9},{5... | collective-permute-start | bytes 516104 | tf_op jit(solution)/shard_map/ppermute | solution.py:299
  12.5 0.0 collective-permute-done.1.near.refs_3_
  12.5 0.2 shard_map.53.refs_1_.refs_2_
  12.7 0.7 %collective-permute-start.3 = (f32[88,256]{1,0:T(8,128)S(1)}, f32[88,256]{1,0:T(8,128)S(1)}, u32[]{:S(2)}, u32[]{:S(2)}) collective-permute-start(f32[88,256]{1,0:T(8,128)S(1)} %shard_map.53.refs_1_.refs_2_), channel_id=1, source_target_pairs={{0,8},{4,12},{8,0},{12,4},{16,24},{20,28},{24,16},{28,20},{1,9},{5... | collective-permute-start | bytes 270344 | tf_op jit(solution)/shard_map/ppermute | solution.py:299
  13.4 0.0 copy-done.3
  13.4 0.1 copy.5.refs_0_
  13.5 0.0 copy-done.1
  13.5 0.5 %shard_map.54 = (f32[2,256,256]{2,1,0:T(8,128)S(1)}, f32[2,256,256]{2,1,0:T(8,128)S(1)}) custom-call(s32[2,1]{1,0:T(2,128)S(1)} %copy.5.refs_0_, f32[2,1,256,256]{3,2,1,0:T(8,128)S(1)} %copy-done.1, f32[168,256]{1,0:T(8,128)S(1)} %collective-permute-done.near.refs_2_, f32[88,256]{1,0:T(8,128)S(1)} %collective-permute-done.1.near.refs_3_), custom_call_target="tpu_custom_call" | custom-call | flops 201326592 | bytes 1048576 | tf_op jit(solution)/shard_map/pallas_call | solution.py:275
  14.0 2.4 %collective-permute-done.2.refs_2_.refs_3_ = f32[168,256]{1,0:T(8,128)S(1)} collective-permute-done((f32[168,256]{1,0:T(8,128)S(1)}, f32[168,256]{1,0:T(8,128)S(1)}, u32[]{:S(2)}, u32[]{:S(2)}) %collective-permute-start.2) | collective-permute-done | bytes 172064 | tf_op jit(solution)/shard_map/ppermute | solution.py:299
  16.4 0.0 copy-start.2
  16.4 0.3 shard_map.55.refs_0_
  16.6 0.7 %collective-permute-done.3.refs_3_.refs_4_ = f32[88,256]{1,0:T(8,128)S(1)} collective-permute-done((f32[88,256]{1,0:T(8,128)S(1)}, f32[88,256]{1,0:T(8,128)S(1)}, u32[]{:S(2)}, u32[]{:S(2)}) %collective-permute-start.3) | collective-permute-done | bytes 90144 | tf_op jit(solution)/shard_map/ppermute | solution.py:299
  17.3 0.4 %shard_map.56 = (f32[256,256]{1,0:T(8,128)S(1)}, f32[56,256]{1,0:T(8,128)S(1)}, f32[144,256]{1,0:T(8,128)S(1)}) custom-call(f32[256,256]{1,0:T(8,128)S(1)} %shard_map.55.refs_0_, f32[168,256]{1,0:T(8,128)S(1)} %shard_map.52.refs_0_.refs_1_, f32[88,256]{1,0:T(8,128)S(1)} %shard_map.53.refs_1_.refs_2_, f32[88,256]{1,0:T(8,128)S(1)} %collective-permute-done.3.refs_3_.refs_4_), custom_call_target="tpu_custom_call" | custom-call | flops 100663296 | bytes 1048576 | tf_op jit(solution)/shard_map/pallas_call | solution.py:275
  17.7 3.6 %collective-permute-start.4 = (f32[56,256]{1,0:T(8,128)S(1)}, f32[56,256]{1,0:T(8,128)S(1)}, u32[]{:S(2)}, u32[]{:S(2)}) collective-permute-start(f32[56,256]{1,0:T(8,128)S(1)} %get-tuple-element.23), channel_id=1, source_target_pairs={{0,24},{4,28},{8,16},{12,20},{16,8},{20,12},{24,0},{28,4},{1,25},{... | collective-permute-start | bytes 172040 | tf_op jit(solution)/shard_map/ppermute | solution.py:299
  21.3 0.0 collective-permute-start.6
  21.3 1.3 %shard_map.57 = (f32[2,256,256]{2,1,0:T(8,128)S(1)}, f32[256,256]{1,0:T(8,128)S(1)}, bf16[2,2,256,256]{3,2,1,0:T(8,128)(2,1)S(1)}, bf16[2,2,256,256]{3,2,1,0:T(8,128)(2,1)S(1)}) custom-call(f32[256,256]{1,0:T(8,128)S(1)} %get-tuple-element.25.refs_0_, f32[2,256,256]{2,1,0:T(8,128)S(1)} %get-tuple-element.26.refs_1_, ...), custom_call_target="tpu_custom_call" | custom-call | flops 503316480 | bytes 1048576 | tf_op jit(solution)/shard_map/pallas_call | solution.py:275
  22.7 1.2 %collective-permute-done.4.share = f32[56,256]{1,0:T(8,128)S(1)} collective-permute-done((f32[56,256]{1,0:T(8,128)S(1)}, f32[56,256]{1,0:T(8,128)S(1)}, u32[]{:S(2)}, u32[]{:S(2)}) %collective-permute-start.4) | collective-permute-done | bytes 57376 | tf_op jit(solution)/shard_map/ppermute | solution.py:299
  23.9 1.5 %collective-permute-start.5 = (f32[56,256]{1,0:T(8,128)S(1)}, f32[56,256]{1,0:T(8,128)S(1)}, u32[]{:S(2)}, u32[]{:S(2)}) collective-permute-start(f32[56,256]{1,0:T(8,128)S(1)} %collective-permute-done.4.share), channel_id=1, source_target_pairs={{0,4},{4,0},{8,12},{12,8},{16,20},{20,16},{24,28},{28,24},{1,5},{5... | collective-permute-start | bytes 172040 | tf_op jit(solution)/shard_map/ppermute | solution.py:299
  25.4 0.0 copy-done.2
  25.4 1.6 %shard_map.58.terms = f32[2,3,256,256]{3,2,1,0:T(8,128)S(1)} custom-call(bf16[2,2,256,256]{3,2,1,0:T(8,128)(2,1)S(1)} %get-tuple-element.28.a, bf16[2,2,256,256]{3,2,1,0:T(8,128)(2,1)S(1)} %get-tuple-element.29.b, f32[2,3,1,256,256]{4,3,2,1,0:T(8,128)S(1)} %copy-done.2), custom_call_target="tpu_custom_call" | custom-call | flops 1207959552 | bytes 1048576 | tf_op jit(solution)/shard_map/pallas_call | solution.py:275
  27.0 1.0 %collective-permute-done.5.passed = f32[56,256]{1,0:T(8,128)S(1)} collective-permute-done((f32[56,256]{1,0:T(8,128)S(1)}, f32[56,256]{1,0:T(8,128)S(1)}, u32[]{:S(2)}, u32[]{:S(2)}) %collective-permute-start.5) | collective-permute-done | bytes 57376 | tf_op jit(solution)/shard_map/ppermute | solution.py:299
  28.1 0.0 collective-permute-done.6.rest
  28.1 0.4 %shard_map.59 = (f32[8,128]{1,0:T(8,128)S(1)}, f32[256,256]{1,0:T(8,128)S(1)}) custom-call(f32[56,256]{1,0:T(8,128)S(1)} %collective-permute-done.4.share, f32[56,256]{1,0:T(8,128)S(1)} %collective-permute-done.5.passed, f32[144,256]{1,0:T(8,128)S(1)} %collective-permute-done.6.rest, f32[2,3,256,256]{3,2,1,0:T(8,128)S(1)} %shard_map.58.terms, ...), custom_call_target="tpu_custom_call" | custom-call | flops 201326592 | bytes 1048576 | tf_op jit(solution)/shard_map/pallas_call | solution.py:275
  28.5 0.1 collective-permute-start.7
  28.6 1.6 %collective-permute-start.8 = (f32[8,128]{1,0:T(8,128)S(1)}, f32[8,128]{1,0:T(8,128)S(1)}, u32[]{:S(2)}, u32[]{:S(2)}) collective-permute-start(f32[8,128]{1,0:T(8,128)S(1)} %get-tuple-element.33.refs_0_), channel_id=1, source_target_pairs={{0,2},{1,3},{2,0},{3,1},{4,6},{5,7},{6,4},{7,5},{8,10},{9,11},{10,... | collective-permute-start | bytes 12296 | tf_op jit(solution)/shard_map/ppermute | solution.py:351
  30.2 0.2 collective-permute-start.9
  30.4 0.8 %shard_map.60 = f32[2,1,256,256]{3,2,1,0:T(8,128)} custom-call(f32[256,256]{1,0:T(8,128)S(1)} %get-tuple-element.31.refs_0_, f32[2,256,256]{2,1,0:T(8,128)S(1)} %get-tuple-element.32.refs_1_), custom_call_target="tpu_custom_call" | custom-call | flops 201326592 | bytes 1048576 | tf_op jit(solution)/shard_map/pallas_call | solution.py:275
  31.2 0.3 %collective-permute-done.7.refs_1_ = f32[8,128]{1,0:T(8,128)S(1)} collective-permute-done((f32[8,128]{1,0:T(8,128)S(1)}, f32[8,128]{1,0:T(8,128)S(1)}, u32[]{:S(2)}, u32[]{:S(2)}) %collective-permute-start.7) | collective-permute-done | bytes 4128 | tf_op jit(solution)/shard_map/ppermute | solution.py:351
  31.6 0.7 %collective-permute-done.8.refs_2_ = f32[8,128]{1,0:T(8,128)S(1)} collective-permute-done((f32[8,128]{1,0:T(8,128)S(1)}, f32[8,128]{1,0:T(8,128)S(1)}, u32[]{:S(2)}, u32[]{:S(2)}) %collective-permute-start.8) | collective-permute-done | bytes 4128 | tf_op jit(solution)/shard_map/ppermute | solution.py:351
  32.2 0.0 collective-permute-done.9.refs_3_
  32.2 0.7 %shard_map.61 = f32[2,3]{1,0:T(2,128)} custom-call(f32[8,128]{1,0:T(8,128)S(1)} %get-tuple-element.33.refs_0_, f32[8,128]{1,0:T(8,128)S(1)} %collective-permute-done.7.refs_1_, f32[8,128]{1,0:T(8,128)S(1)} %collective-permute-done.8.refs_2_, f32[8,128]{1,0:T(8,128)S(1)} %collective-permute-done.9.refs_3_), custom_call_target="tpu_custom_call" | custom-call | flops 1000 | bytes 1048576 | tf_op jit(solution)/shard_map/pallas_call | solution.py:275
Async XLA Ops:
  0.6 1.0 %copy-start = (f32[2,1,256,256]{3,2,1,0:T(8,128)S(1)}, f32[2,1,256,256]{3,2,1,0:T(8,128)}, u32[]{:S(2)}) copy-start(f32[2,1,256,256]{3,2,1,0:T(8,128)} %refs_1_.1) | copy-start | bytes 1572868
  1.7 11.7 %copy-start.3 = (s32[2,1]{0,1:T(1,128)S(1)}, s32[2,1]{0,1:T(1,128)}, u32[]{:S(2)}) copy-start(s32[2,1]{0,1:T(1,128)} %param.5) | copy-start | bytes 28
  1.7 11.8 %copy-start.1 = (f32[2,1,256,256]{3,2,1,0:T(8,128)S(1)}, f32[2,1,256,256]{3,2,1,0:T(8,128)}, u32[]{:S(2)}) copy-start(f32[2,1,256,256]{3,2,1,0:T(8,128)} %refs_1_.1) | copy-start | bytes 1572868
  2.0 8.3 %collective-permute-start = (f32[168,256]{1,0:T(8,128)S(1)}, f32[168,256]{1,0:T(8,128)S(1)}, u32[]{:S(2)}, u32[]{:S(2)}) collective-permute-start(f32[168,256]{1,0:T(8,128)S(1)} %get-tuple-element.18), channel_id=1, source_target_pairs={{0,4},{4,0},{8,12},{12,8},{16,20},{20,16},{24,28},{28,24},{1,5},{5... | collective-permute-start | bytes 516104 | tf_op jit(solution)/shard_map/ppermute | solution.py:299
  5.1 7.4 %collective-permute-start.1 = (f32[88,256]{1,0:T(8,128)S(1)}, f32[88,256]{1,0:T(8,128)S(1)}, u32[]{:S(2)}, u32[]{:S(2)}) collective-permute-start(f32[88,256]{1,0:T(8,128)S(1)} %get-tuple-element.20), channel_id=1, source_target_pairs={{0,4},{4,0},{8,12},{12,8},{16,20},{20,16},{24,28},{28,24},{1,5},{5... | collective-permute-start | bytes 270344 | tf_op jit(solution)/shard_map/ppermute | solution.py:299
  10.5 5.8 %collective-permute-start.2 = (f32[168,256]{1,0:T(8,128)S(1)}, f32[168,256]{1,0:T(8,128)S(1)}, u32[]{:S(2)}, u32[]{:S(2)}) collective-permute-start(f32[168,256]{1,0:T(8,128)S(1)} %shard_map.52.refs_0_.refs_1_), channel_id=1, source_target_pairs={{0,8},{4,12},{8,0},{12,4},{16,24},{20,28},{24,16},{28,20},{1,9},{5... | collective-permute-start | bytes 516104 | tf_op jit(solution)/shard_map/ppermute | solution.py:299
  12.7 4.6 %collective-permute-start.3 = (f32[88,256]{1,0:T(8,128)S(1)}, f32[88,256]{1,0:T(8,128)S(1)}, u32[]{:S(2)}, u32[]{:S(2)}) collective-permute-start(f32[88,256]{1,0:T(8,128)S(1)} %shard_map.53.refs_1_.refs_2_), channel_id=1, source_target_pairs={{0,8},{4,12},{8,0},{12,4},{16,24},{20,28},{24,16},{28,20},{1,9},{5... | collective-permute-start | bytes 270344 | tf_op jit(solution)/shard_map/ppermute | solution.py:299
  16.4 9.0 %copy-start.2 = (f32[2,3,1,256,256]{4,3,2,1,0:T(8,128)S(1)}, f32[2,3,1,256,256]{4,3,2,1,0:T(8,128)}, u32[]{:S(2)}) copy-start(f32[2,3,1,256,256]{4,3,2,1,0:T(8,128)} %hamiltonian.1) | copy-start | bytes 4718596
  17.7 6.1 %collective-permute-start.4 = (f32[56,256]{1,0:T(8,128)S(1)}, f32[56,256]{1,0:T(8,128)S(1)}, u32[]{:S(2)}, u32[]{:S(2)}) collective-permute-start(f32[56,256]{1,0:T(8,128)S(1)} %get-tuple-element.23), channel_id=1, source_target_pairs={{0,24},{4,28},{8,16},{12,20},{16,8},{20,12},{24,0},{28,4},{1,25},{... | collective-permute-start | bytes 172040 | tf_op jit(solution)/shard_map/ppermute | solution.py:299
  21.3 6.7 %collective-permute-start.6 = (f32[144,256]{1,0:T(8,128)S(1)}, f32[144,256]{1,0:T(8,128)S(1)}, u32[]{:S(2)}, u32[]{:S(2)}) collective-permute-start(f32[144,256]{1,0:T(8,128)S(1)} %get-tuple-element.24), channel_id=1, source_target_pairs={{0,16},{4,20},{8,24},{12,28},{16,0},{20,4},{24,8},{28,12},{1,17},{... | collective-permute-start | bytes 442376 | tf_op jit(solution)/shard_map/ppermute | solution.py:299
  23.9 4.2 %collective-permute-start.5 = (f32[56,256]{1,0:T(8,128)S(1)}, f32[56,256]{1,0:T(8,128)S(1)}, u32[]{:S(2)}, u32[]{:S(2)}) collective-permute-start(f32[56,256]{1,0:T(8,128)S(1)} %collective-permute-done.4.share), channel_id=1, source_target_pairs={{0,4},{4,0},{8,12},{12,8},{16,20},{20,16},{24,28},{28,24},{1,5},{5... | collective-permute-start | bytes 172040 | tf_op jit(solution)/shard_map/ppermute | solution.py:299
  28.5 3.1 %collective-permute-start.7 = (f32[8,128]{1,0:T(8,128)S(1)}, f32[8,128]{1,0:T(8,128)S(1)}, u32[]{:S(2)}, u32[]{:S(2)}) collective-permute-start(f32[8,128]{1,0:T(8,128)S(1)} %get-tuple-element.33.refs_0_), channel_id=1, source_target_pairs={{0,3},{1,2},{2,1},{3,0},{4,7},{5,6},{6,5},{7,4},{8,11},{9,10},{10,... | collective-permute-start | bytes 12296 | tf_op jit(solution)/shard_map/ppermute | solution.py:351
  28.6 3.7 %collective-permute-start.8 = (f32[8,128]{1,0:T(8,128)S(1)}, f32[8,128]{1,0:T(8,128)S(1)}, u32[]{:S(2)}, u32[]{:S(2)}) collective-permute-start(f32[8,128]{1,0:T(8,128)S(1)} %get-tuple-element.33.refs_0_), channel_id=1, source_target_pairs={{0,2},{1,3},{2,0},{3,1},{4,6},{5,7},{6,4},{7,5},{8,10},{9,11},{10,... | collective-permute-start | bytes 12296 | tf_op jit(solution)/shard_map/ppermute | solution.py:351
  30.2 2.1 %collective-permute-start.9 = (f32[8,128]{1,0:T(8,128)S(1)}, f32[8,128]{1,0:T(8,128)S(1)}, u32[]{:S(2)}, u32[]{:S(2)}) collective-permute-start(f32[8,128]{1,0:T(8,128)S(1)} %get-tuple-element.33.refs_0_), channel_id=1, source_target_pairs={{0,1},{1,0},{2,3},{3,2},{4,5},{5,4},{6,7},{7,6},{8,9},{9,8},{10,11... | collective-permute-start | bytes 12296 | tf_op jit(solution)/shard_map/ppermute | solution.py:351

commit v10 on v7

--- a/solution.py
+++ b/solution.py
@@ -342,7 +342,6 @@
         lefts, norm, a, b = call(
             lambda *refs: prepare_kernel(half, *refs), prepared, 3 * one, sent, left, right
         )
-    share, norm = lax.optimization_barrier((share, norm))
     passed = swap(share, 1)
     products = call(terms_kernel, array(columns, terms, width, width), 12 * one, a, b, hamiltonian)
     table_rows = -(-(columns * terms + 1) // 8) * 8

time: 33.2 us -> 33.2 us (level)
  no operation moved by 1% of the time
where the time goes in v10:
time: 33.2 us; the launch traced here: 33.1 us
  starting transfers between devices  12.9 us (39%)
  waiting for transfers between devices  11.4 us (34%)
  Pallas kernels  6.9 us (21%)
  local copies, waits for them, and re-layouts  1.14 us (3%)
  between operations  0.74 us (2%)
    ppermute x7, starting transfers between devices, swap(): return lax.ppermute(a, 'col', [(i, i ^ k) for i in range(total)])  10.9 us
    ppermute x7, waiting for transfers between devices, swap(): return lax.ppermute(a, 'col', [(i, i ^ k) for i in range(total)])  10.4 us
    pallas_call x12, Pallas kernels, call(): pl.pallas_call(kernel, out_shape=outs, in_specs=[VMEM] * len(args), out_s...  6.9 us
    ppermute x3, starting transfers between devices, per_device(): lax.ppermute(table, 'sec', [(i, i ^ k) for i in range(sectors)])  1.92 us
    unnamed x9, local copies, waits for them, and re-layouts  1.14 us
    ppermute x3, waiting for transfers between devices, per_device(): lax.ppermute(table, 'sec', [(i, i ^ k) for i in range(sectors)])  1 us
  transfers between devices with their start and end apart: 10, of which 7 were waited for; matrix products, arithmetic and copies ran while one was open for 0% of the time, Pallas kernels for 15%

profile of v10, /device:TPU:0, one launch (start us, length us, event | category | flops | bytes accessed | tf_op | source)
XLA Modules:
  0.0 33.1 jit_solution(17531924392619613683)
XLA Ops:
  0.6 0.0 copy-start
  0.6 1.0 %copy-done = f32[2,1,256,256]{3,2,1,0:T(8,128)S(1)} copy-done((f32[2,1,256,256]{3,2,1,0:T(8,128)S(1)}, f32[2,1,256,256]{3,2,1,0:T(8,128)}, u32[]{:S(2)}) %copy-start) | copy-done | bytes 524312
  1.7 0.0 copy-start.3
  1.7 0.0 copy-start.1
  1.7 0.3 shard_map.50
  2.0 3.1 %collective-permute-start = (f32[168,256]{1,0:T(8,128)S(1)}, f32[168,256]{1,0:T(8,128)S(1)}, u32[]{:S(2)}, u32[]{:S(2)}) collective-permute-start(f32[168,256]{1,0:T(8,128)S(1)} %get-tuple-element.18), channel_id=1, source_target_pairs={{0,4},{4,0},{8,12},{12,8},{16,20},{20,16},{24,28},{28,24},{1,5},{5... | collective-permute-start | bytes 516104 | tf_op jit(solution)/shard_map/ppermute | solution.py:299
  5.1 0.1 collective-permute-start.1
  5.2 0.1 shard_map.51.turned
  5.3 5.0 %collective-permute-done.near.refs_2_ = f32[168,256]{1,0:T(8,128)S(1)} collective-permute-done((f32[168,256]{1,0:T(8,128)S(1)}, f32[168,256]{1,0:T(8,128)S(1)}, u32[]{:S(2)}, u32[]{:S(2)}) %collective-permute-start) | collective-permute-done | bytes 172064 | tf_op jit(solution)/shard_map/ppermute | solution.py:299
  10.3 0.2 shard_map.52.refs_0_.refs_1_
  10.5 1.9 %collective-permute-start.2 = (f32[168,256]{1,0:T(8,128)S(1)}, f32[168,256]{1,0:T(8,128)S(1)}, u32[]{:S(2)}, u32[]{:S(2)}) collective-permute-start(f32[168,256]{1,0:T(8,128)S(1)} %shard_map.52.refs_0_.refs_1_), channel_id=1, source_target_pairs={{0,8},{4,12},{8,0},{12,4},{16,24},{20,28},{24,16},{28,20},{1,9},{5... | collective-permute-start | bytes 516104 | tf_op jit(solution)/shard_map/ppermute | solution.py:299
  12.5 0.0 collective-permute-done.1.near.refs_3_
  12.5 0.2 shard_map.53.refs_1_.refs_2_
  12.7 0.7 %collective-permute-start.3 = (f32[88,256]{1,0:T(8,128)S(1)}, f32[88,256]{1,0:T(8,128)S(1)}, u32[]{:S(2)}, u32[]{:S(2)}) collective-permute-start(f32[88,256]{1,0:T(8,128)S(1)} %shard_map.53.refs_1_.refs_2_), channel_id=1, source_target_pairs={{0,8},{4,12},{8,0},{12,4},{16,24},{20,28},{24,16},{28,20},{1,9},{5... | collective-permute-start | bytes 270344 | tf_op jit(solution)/shard_map/ppermute | solution.py:299
  13.4 0.0 copy-done.3
  13.4 0.1 copy.5.refs_0_
  13.5 0.0 copy-done.1
  13.5 0.5 %shard_map.54 = (f32[2,256,256]{2,1,0:T(8,128)S(1)}, f32[2,256,256]{2,1,0:T(8,128)S(1)}) custom-call(s32[2,1]{1,0:T(2,128)S(1)} %copy.5.refs_0_, f32[2,1,256,256]{3,2,1,0:T(8,128)S(1)} %copy-done.1, f32[168,256]{1,0:T(8,128)S(1)} %collective-permute-done.near.refs_2_, f32[88,256]{1,0:T(8,128)S(1)} %collective-permute-done.1.near.refs_3_), custom_call_target="tpu_custom_call" | custom-call | flops 201326592 | bytes 1048576 | tf_op jit(solution)/shard_map/pallas_call | solution.py:275
  14.0 2.4 %collective-permute-done.2.refs_2_.refs_3_ = f32[168,256]{1,0:T(8,128)S(1)} collective-permute-done((f32[168,256]{1,0:T(8,128)S(1)}, f32[168,256]{1,0:T(8,128)S(1)}, u32[]{:S(2)}, u32[]{:S(2)}) %collective-permute-start.2) | collective-permute-done | bytes 172064 | tf_op jit(solution)/shard_map/ppermute | solution.py:299
  16.4 0.0 copy-start.2
  16.4 0.3 shard_map.55.refs_0_
  16.6 0.7 %collective-permute-done.3.refs_3_.refs_4_ = f32[88,256]{1,0:T(8,128)S(1)} collective-permute-done((f32[88,256]{1,0:T(8,128)S(1)}, f32[88,256]{1,0:T(8,128)S(1)}, u32[]{:S(2)}, u32[]{:S(2)}) %collective-permute-start.3) | collective-permute-done | bytes 90144 | tf_op jit(solution)/shard_map/ppermute | solution.py:299
  17.3 0.4 %shard_map.56 = (f32[256,256]{1,0:T(8,128)S(1)}, f32[64,256]{1,0:T(8,128)S(1)}, f32[128,256]{1,0:T(8,128)S(1)}) custom-call(f32[256,256]{1,0:T(8,128)S(1)} %shard_map.55.refs_0_, f32[168,256]{1,0:T(8,128)S(1)} %shard_map.52.refs_0_.refs_1_, f32[88,256]{1,0:T(8,128)S(1)} %shard_map.53.refs_1_.refs_2_, f32[88,256]{1,0:T(8,128)S(1)} %collective-permute-done.3.refs_3_.refs_4_), custom_call_target="tpu_custom_call" | custom-call | flops 100663296 | bytes 1048576 | tf_op jit(solution)/shard_map/pallas_call | solution.py:275
  17.7 3.6 %collective-permute-start.4 = (f32[64,256]{1,0:T(8,128)S(1)}, f32[64,256]{1,0:T(8,128)S(1)}, u32[]{:S(2)}, u32[]{:S(2)}) collective-permute-start(f32[64,256]{1,0:T(8,128)S(1)} %get-tuple-element.23), channel_id=1, source_target_pairs={{0,24},{4,28},{8,16},{12,20},{16,8},{20,12},{24,0},{28,4},{1,25},{... | collective-permute-start | bytes 196616 | tf_op jit(solution)/shard_map/ppermute | solution.py:299
  21.3 0.0 collective-permute-start.6
  21.3 1.3 %shard_map.57 = (f32[2,256,256]{2,1,0:T(8,128)S(1)}, f32[256,256]{1,0:T(8,128)S(1)}, bf16[2,2,256,256]{3,2,1,0:T(8,128)(2,1)S(1)}, bf16[2,2,256,256]{3,2,1,0:T(8,128)(2,1)S(1)}) custom-call(f32[256,256]{1,0:T(8,128)S(1)} %get-tuple-element.25.refs_0_, f32[2,256,256]{2,1,0:T(8,128)S(1)} %get-tuple-element.26.refs_1_, ...), custom_call_target="tpu_custom_call" | custom-call | flops 503316480 | bytes 1048576 | tf_op jit(solution)/shard_map/pallas_call | solution.py:275
  22.7 1.3 %collective-permute-done.4.share = f32[64,256]{1,0:T(8,128)S(1)} collective-permute-done((f32[64,256]{1,0:T(8,128)S(1)}, f32[64,256]{1,0:T(8,128)S(1)}, u32[]{:S(2)}, u32[]{:S(2)}) %collective-permute-start.4) | collective-permute-done | bytes 65568 | tf_op jit(solution)/shard_map/ppermute | solution.py:299
  24.0 1.5 %collective-permute-start.5 = (f32[64,256]{1,0:T(8,128)S(1)}, f32[64,256]{1,0:T(8,128)S(1)}, u32[]{:S(2)}, u32[]{:S(2)}) collective-permute-start(f32[64,256]{1,0:T(8,128)S(1)} %collective-permute-done.4.share), channel_id=1, source_target_pairs={{0,4},{4,0},{8,12},{12,8},{16,20},{20,16},{24,28},{28,24},{1,5},{5... | collective-permute-start | bytes 196616 | tf_op jit(solution)/shard_map/ppermute | solution.py:299
  25.5 0.0 copy-done.2
  25.5 1.7 %shard_map.58.terms = f32[2,3,256,256]{3,2,1,0:T(8,128)S(1)} custom-call(bf16[2,2,256,256]{3,2,1,0:T(8,128)(2,1)S(1)} %get-tuple-element.28.a, bf16[2,2,256,256]{3,2,1,0:T(8,128)(2,1)S(1)} %get-tuple-element.29.b, f32[2,3,1,256,256]{4,3,2,1,0:T(8,128)S(1)} %copy-done.2), custom_call_target="tpu_custom_call" | custom-call | flops 1207959552 | bytes 1048576 | tf_op jit(solution)/shard_map/pallas_call | solution.py:275
  27.2 1.1 %collective-permute-done.5.passed = f32[64,256]{1,0:T(8,128)S(1)} collective-permute-done((f32[64,256]{1,0:T(8,128)S(1)}, f32[64,256]{1,0:T(8,128)S(1)}, u32[]{:S(2)}, u32[]{:S(2)}) %collective-permute-start.5) | collective-permute-done | bytes 65568 | tf_op jit(solution)/shard_map/ppermute | solution.py:299
  28.2 0.0 collective-permute-done.6.rest
  28.2 0.4 %shard_map.59 = (f32[8,128]{1,0:T(8,128)S(1)}, f32[256,256]{1,0:T(8,128)S(1)}) custom-call(f32[64,256]{1,0:T(8,128)S(1)} %collective-permute-done.4.share, f32[64,256]{1,0:T(8,128)S(1)} %collective-permute-done.5.passed, f32[128,256]{1,0:T(8,128)S(1)} %collective-permute-done.6.rest, f32[2,3,256,256]{3,2,1,0:T(8,128)S(1)} %shard_map.58.terms, ...), custom_call_target="tpu_custom_call" | custom-call | flops 201326592 | bytes 1048576 | tf_op jit(solution)/shard_map/pallas_call | solution.py:275
  28.7 0.1 collective-permute-start.7
  28.7 1.5 %collective-permute-start.8 = (f32[8,128]{1,0:T(8,128)S(1)}, f32[8,128]{1,0:T(8,128)S(1)}, u32[]{:S(2)}, u32[]{:S(2)}) collective-permute-start(f32[8,128]{1,0:T(8,128)S(1)} %get-tuple-element.33.refs_0_), channel_id=1, source_target_pairs={{0,2},{1,3},{2,0},{3,1},{4,6},{5,7},{6,4},{7,5},{8,10},{9,11},{10,... | collective-permute-start | bytes 12296 | tf_op jit(solution)/shard_map/ppermute | solution.py:351
  30.3 0.3 %collective-permute-start.9 = (f32[8,128]{1,0:T(8,128)S(1)}, f32[8,128]{1,0:T(8,128)S(1)}, u32[]{:S(2)}, u32[]{:S(2)}) collective-permute-start(f32[8,128]{1,0:T(8,128)S(1)} %get-tuple-element.33.refs_0_), channel_id=1, source_target_pairs={{0,1},{1,0},{2,3},{3,2},{4,5},{5,4},{6,7},{7,6},{8,9},{9,8},{10,11... | collective-permute-start | bytes 12296 | tf_op jit(solution)/shard_map/ppermute | solution.py:351
  30.6 0.8 %shard_map.60 = f32[2,1,256,256]{3,2,1,0:T(8,128)} custom-call(f32[256,256]{1,0:T(8,128)S(1)} %get-tuple-element.31.refs_0_, f32[2,256,256]{2,1,0:T(8,128)S(1)} %get-tuple-element.32.refs_1_), custom_call_target="tpu_custom_call" | custom-call | flops 201326592 | bytes 1048576 | tf_op jit(solution)/shard_map/pallas_call | solution.py:275
  31.4 0.4 %collective-permute-done.7.refs_1_ = f32[8,128]{1,0:T(8,128)S(1)} collective-permute-done((f32[8,128]{1,0:T(8,128)S(1)}, f32[8,128]{1,0:T(8,128)S(1)}, u32[]{:S(2)}, u32[]{:S(2)}) %collective-permute-start.7) | collective-permute-done | bytes 4128 | tf_op jit(solution)/shard_map/ppermute | solution.py:351
  31.8 0.6 %collective-permute-done.8.refs_2_ = f32[8,128]{1,0:T(8,128)S(1)} collective-permute-done((f32[8,128]{1,0:T(8,128)S(1)}, f32[8,128]{1,0:T(8,128)S(1)}, u32[]{:S(2)}, u32[]{:S(2)}) %collective-permute-start.8) | collective-permute-done | bytes 4128 | tf_op jit(solution)/shard_map/ppermute | solution.py:351
  32.4 0.0 collective-permute-done.9.refs_3_
  32.4 0.7 %shard_map.61 = f32[2,3]{1,0:T(2,128)} custom-call(f32[8,128]{1,0:T(8,128)S(1)} %get-tuple-element.33.refs_0_, f32[8,128]{1,0:T(8,128)S(1)} %collective-permute-done.7.refs_1_, f32[8,128]{1,0:T(8,128)S(1)} %collective-permute-done.8.refs_2_, f32[8,128]{1,0:T(8,128)S(1)} %collective-permute-done.9.refs_3_), custom_call_target="tpu_custom_call" | custom-call | flops 1000 | bytes 1048576 | tf_op jit(solution)/shard_map/pallas_call | solution.py:275
Async XLA Ops:
  0.6 1.0 %copy-start = (f32[2,1,256,256]{3,2,1,0:T(8,128)S(1)}, f32[2,1,256,256]{3,2,1,0:T(8,128)}, u32[]{:S(2)}) copy-start(f32[2,1,256,256]{3,2,1,0:T(8,128)} %refs_1_.1) | copy-start | bytes 1572868
  1.7 11.7 %copy-start.3 = (s32[2,1]{0,1:T(1,128)S(1)}, s32[2,1]{0,1:T(1,128)}, u32[]{:S(2)}) copy-start(s32[2,1]{0,1:T(1,128)} %param.5) | copy-start | bytes 28
  1.7 11.8 %copy-start.1 = (f32[2,1,256,256]{3,2,1,0:T(8,128)S(1)}, f32[2,1,256,256]{3,2,1,0:T(8,128)}, u32[]{:S(2)}) copy-start(f32[2,1,256,256]{3,2,1,0:T(8,128)} %refs_1_.1) | copy-start | bytes 1572868
  2.0 8.3 %collective-permute-start = (f32[168,256]{1,0:T(8,128)S(1)}, f32[168,256]{1,0:T(8,128)S(1)}, u32[]{:S(2)}, u32[]{:S(2)}) collective-permute-start(f32[168,256]{1,0:T(8,128)S(1)} %get-tuple-element.18), channel_id=1, source_target_pairs={{0,4},{4,0},{8,12},{12,8},{16,20},{20,16},{24,28},{28,24},{1,5},{5... | collective-permute-start | bytes 516104 | tf_op jit(solution)/shard_map/ppermute | solution.py:299
  5.1 7.4 %collective-permute-start.1 = (f32[88,256]{1,0:T(8,128)S(1)}, f32[88,256]{1,0:T(8,128)S(1)}, u32[]{:S(2)}, u32[]{:S(2)}) collective-permute-start(f32[88,256]{1,0:T(8,128)S(1)} %get-tuple-element.20), channel_id=1, source_target_pairs={{0,4},{4,0},{8,12},{12,8},{16,20},{20,16},{24,28},{28,24},{1,5},{5... | collective-permute-start | bytes 270344 | tf_op jit(solution)/shard_map/ppermute | solution.py:299
  10.5 5.8 %collective-permute-start.2 = (f32[168,256]{1,0:T(8,128)S(1)}, f32[168,256]{1,0:T(8,128)S(1)}, u32[]{:S(2)}, u32[]{:S(2)}) collective-permute-start(f32[168,256]{1,0:T(8,128)S(1)} %shard_map.52.refs_0_.refs_1_), channel_id=1, source_target_pairs={{0,8},{4,12},{8,0},{12,4},{16,24},{20,28},{24,16},{28,20},{1,9},{5... | collective-permute-start | bytes 516104 | tf_op jit(solution)/shard_map/ppermute | solution.py:299
  12.7 4.6 %collective-permute-start.3 = (f32[88,256]{1,0:T(8,128)S(1)}, f32[88,256]{1,0:T(8,128)S(1)}, u32[]{:S(2)}, u32[]{:S(2)}) collective-permute-start(f32[88,256]{1,0:T(8,128)S(1)} %shard_map.53.refs_1_.refs_2_), channel_id=1, source_target_pairs={{0,8},{4,12},{8,0},{12,4},{16,24},{20,28},{24,16},{28,20},{1,9},{5... | collective-permute-start | bytes 270344 | tf_op jit(solution)/shard_map/ppermute | solution.py:299
  16.4 9.1 %copy-start.2 = (f32[2,3,1,256,256]{4,3,2,1,0:T(8,128)S(1)}, f32[2,3,1,256,256]{4,3,2,1,0:T(8,128)}, u32[]{:S(2)}) copy-start(f32[2,3,1,256,256]{4,3,2,1,0:T(8,128)} %hamiltonian.1) | copy-start | bytes 4718596
  17.7 6.2 %collective-permute-start.4 = (f32[64,256]{1,0:T(8,128)S(1)}, f32[64,256]{1,0:T(8,128)S(1)}, u32[]{:S(2)}, u32[]{:S(2)}) collective-permute-start(f32[64,256]{1,0:T(8,128)S(1)} %get-tuple-element.23), channel_id=1, source_target_pairs={{0,24},{4,28},{8,16},{12,20},{16,8},{20,12},{24,0},{28,4},{1,25},{... | collective-permute-start | bytes 196616 | tf_op jit(solution)/shard_map/ppermute | solution.py:299
  21.3 6.9 %collective-permute-start.6 = (f32[128,256]{1,0:T(8,128)S(1)}, f32[128,256]{1,0:T(8,128)S(1)}, u32[]{:S(2)}, u32[]{:S(2)}) collective-permute-start(f32[128,256]{1,0:T(8,128)S(1)} %get-tuple-element.24), channel_id=1, source_target_pairs={{0,16},{4,20},{8,24},{12,28},{16,0},{20,4},{24,8},{28,12},{1,17},{... | collective-permute-start | bytes 393224 | tf_op jit(solution)/shard_map/ppermute | solution.py:299
  24.0 4.3 %collective-permute-start.5 = (f32[64,256]{1,0:T(8,128)S(1)}, f32[64,256]{1,0:T(8,128)S(1)}, u32[]{:S(2)}, u32[]{:S(2)}) collective-permute-start(f32[64,256]{1,0:T(8,128)S(1)} %collective-permute-done.4.share), channel_id=1, source_target_pairs={{0,4},{4,0},{8,12},{12,8},{16,20},{20,16},{24,28},{28,24},{1,5},{5... | collective-permute-start | bytes 196616 | tf_op jit(solution)/shard_map/ppermute | solution.py:299
  28.7 3.1 %collective-permute-start.7 = (f32[8,128]{1,0:T(8,128)S(1)}, f32[8,128]{1,0:T(8,128)S(1)}, u32[]{:S(2)}, u32[]{:S(2)}) collective-permute-start(f32[8,128]{1,0:T(8,128)S(1)} %get-tuple-element.33.refs_0_), channel_id=1, source_target_pairs={{0,3},{1,2},{2,1},{3,0},{4,7},{5,6},{6,5},{7,4},{8,11},{9,10},{10,... | collective-permute-start | bytes 12296 | tf_op jit(solution)/shard_map/ppermute | solution.py:351
  28.7 3.7 %collective-permute-start.8 = (f32[8,128]{1,0:T(8,128)S(1)}, f32[8,128]{1,0:T(8,128)S(1)}, u32[]{:S(2)}, u32[]{:S(2)}) collective-permute-start(f32[8,128]{1,0:T(8,128)S(1)} %get-tuple-element.33.refs_0_), channel_id=1, source_target_pairs={{0,2},{1,3},{2,0},{3,1},{4,6},{5,7},{6,4},{7,5},{8,10},{9,11},{10,... | collective-permute-start | bytes 12296 | tf_op jit(solution)/shard_map/ppermute | solution.py:351
  30.3 2.2 %collective-permute-start.9 = (f32[8,128]{1,0:T(8,128)S(1)}, f32[8,128]{1,0:T(8,128)S(1)}, u32[]{:S(2)}, u32[]{:S(2)}) collective-permute-start(f32[8,128]{1,0:T(8,128)S(1)} %get-tuple-element.33.refs_0_), channel_id=1, source_target_pairs={{0,1},{1,0},{2,3},{3,2},{4,5},{5,4},{6,7},{7,6},{8,9},{9,8},{10,11... | collective-permute-start | bytes 12296 | tf_op jit(solution)/shard_map/ppermute | solution.py:351
